TPU v7x, 128 devices: a whole 4x4x4 slice. The times are simulated.
128 devices in a mesh: ctx: 16 (over z, x), head: 8 (over y, core).
Axes of the slice: x: 4, y: 4, z: 4, core: 2. Of those that a mesh axis runs over, the one named last changes fastest.
Arguments:
- ssm_input: bfloat16 [16384, 8192], P(('ctx', 'head')), may hold values from -6 to 6
- gate_input: bfloat16 [16384, 8192], P(('ctx', 'head')), may hold values from -6 to 6
- b_input: bfloat16 [16384, 1024], P(('ctx', 'head')), may hold values from -3 to 3
- c_input: bfloat16 [16384, 1024], P(('ctx', 'head')), may hold values from -3 to 3
- dt_raw: bfloat16 [16384, 128], P(('ctx', 'head')), may hold values from -13 to 0
- dt_bias: float32 [128], replicated, may hold values from -0.25 to 0.25
- a_log: float32 [128], replicated, may hold values from -6 to 3
- skip_gain: float32 [128], replicated, may hold values from 0.5 to 1.5
- out_grad: bfloat16 [16384, 8192], P(('ctx', 'head')), may hold values from -6 to 6
Outputs:
- gated_out: bfloat16 [16384, 8192], P(('ctx', 'head'))
- input_grad: float32 [16384, 8192], P(('ctx', 'head'))
- b_grad: float32 [16384, 1024], P(('ctx', 'head'))
- c_grad: float32 [16384, 1024], P(('ctx', 'head'))
All inputs are finite; a program needn't handle non-finite values.
Results may differ from a plain program's by a relative error of at most 0.014.
Values may be sent and summed in bfloat16 or wider, within the bound.
No kernel may reach another device: no remote copies, remote signals or barrier semaphores. Data moves between devices by JAX's collectives and lax.ppermute only.
A program may use at most 128 MiB of HBM per device.

v0:
```python
import functools

import jax
import jax.numpy as jnp
from jax import lax
from jax.experimental import pallas as pl
from jax.experimental.pallas import tpu as pltpu
from jax.sharding import PartitionSpec as P

NH = 128
P_SIZE = 64
N = 128
NG = 8
PER = NH // NG
W = PER * P_SIZE
T = 128
HALF = NG // 2
LANES = 128
WIDE = 2 * W + LANES
F32 = jnp.float32
BF16 = jnp.bfloat16


def params():
    return pltpu.CompilerParams(
        dimension_semantics=("arbitrary",), vmem_limit_bytes=48 * 1024 * 1024
    )


def lane(shape):
    return lax.broadcasted_iota(jnp.int32, shape, len(shape) - 1)


def fill_spread(e_ref):
    row = lax.broadcasted_iota(jnp.int32, (LANES, W), 0)
    col = lax.broadcasted_iota(jnp.int32, (LANES, W), 1)
    hit = ((row & (PER - 1)) == (col >> 6)) & (row < 2 * PER)
    e_ref[...] = jnp.where(hit, 1.0, 0.0).astype(BF16)


def to_front(values, group):
    return pltpu.roll(values, lax.rem(LANES - PER * group, LANES), 1)


def pair_up(front):
    high = front.astype(BF16).astype(F32)
    low = front - high
    where = lane(front.shape)
    return jnp.where(
        where < PER, high, jnp.where(where < 2 * PER, pltpu.roll(low, PER, 1), 0.0)
    ).astype(BF16)


def spread(values, group, e_ref):
    return jnp.dot(pair_up(to_front(values, group)), e_ref[...], preferred_element_type=F32)


def silu(v):
    return v * (0.5 * jnp.tanh(0.5 * v) + 0.5)


def steps_of(dt_ref, bias_ref, alog_ref):
    u = jnp.exp(dt_ref[...].astype(F32) + bias_ref[...])
    one = 1.0 + u
    step = jnp.where(one == 1.0, u, jnp.log(one) * (u / jnp.where(one == 1.0, 1.0, one - 1.0)))
    rate = -step * jnp.exp(alog_ref[...])
    row = lax.broadcasted_iota(jnp.int32, (T, T), 0)
    col = lax.broadcasted_iota(jnp.int32, (T, T), 1)
    tri = jnp.where(row >= col, 1.0, 0.0).astype(BF16)
    running = jnp.zeros((T, NH), F32)
    for _ in range(3):
        piece = rate.astype(BF16)
        running = running + jnp.dot(tri, piece, preferred_element_type=F32)
        rate = rate - piece.astype(F32)
    from_start = jnp.exp(running)
    to_end = jnp.exp(running[T - 1 : T] - running) * step
    return step, running, from_start, to_end


def states_kernel(first, sc_ref, *refs):
    if first:
        dt_ref, bias_ref, alog_ref, x_ref, z_ref, og_ref, b_ref, c_ref = refs[:8]
        st_ref, hg_ref, aux_ref, e_ref = refs[8:]
    else:
        aux_ref, x_ref, z_ref, og_ref, b_ref, c_ref = refs[:6]
        st_ref, hg_ref, e_ref = refs[6:]
    i = pl.program_id(0)
    group = sc_ref[0] + i

    @pl.when(i == 0)
    def _():
        fill_spread(e_ref)
        if first:
            for k, v in enumerate(steps_of(dt_ref, bias_ref, alog_ref)):
                aux_ref[k] = v

    from_start = aux_ref[2]
    to_end = aux_ref[3]
    head_grad = (og_ref[...].astype(F32) * silu(z_ref[...].astype(F32))).astype(BF16)
    hg_ref[...] = head_grad
    xs = (x_ref[...].astype(F32) * spread(to_end, group, e_ref)).astype(BF16)
    st_ref[:, :W] = jnp.dot(b_ref[...].T, xs, preferred_element_type=F32).astype(BF16)
    gs = (head_grad.astype(F32) * spread(from_start, group, e_ref)).astype(BF16)
    st_ref[:, W : 2 * W] = jnp.dot(c_ref[...].T, gs, preferred_element_type=F32).astype(BF16)
    decay = jnp.broadcast_to(from_start[T - 1 : T], (8, NH))
    decay = pair_up(to_front(decay, group)).astype(F32)
    st_ref[:, 2 * W :] = jnp.broadcast_to(decay[0:1], (N, LANES)).astype(BF16)


def cols(i, sc):
    return (0, sc[0] + i)


def whole2(i, sc):
    return (0, 0)


def whole3(i, sc):
    return (0, 0, 0)


def rows(i, sc):
    return (i, 0)


TOKEN_BLOCK = pl.BlockSpec((T, W), cols)
BC_BLOCK = pl.BlockSpec((T, N), cols)
AUX_BLOCK = pl.BlockSpec((4, T, NH), whole3)
ROW_BLOCK = pl.BlockSpec((1, NH), whole2)
STATE_BLOCK = pl.BlockSpec((N, WIDE), rows)
EL_BLOCK = pl.BlockSpec((N, 2 * W), rows)
LOCAL_BLOCK = pl.BlockSpec((T, W), lambda i, sc: (0, i))
LOCAL_BC = pl.BlockSpec((T, N), lambda i, sc: (0, i))
SPREAD = pltpu.VMEM((LANES, W), BF16)


def states(first, sc, *args):
    out_shape = [
        jax.ShapeDtypeStruct((HALF * N, WIDE), BF16),
        jax.ShapeDtypeStruct((T, HALF * W), BF16),
    ]
    out_specs = [STATE_BLOCK, LOCAL_BLOCK]
    if first:
        in_specs = [pl.BlockSpec((T, NH), whole2), ROW_BLOCK, ROW_BLOCK]
        out_shape.append(jax.ShapeDtypeStruct((4, T, NH), F32))
        out_specs.append(AUX_BLOCK)
    else:
        in_specs = [AUX_BLOCK]
    in_specs += [TOKEN_BLOCK] * 3 + [BC_BLOCK] * 2
    return pl.pallas_call(
        functools.partial(states_kernel, first),
        grid_spec=pltpu.PrefetchScalarGridSpec(
            num_scalar_prefetch=1,
            grid=(HALF,),
            in_specs=in_specs,
            out_specs=out_specs,
            scratch_shapes=[SPREAD],
        ),
        out_shape=out_shape,
        compiler_params=params(),
        name="states_send" if first else "states_keep",
    )(sc, *args)


def decay_row(state_ref, e_ref):
    return jnp.dot(state_ref[0:16, 2 * W :], e_ref[...], preferred_element_type=F32)[0:1]


def merge_kernel(sc_ref, own_ref, got_ref, out_ref, e_ref):
    @pl.when(pl.program_id(0) == 0)
    def _():
        fill_spread(e_ref)

    def merge(r0, r1):
        d0 = decay_row(r0, e_ref)
        d1 = decay_row(r1, e_ref)
        forward = d1 * r0[:, :W].astype(F32) + r1[:, :W].astype(F32)
        backward = r0[:, W : 2 * W].astype(F32) + d0 * r1[:, W : 2 * W].astype(F32)
        out_ref[:, :, :W] = forward.reshape(N // 8, 8, W).astype(BF16)
        out_ref[:, :, W : 2 * W] = backward.reshape(N // 8, 8, W).astype(BF16)
        p0 = r0[0:16, 2 * W :].astype(F32)
        p1 = r1[0:16, 2 * W :].astype(F32)
        p0 = p0 + pltpu.roll(p0, LANES - PER, 1)
        p1 = p1 + pltpu.roll(p1, LANES - PER, 1)
        both = pair_up(p0 * p1).astype(F32)[0:8]
        out_ref[:, :, 2 * W :] = jnp.broadcast_to(both[None], (N // 8, 8, LANES)).astype(BF16)

    @pl.when(sc_ref[1] == 0)
    def _():
        merge(own_ref, got_ref)

    @pl.when(sc_ref[1] != 0)
    def _():
        merge(got_ref, own_ref)


def merge(sc, own, got):
    return pl.pallas_call(
        merge_kernel,
        grid_spec=pltpu.PrefetchScalarGridSpec(
            num_scalar_prefetch=1,
            grid=(HALF,),
            in_specs=[STATE_BLOCK, STATE_BLOCK],
            out_specs=pl.BlockSpec((N // 8, 8, WIDE), lambda i, sc: (i, 0, 0)),
            scratch_shapes=[SPREAD],
        ),
        out_shape=jax.ShapeDtypeStruct((HALF * N // 8, 8, WIDE), BF16),
        compiler_params=params(),
        name="merge_cores",
    )(sc, own, got)


def scan_kernel(chips, in_ref, after_ref, out_ref, e_ref, d_ref):
    fill_spread(e_ref)
    pairs = in_ref[:, :, 2 * W :].astype(F32).reshape(chips * 8, LANES).astype(BF16)
    d_ref[...] = jnp.dot(pairs, e_ref[...], preferred_element_type=F32).reshape(chips, 8, W)

    def step(k, carry):
        e, l = carry
        out_ref[k, :, :W] = e.astype(BF16)
        e = d_ref[k] * e + in_ref[k, :, :W].astype(F32)
        j = chips - 1 - k
        out_ref[j, :, W:] = l.astype(BF16)
        l = d_ref[j] * l + in_ref[j, :, W : 2 * W].astype(F32)
        return e, l

    zero = jnp.zeros((8, W), F32)
    lax.fori_loop(0, chips, step, (zero, zero), unroll=4)


def scan(parts, after):
    chips = parts.shape[0]
    return pl.pallas_call(
        functools.partial(scan_kernel, chips),
        in_specs=[pl.BlockSpec(memory_space=pltpu.VMEM), pl.BlockSpec(memory_space=pl.ANY)],
        out_specs=pl.BlockSpec(memory_space=pltpu.VMEM),
        out_shape=jax.ShapeDtypeStruct((chips, 8, 2 * W), BF16),
        scratch_shapes=[SPREAD, pltpu.VMEM((chips, 8, W), F32)],
        compiler_params=pltpu.CompilerParams(vmem_limit_bytes=48 * 1024 * 1024),
        name="scan_chips",
    )(parts, after)


def pass_on_kernel(sc_ref, el_ref, own_ref, after_ref, out_ref, e_ref):
    @pl.when(pl.program_id(0) == 0)
    def _():
        fill_spread(e_ref)

    d = decay_row(own_ref, e_ref)

    @pl.when(sc_ref[1] == 0)
    def _():
        e = d * el_ref[:, :W].astype(F32) + own_ref[:, :W].astype(F32)
        out_ref[:, :W] = e.astype(BF16)
        out_ref[:, W:] = el_ref[:, W:]

    @pl.when(sc_ref[1] != 0)
    def _():
        l = d * el_ref[:, W:].astype(F32) + own_ref[:, W : 2 * W].astype(F32)
        out_ref[:, :W] = el_ref[:, :W]
        out_ref[:, W:] = l.astype(BF16)


def pass_on(sc, el, own, after):
    return pl.pallas_call(
        pass_on_kernel,
        grid_spec=pltpu.PrefetchScalarGridSpec(
            num_scalar_prefetch=1,
            grid=(HALF,),
            in_specs=[EL_BLOCK, STATE_BLOCK, pl.BlockSpec(memory_space=pl.ANY)],
            out_specs=EL_BLOCK,
            scratch_shapes=[SPREAD],
        ),
        out_shape=jax.ShapeDtypeStruct((HALF * N, 2 * W), BF16),
        compiler_params=params(),
        name="pass_on",
    )(sc, el, own, after)


NT = (((1,), (1,)), ((), ()))


def local_kernel(
    sc_ref, aux_ref, skip_ref, x_ref, hg_ref, b_ref, c_ref, y_ref, dx_ref, db_ref, dc_ref, e_ref, runt_ref, stept_ref
):
    i = pl.program_id(0)
    group = sc_ref[0] + i

    @pl.when(i == 0)
    def _():
        fill_spread(e_ref)
        stept_ref[...] = aux_ref[0].T
        runt_ref[...] = aux_ref[1].T

    first = pl.multiple_of(group * PER, PER)
    run_rows = runt_ref[pl.ds(first, PER), :]
    step_rows = stept_ref[pl.ds(first, PER), :]
    run_cols = to_front(aux_ref[1], group)
    skip = spread(jnp.broadcast_to(skip_ref[...], (8, NH)), group, e_ref)[0:1]
    b, c = b_ref[...], c_ref[...]
    cb = lax.dot_general(c, b, NT, preferred_element_type=F32)
    row = lax.broadcasted_iota(jnp.int32, (T, T), 0)
    col = lax.broadcasted_iota(jnp.int32, (T, T), 1)
    below = row >= col
    left = col < P_SIZE
    mass = jnp.zeros((T, T), F32)
    for pair in range(PER // 2):
        here = slice(pair * LANES, (pair + 1) * LANES)
        x = x_ref[:, here]
        g = hg_ref[:, here]
        ys, dxs = [], []
        for k in range(2):
            j = 2 * pair + k
            gap = run_cols[:, j : j + 1] - run_rows[j : j + 1, :]
            weight = jnp.exp(jnp.where(below, gap, -1e30)) * step_rows[j : j + 1, :]
            mine = left if k == 0 else ~left
            inner = lax.dot_general(
                jnp.where(mine, g, jnp.zeros_like(g)), x, NT, preferred_element_type=F32
            )
            mass = mass + weight * inner
            joint = (weight * cb).astype(BF16)
            ys.append(jnp.dot(joint, x, preferred_element_type=F32))
            dxs.append(jnp.dot(joint.T, g, preferred_element_type=F32))
        y_ref[:, here] = jnp.where(left, ys[0], ys[1]) + skip[:, here] * x.astype(F32)
        dx_ref[:, here] = jnp.where(left, dxs[0], dxs[1]) + skip[:, here] * g.astype(F32)
    high = mass.astype(BF16)
    low = (mass - high.astype(F32)).astype(BF16)
    dc_ref[...] = jnp.dot(high, b, preferred_element_type=F32) + jnp.dot(
        low, b, preferred_element_type=F32
    )
    db_ref[...] = jnp.dot(high.T, c, preferred_element_type=F32) + jnp.dot(
        low.T, c, preferred_element_type=F32
    )


def local(name, sc, aux, skip, x, hg, b, c):
    return pl.pallas_call(
        local_kernel,
        grid_spec=pltpu.PrefetchScalarGridSpec(
            num_scalar_prefetch=1,
            grid=(HALF,),
            in_specs=[AUX_BLOCK, ROW_BLOCK, TOKEN_BLOCK, LOCAL_BLOCK, BC_BLOCK, BC_BLOCK],
            out_specs=[LOCAL_BLOCK, LOCAL_BLOCK, LOCAL_BC, LOCAL_BC],
            scratch_shapes=[SPREAD, pltpu.VMEM((NH, T), F32), pltpu.VMEM((NH, T), F32)],
        ),
        out_shape=[
            jax.ShapeDtypeStruct((T, HALF * W), F32),
            jax.ShapeDtypeStruct((T, HALF * W), F32),
            jax.ShapeDtypeStruct((T, HALF * N), F32),
            jax.ShapeDtypeStruct((T, HALF * N), F32),
        ],
        compiler_params=params(),
        name=name,
    )(sc, aux, skip, x, hg, b, c)


def final_kernel(own, sc_ref, *refs):
    aux_ref, x_ref, hg_ref, z_ref, b_ref, c_ref, yl_ref, dxl_ref, dbl_ref, dcl_ref, el_ref = refs[:11]
    if own:
        got_ref, out_ref, dx_ref, db_ref, dc_ref, e_ref, cur_ref = refs[11:]
    else:
        out_ref, dx_ref, db_ref, dc_ref, e_ref = refs[15:]
        cur_ref = el_ref
    i = pl.program_id(0)
    group = sc_ref[0] + i

    @pl.when(i == 0)
    def _():
        fill_spread(e_ref)

    if own:
        d = decay_row(got_ref, e_ref)

        @pl.when(sc_ref[1] == 0)
        def _():
            l = d * el_ref[:, W:].astype(F32) + got_ref[:, W : 2 * W].astype(F32)
            cur_ref[:, :W] = el_ref[:, :W]
            cur_ref[:, W:] = l.astype(BF16)

        @pl.when(sc_ref[1] != 0)
        def _():
            e = d * el_ref[:, :W].astype(F32) + got_ref[:, :W].astype(F32)
            cur_ref[:, :W] = e.astype(BF16)
            cur_ref[:, W:] = el_ref[:, W:]

    entering = cur_ref[:, :W]
    later = cur_ref[:, W:]
    from_start = spread(aux_ref[2], group, e_ref)
    to_end = spread(aux_ref[3], group, e_ref)
    b, c = b_ref[...], c_ref[...]
    mixed = yl_ref[...] + from_start * jnp.dot(c, entering, preferred_element_type=F32)
    out_ref[...] = (mixed.astype(BF16).astype(F32) * silu(z_ref[...].astype(F32))).astype(BF16)
    dx_ref[...] = dxl_ref[...] + to_end * jnp.dot(b, later, preferred_element_type=F32)
    xs = (x_ref[...].astype(F32) * to_end).astype(BF16)
    gs = (hg_ref[...].astype(F32) * from_start).astype(BF16)
    db_ref[...] = dbl_ref[...] + lax.dot_general(xs, later, NT, preferred_element_type=F32)
    dc_ref[...] = dcl_ref[...] + lax.dot_general(gs, entering, NT, preferred_element_type=F32)


def final(own, sc, aux, x, hg, z, b, c, local_parts, el, extra):
    in_specs = [AUX_BLOCK, TOKEN_BLOCK, LOCAL_BLOCK, TOKEN_BLOCK, BC_BLOCK, BC_BLOCK]
    in_specs += [LOCAL_BLOCK, LOCAL_BLOCK, LOCAL_BC, LOCAL_BC, EL_BLOCK]
    scratch = [SPREAD]
    aliases = {}
    if own:
        in_specs.append(STATE_BLOCK)
        scratch.append(pltpu.VMEM((N, 2 * W), BF16))
    else:
        aliases = {1 + len(in_specs) + k: k for k in range(4)}
        in_specs += [pl.BlockSpec(memory_space=pl.ANY)] * 4
    return pl.pallas_call(
        functools.partial(final_kernel, own),
        grid_spec=pltpu.PrefetchScalarGridSpec(
            num_scalar_prefetch=1,
            grid=(HALF,),
            in_specs=in_specs,
            out_specs=[TOKEN_BLOCK, TOKEN_BLOCK, BC_BLOCK, BC_BLOCK],
            scratch_shapes=scratch,
        ),
        out_shape=[
            jax.ShapeDtypeStruct((T, NH * P_SIZE), BF16),
            jax.ShapeDtypeStruct((T, NH * P_SIZE), F32),
            jax.ShapeDtypeStruct((T, NG * N), F32),
            jax.ShapeDtypeStruct((T, NG * N), F32),
        ],
        input_output_aliases=aliases,
        compiler_params=params(),
        name="final_own" if own else "final_other",
    )(sc, aux, x, hg, z, b, c, *local_parts, el, *extra)


def body(ssm_input, gate_input, b_input, c_input, dt_raw, dt_bias, a_log, skip_gain, out_grad):
    ctx_count = lax.axis_size("ctx")
    head_count = lax.axis_size("head")
    core = (lax.axis_index("head") % 2).astype(jnp.int32)
    sc_other = jnp.stack([HALF * (1 - core), core])
    sc_own = jnp.stack([HALF * core, core])
    bias, alog, skip = dt_bias[None, :], a_log[None, :], skip_gain[None, :]
    swap = [(k, k ^ 1) for k in range(head_count)]
    chips = [[2 * k + c for k in range(ctx_count * head_count // 2)] for c in range(2)]

    def exchange(parts):
        return lax.all_to_all(
            parts, ("ctx", "head"), split_axis=0, concat_axis=0, tiled=True, axis_index_groups=chips
        )

    tokens = (ssm_input, gate_input, out_grad, b_input, c_input)
    send, hg_other, aux = states(True, sc_other, dt_raw, bias, alog, *tokens)
    got = lax.ppermute(send, "head", swap)
    keep, hg_own = states(False, sc_own, aux, *tokens)
    gathered = exchange(merge(sc_own, keep, got))
    loc_own = local("local_own", sc_own, aux, skip, ssm_input, hg_own, b_input, c_input)
    back = exchange(scan(gathered, loc_own[3]))
    loc_other = local("local_other", sc_other, aux, skip, ssm_input, hg_other, b_input, c_input)
    el = back.reshape(HALF * N, 2 * W)
    el_other = lax.ppermute(pass_on(sc_own, el, keep, loc_other[3]), "head", swap)
    shared = (gate_input, b_input, c_input)
    outs = final(True, sc_own, aux, ssm_input, hg_own, *shared, loc_own, el, (got,))
    return tuple(
        final(False, sc_other, aux, ssm_input, hg_other, *shared, loc_other, el_other, tuple(outs))
    )


def solution(mesh):
    row_spec = P(("ctx", "head"), None)
    in_specs = (row_spec,) * 5 + (P(), P(), P(), row_spec)
    return jax.shard_map(
        body, mesh=mesh, in_specs=in_specs, out_specs=(row_spec,) * 4, check_vma=False
    )
```

profile of v0, /device:TPU:1, one launch (start us, length us, event | category | flops | bytes accessed | tf_op | source)
XLA Modules:
  0.0 136.9 jit_solution(10737580974681563638)
XLA Ops:
  0.6 0.1 pad_add_fusion.sc_ref
  0.7 1.6 %copy-done = bf16[128,8192]{1,0:T(8,128)(2,1)S(1)} copy-done((bf16[128,8192]{1,0:T(8,128)(2,1)S(1)}, bf16[128,8192]{1,0:T(8,128)(2,1)}, u32[]{:S(2)}) %copy-start) | copy-done | bytes 2097176
  2.3 0.0 copy-start.3
  2.3 1.6 %copy-done.3 = bf16[128,8192]{1,0:T(8,128)(2,1)S(1)} copy-done((bf16[128,8192]{1,0:T(8,128)(2,1)S(1)}, bf16[128,8192]{1,0:T(8,128)(2,1)}, u32[]{:S(2)}) %copy-start.3) | copy-done | bytes 2097176
  3.9 0.0 copy-start.6
  3.9 0.9 copy-done.6
  4.9 0.0 copy-start.8
  4.9 0.9 copy-done.8
  5.8 0.0 copy-start.24
  5.8 0.8 copy-done.24
  6.6 0.0 copy-start.26
  6.6 0.7 copy-done.26
  7.2 0.0 copy-start.27
  7.2 0.7 copy-done.27
  7.9 0.0 copy-start.1
  7.9 0.0 copy-start.7
  7.9 0.0 copy-start.9
  7.9 6.6 %states_send.1 = (bf16[512,2176]{1,0:T(8,128)(2,1)}, bf16[128,4096]{1,0:T(8,128)(2,1)S(1)}, f32[4,128,128]{2,1,0:T(8,128)S(1)}) custom-call(s32[2]{0:T(128)S(1)} %pad_add_fusion.sc_ref, bf16[128,128]{1,0:T(8,128)(2,1)S(1)} %copy-done.24, f32[1,128]{1,0:T(1,128)S(1)} %bitcast.11, f32[1,128]{1,0:T(1,128)S(1)} %bitcast.12, bf16[128,8192]{1,0:T(8,128)(2,1)S(1)} %copy-done, ...), custom_call_target="tpu_custom_call" | custom-call | tf_op jit(solution)/shard_map/states_send/pallas_call | solution.py:150
  14.5 0.0 copy-start.12
  14.5 1.0 copy-done.12
  15.5 1.4 %collective-permute-start = (bf16[512,2176]{1,0:T(8,128)(2,1)}, bf16[512,2176]{1,0:T(8,128)(2,1)}, u32[]{:S(2)}, u32[]{:S(2)}) collective-permute-start(bf16[512,2176]{1,0:T(8,128)(2,1)} %get-tuple-element.28), channel_id=1, source_target_pairs={{0,1},{1,0},{2,3},{3,2},{4,5},{5,4},{6,7},{7,6},{8,9},{9,8},{10,11... | collective-permute-start | bytes 6684680 | tf_op jit(solution)/shard_map/ppermute | solution.py:449
  16.9 0.1 pad_add_fusion.1.sc_ref
  17.0 0.0 copy-done.1
  17.0 0.0 copy-done.7
  17.0 0.0 copy-done.9
  17.0 0.0 copy-start.4
  17.0 1.6 %copy-done.4 = bf16[128,8192]{1,0:T(8,128)(2,1)S(1)} copy-done((bf16[128,8192]{1,0:T(8,128)(2,1)S(1)}, bf16[128,8192]{1,0:T(8,128)(2,1)}, u32[]{:S(2)}) %copy-start.4) | copy-done | bytes 2097176
  18.6 6.2 %states_keep.1 = (bf16[512,2176]{1,0:T(8,128)(2,1)}, bf16[128,4096]{1,0:T(8,128)(2,1)S(1)}) custom-call(s32[2]{0:T(128)S(1)} %pad_add_fusion.1.sc_ref, f32[4,128,128]{2,1,0:T(8,128)S(1)} %get-tuple-element.21.aux_ref.refs_0_, bf16[128,8192]{1,0:T(8,128)(2,1)S(1)} %copy-done.1, bf16[128,8192]{1,0:T(8,128)(2,1)S(1)} %copy-done.4, bf16[128,8192]{1,0:T(8,128)(2,1)} %refs_3_.5, ...), custom_call_target="tpu_custom_call" | custom-call | tf_op jit(solution)/shard_map/states_keep/pallas_call | solution.py:150
  24.8 0.0 copy-start.15
  24.8 1.0 copy-done.15
  25.8 0.0 collective-permute-done.got_ref.refs_11_
  25.8 1.6 %copy-done.10 = bf16[512,2176]{1,0:T(8,128)(2,1)S(1)} copy-done((bf16[512,2176]{1,0:T(8,128)(2,1)S(1)}, bf16[512,2176]{1,0:T(8,128)(2,1)}, u32[]{:S(2)}) %copy-start.10) | copy-done | bytes 2228248
  27.4 4.9 %merge_cores.1 = bf16[64,8,2176]{2,1,0:T(8,128)(2,1)} custom-call(s32[2]{0:T(128)S(1)} %pad_add_fusion.1.sc_ref, bf16[512,2176]{1,0:T(8,128)(2,1)S(1)} %copy-done.10, bf16[512,2176]{1,0:T(8,128)(2,1)} %collective-permute-done.got_ref.refs_11_), custom_call_target="tpu_custom_call" | custom-call | tf_op jit(solution)/shard_map/merge_cores/pallas_call | solution.py:198
  32.4 11.6 %all-to-all-start = ((bf16[64,8,2176]{2,1,0:T(8,128)(2,1)}), bf16[64,8,2176]{2,1,0:T(8,128)(2,1)}, u32[]{:S(2)}, u32[]{:S(2)}) async-start(bf16[64,8,2176]{2,1,0:T(8,128)(2,1)} %merge_cores.1), calls=%async_computation | async-start | bytes 4456448 | tf_op jit(solution)/shard_map/all_to_all | solution.py:443
  44.0 0.0 copy-done.16
  44.0 0.0 copy-done.25
  44.0 7.8 %local_own.1 = (f32[128,4096]{1,0:T(8,128)S(1)}, f32[128,4096]{1,0:T(8,128)}, f32[128,512]{1,0:T(8,128)S(1)}, f32[128,512]{1,0:T(8,128)S(1)}) custom-call(s32[2]{0:T(128)S(1)} %pad_add_fusion.1.sc_ref, f32[4,128,128]{2,1,0:T(8,128)S(1)} %get-tuple-element.21.aux_ref.refs_0_, f32[1,128]{1,0:T(1,128)S(1)} %bitcast.9, bf16[128,8192]{1,0:T(8,128)(2,1)} %refs_1_.5, ...), custom_call_target="tpu_custom_call" | custom-call | tf_op jit(solution)/shard_map/local_own/pallas_call | solution.py:337
  51.8 1.4 %copy-done.19 = f32[128,4096]{1,0:T(8,128)} copy-done((f32[128,4096]{1,0:T(8,128)}, f32[128,4096]{1,0:T(8,128)S(1)}, u32[]{:S(2)}) %copy-start.19) | copy-done | bytes 2097176
  53.3 20.7 %all-to-all-done.in_ref = bf16[64,8,2176]{2,1,0:T(8,128)(2,1)} async-done(((bf16[64,8,2176]{2,1,0:T(8,128)(2,1)}), bf16[64,8,2176]{2,1,0:T(8,128)(2,1)}, u32[]{:S(2)}, u32[]{:S(2)}) %all-to-all-start) | async-done | bytes 2228256 | tf_op jit(solution)/shard_map/all_to_all | solution.py:443
  74.0 2.7 %scan_chips.1 = bf16[64,8,2048]{2,1,0:T(8,128)(2,1)S(1)} custom-call(bf16[64,8,2176]{2,1,0:T(8,128)(2,1)} %all-to-all-done.in_ref, f32[128,512]{1,0:T(8,128)S(1)} %get-tuple-element.30.after_ref.refs_9_), custom_call_target="tpu_custom_call" | custom-call | tf_op jit(solution)/shard_map/scan_chips/pallas_call | solution.py:233
  76.7 0.0 copy-done.22
  76.7 0.0 copy-start.11
  76.7 1.3 copy-done.11
  78.0 6.4 %all-to-all-start.1 = ((bf16[64,8,2048]{2,1,0:T(8,128)(2,1)}), bf16[64,8,2048]{2,1,0:T(8,128)(2,1)S(1)}, u32[]{:S(2)}, u32[]{:S(2)}) async-start(bf16[64,8,2048]{2,1,0:T(8,128)(2,1)} %copy-done.11), calls=%async_computation.1 | async-start | bytes 4194304 | tf_op jit(solution)/shard_map/all_to_all | solution.py:443
  84.4 0.0 copy-start.13
  84.4 1.2 copy-done.13
  85.7 7.8 %local_other.1 = (f32[128,4096]{1,0:T(8,128)S(1)}, f32[128,4096]{1,0:T(8,128)}, f32[128,512]{1,0:T(8,128)S(1)}, f32[128,512]{1,0:T(8,128)S(1)}) custom-call(s32[2]{0:T(128)S(1)} %pad_add_fusion.sc_ref, f32[4,128,128]{2,1,0:T(8,128)S(1)} %get-tuple-element.21.aux_ref.refs_0_, f32[1,128]{1,0:T(1,128)S(1)} %bitcast.10, bf16[128,8192]{1,0:T(8,128)(2,1)} %refs_1_.5, ...), custom_call_target="tpu_custom_call" | custom-call | tf_op jit(solution)/shard_map/local_other/pallas_call | solution.py:337
  93.5 1.4 %copy-done.18 = f32[128,4096]{1,0:T(8,128)} copy-done((f32[128,4096]{1,0:T(8,128)}, f32[128,4096]{1,0:T(8,128)S(1)}, u32[]{:S(2)}) %copy-start.18) | copy-done | bytes 2097176
  94.9 0.7 copy-done.20
  95.6 16.4 %all-to-all-done.1 = bf16[64,8,2048]{2,1,0:T(8,128)(2,1)S(1)} async-done(((bf16[64,8,2048]{2,1,0:T(8,128)(2,1)}), bf16[64,8,2048]{2,1,0:T(8,128)(2,1)S(1)}, u32[]{:S(2)}, u32[]{:S(2)}) %all-to-all-start.1) | async-done | bytes 2097184 | tf_op jit(solution)/shard_map/all_to_all | solution.py:443
  111.9 4.5 %pass_on.1 = bf16[512,2048]{1,0:T(8,128)(2,1)S(1)} custom-call(s32[2]{0:T(128)S(1)} %pad_add_fusion.1.sc_ref, bf16[512,2048]{1,0:T(8,128)(2,1)S(1)} %bitcast.7, bf16[512,2176]{1,0:T(8,128)(2,1)} %get-tuple-element.27.own_ref, f32[128,512]{1,0:T(8,128)S(1)} %get-tuple-element.26.after_ref.refs_9_), custom_call_target="tpu_custom_call" | custom-call | tf_op jit(solution)/shard_map/pass_on/pallas_call | solution.py:265
  116.5 0.0 copy-done.5
  116.5 3.2 %collective-permute-start.1 = (bf16[512,2048]{1,0:T(8,128)(2,1)S(1)}, bf16[512,2048]{1,0:T(8,128)(2,1)S(1)}, u32[]{:S(2)}, u32[]{:S(2)}) collective-permute-start(bf16[512,2048]{1,0:T(8,128)(2,1)S(1)} %pass_on.1), channel_id=1, source_target_pairs={{0,1},{1,0},{2,3},{3,2},{4,5},{5,4},{6,7},{7,6},{8,9},{9,8},{10,11... | collective-permute-start | bytes 6291464 | tf_op jit(solution)/shard_map/ppermute | solution.py:456
  119.7 0.0 copy-done.2
  119.7 0.0 copy-done.17
  119.7 0.0 copy-done.23
  119.7 0.0 copy-start.21
  119.7 8.4 %final_own.1 = (bf16[128,8192]{1,0:T(8,128)(2,1)}, f32[128,8192]{1,0:T(8,128)}, f32[128,1024]{1,0:T(8,128)}, f32[128,1024]{1,0:T(8,128)}) custom-call(s32[2]{0:T(128)S(1)} %pad_add_fusion.1.sc_ref, f32[4,128,128]{2,1,0:T(8,128)S(1)} %get-tuple-element.21.aux_ref.refs_0_, bf16[128,8192]{1,0:T(8,128)(2,1)S(1)} %copy-done.2, bf16[128,4096]{1,0:T(8,128)(2,1)S(1)} %copy-done.17, ...), custom_call_target="tpu_custom_call" | custom-call | tf_op jit(solution)/shard_map/final_own/pallas_call | solution.py:411
  128.1 0.0 collective-permute-done.1.refs_10_
  128.1 0.0 copy-start.28
  128.1 1.4 copy-done.28
  129.5 0.0 copy-done.14
  129.5 0.0 copy-done.21
  129.5 7.4 %final_other.1 = (bf16[128,8192]{1,0:T(8,128)(2,1)}, f32[128,8192]{1,0:T(8,128)}, f32[128,1024]{1,0:T(8,128)}, f32[128,1024]{1,0:T(8,128)}) custom-call(s32[2]{0:T(128)S(1)} %pad_add_fusion.sc_ref, f32[4,128,128]{2,1,0:T(8,128)S(1)} %get-tuple-element.21.aux_ref.refs_0_, ...), custom_call_target="tpu_custom_call", output_to_operand_aliasing={{0}: (12, {}), {1}: (13, {}), {2}: (14, {}), {3}: (15, {})} | custom-call | tf_op jit(solution)/shard_map/final_other/pallas_call | solution.py:411
  (13 shorter events, 0.0 us)
Async XLA Ops:
  0.7 1.6 %copy-start = (bf16[128,8192]{1,0:T(8,128)(2,1)S(1)}, bf16[128,8192]{1,0:T(8,128)(2,1)}, u32[]{:S(2)}) copy-start(bf16[128,8192]{1,0:T(8,128)(2,1)} %refs_1_.5) | copy-start | bytes 6291460
  2.3 1.6 %copy-start.3 = (bf16[128,8192]{1,0:T(8,128)(2,1)S(1)}, bf16[128,8192]{1,0:T(8,128)(2,1)}, u32[]{:S(2)}) copy-start(bf16[128,8192]{1,0:T(8,128)(2,1)} %refs_3_.7) | copy-start | bytes 6291460
  3.9 0.9 copy-start.6
  4.9 0.9 copy-start.8
  5.8 0.8 copy-start.24
  6.6 0.7 copy-start.26
  7.2 0.7 copy-start.27
  7.9 9.1 %copy-start.1 = (bf16[128,8192]{1,0:T(8,128)(2,1)S(1)}, bf16[128,8192]{1,0:T(8,128)(2,1)}, u32[]{:S(2)}) copy-start(bf16[128,8192]{1,0:T(8,128)(2,1)} %refs_1_.5) | copy-start | bytes 6291460
  7.9 9.1 %copy-start.7 = (bf16[128,1024]{1,0:T(8,128)(2,1)S(1)}, bf16[128,1024]{1,0:T(8,128)(2,1)}, u32[]{:S(2)}) copy-start(bf16[128,1024]{1,0:T(8,128)(2,1)} %refs_4_.7) | copy-start | bytes 786436
  7.9 9.1 %copy-start.9 = (bf16[128,1024]{1,0:T(8,128)(2,1)S(1)}, bf16[128,1024]{1,0:T(8,128)(2,1)}, u32[]{:S(2)}) copy-start(bf16[128,1024]{1,0:T(8,128)(2,1)} %refs_5_.7) | copy-start | bytes 786436
  14.5 1.0 copy-start.12
  15.5 10.3 %collective-permute-start = (bf16[512,2176]{1,0:T(8,128)(2,1)}, bf16[512,2176]{1,0:T(8,128)(2,1)}, u32[]{:S(2)}, u32[]{:S(2)}) collective-permute-start(bf16[512,2176]{1,0:T(8,128)(2,1)} %get-tuple-element.28), channel_id=1, source_target_pairs={{0,1},{1,0},{2,3},{3,2},{4,5},{5,4},{6,7},{7,6},{8,9},{9,8},{10,11... | collective-permute-start | bytes 6684680 | tf_op jit(solution)/shard_map/ppermute | solution.py:449
  17.0 1.6 %copy-start.4 = (bf16[128,8192]{1,0:T(8,128)(2,1)S(1)}, bf16[128,8192]{1,0:T(8,128)(2,1)}, u32[]{:S(2)}) copy-start(bf16[128,8192]{1,0:T(8,128)(2,1)} %refs_3_.7) | copy-start | bytes 6291460
  24.8 1.0 copy-start.15
  25.8 1.6 %copy-start.10 = (bf16[512,2176]{1,0:T(8,128)(2,1)S(1)}, bf16[512,2176]{1,0:T(8,128)(2,1)}, u32[]{:S(2)}) copy-start(bf16[512,2176]{1,0:T(8,128)(2,1)} %get-tuple-element.27.own_ref) | copy-start | bytes 6684676
  32.4 11.6 %copy-start.16 = (bf16[128,4096]{1,0:T(8,128)(2,1)S(1)}, bf16[128,4096]{1,0:T(8,128)(2,1)}, u32[]{:S(2)}) copy-start(bf16[128,4096]{1,0:T(8,128)(2,1)} %copy-done.15) | copy-start | bytes 3145732
  32.4 11.6 %copy-start.25 = (f32[128]{0:T(128)S(1)}, f32[128]{0:T(128)}, u32[]{:S(2)}) copy-start(f32[128]{0:T(128)} %param.16) | copy-start | bytes 1540
  32.4 41.6 %all-to-all-start = ((bf16[64,8,2176]{2,1,0:T(8,128)(2,1)}), bf16[64,8,2176]{2,1,0:T(8,128)(2,1)}, u32[]{:S(2)}, u32[]{:S(2)}) async-start(bf16[64,8,2176]{2,1,0:T(8,128)(2,1)} %merge_cores.1), calls=%async_computation | async-start | bytes 4456448 | tf_op jit(solution)/shard_map/all_to_all | solution.py:443
  51.8 1.4 %copy-start.19 = (f32[128,4096]{1,0:T(8,128)}, f32[128,4096]{1,0:T(8,128)S(1)}, u32[]{:S(2)}) copy-start(f32[128,4096]{1,0:T(8,128)S(1)} %get-tuple-element.31.refs_6_) | copy-start | bytes 6291460
  53.3 23.4 %copy-start.22 = (f32[128,512]{1,0:T(8,128)}, f32[128,512]{1,0:T(8,128)S(1)}, u32[]{:S(2)}) copy-start(f32[128,512]{1,0:T(8,128)S(1)} %get-tuple-element.33.refs_8_) | copy-start | bytes 786436
  76.7 1.3 copy-start.11
  78.0 33.9 %all-to-all-start.1 = ((bf16[64,8,2048]{2,1,0:T(8,128)(2,1)}), bf16[64,8,2048]{2,1,0:T(8,128)(2,1)S(1)}, u32[]{:S(2)}, u32[]{:S(2)}) async-start(bf16[64,8,2048]{2,1,0:T(8,128)(2,1)} %copy-done.11), calls=%async_computation.1 | async-start | bytes 4194304 | tf_op jit(solution)/shard_map/all_to_all | solution.py:443
  84.4 1.2 copy-start.13
  93.5 1.4 %copy-start.18 = (f32[128,4096]{1,0:T(8,128)}, f32[128,4096]{1,0:T(8,128)S(1)}, u32[]{:S(2)}) copy-start(f32[128,4096]{1,0:T(8,128)S(1)} %get-tuple-element.23.refs_6_) | copy-start | bytes 6291460
  94.9 0.7 copy-start.20
  111.9 4.5 %copy-start.5 = (bf16[64,8,2048]{2,1,0:T(8,128)(2,1)}, bf16[64,8,2048]{2,1,0:T(8,128)(2,1)S(1)}, u32[]{:S(2)}) copy-start(bf16[64,8,2048]{2,1,0:T(8,128)(2,1)S(1)} %all-to-all-done.1) | copy-start | bytes 6291460
  111.9 7.7 %copy-start.2 = (bf16[128,8192]{1,0:T(8,128)(2,1)S(1)}, bf16[128,8192]{1,0:T(8,128)(2,1)}, u32[]{:S(2)}) copy-start(bf16[128,8192]{1,0:T(8,128)(2,1)} %refs_1_.5) | copy-start | bytes 6291460
  111.9 7.7 %copy-start.17 = (bf16[128,4096]{1,0:T(8,128)(2,1)S(1)}, bf16[128,4096]{1,0:T(8,128)(2,1)}, u32[]{:S(2)}) copy-start(bf16[128,4096]{1,0:T(8,128)(2,1)} %copy-done.15) | copy-start | bytes 3145732
  111.9 7.7 %copy-start.23 = (f32[128,512]{1,0:T(8,128)S(1)}, f32[128,512]{1,0:T(8,128)}, u32[]{:S(2)}) copy-start(f32[128,512]{1,0:T(8,128)} %copy-done.22) | copy-start | bytes 786436
  116.5 11.6 %collective-permute-start.1 = (bf16[512,2048]{1,0:T(8,128)(2,1)S(1)}, bf16[512,2048]{1,0:T(8,128)(2,1)S(1)}, u32[]{:S(2)}, u32[]{:S(2)}) collective-permute-start(bf16[512,2048]{1,0:T(8,128)(2,1)S(1)} %pass_on.1), channel_id=1, source_target_pairs={{0,1},{1,0},{2,3},{3,2},{4,5},{5,4},{6,7},{7,6},{8,9},{9,8},{10,11... | collective-permute-start | bytes 6291464 | tf_op jit(solution)/shard_map/ppermute | solution.py:456
  119.7 9.8 %copy-start.14 = (bf16[128,4096]{1,0:T(8,128)(2,1)S(1)}, bf16[128,4096]{1,0:T(8,128)(2,1)}, u32[]{:S(2)}) copy-start(bf16[128,4096]{1,0:T(8,128)(2,1)} %copy-done.12) | copy-start | bytes 3145732
  119.7 9.8 %copy-start.21 = (f32[128,512]{1,0:T(8,128)S(1)}, f32[128,512]{1,0:T(8,128)}, u32[]{:S(2)}) copy-start(f32[128,512]{1,0:T(8,128)} %copy-done.20) | copy-start | bytes 786436
  128.1 1.4 copy-start.28
where the time goes:
time: 138 us; the launch traced here: 137 us
  Pallas kernels  56.4 us (41%)
  waiting for transfers between devices  37.1 us (27%)
  starting transfers between devices  22.6 us (16%)
  local copies, waits for them, and re-layouts  19.8 us (14%)
    all_to_all x2, waiting for transfers between devices, exchange(): lax.all_to_all(parts, ('ctx', 'head'), split_axis=0, concat_axis=0, tiled...  37.1 us
    unnamed x58, local copies, waits for them, and re-layouts  19.8 us
    all_to_all x2, starting transfers between devices, exchange(): lax.all_to_all(parts, ('ctx', 'head'), split_axis=0, concat_axis=0, tiled...  18 us
    pallas_call x2, Pallas kernels, final(): pl.pallas_call(functools.partial(final_kernel, own), grid_spec=pltpu.Pref...  15.8 us
    pallas_call x2, Pallas kernels, local(): pl.pallas_call(local_kernel, grid_spec=pltpu.PrefetchScalarGridSpec(num_s...  15.6 us
    pallas_call x2, Pallas kernels, states(): pl.pallas_call(functools.partial(states_kernel, first), grid_spec=pltpu.P...  12.9 us
    pallas_call x1, Pallas kernels, merge(): pl.pallas_call(merge_kernel, grid_spec=pltpu.PrefetchScalarGridSpec(num_s...  4.93 us
    pallas_call x1, Pallas kernels, pass_on(): pl.pallas_call(pass_on_kernel, grid_spec=pltpu.PrefetchScalarGridSpec(num...  4.52 us
  transfers between devices with their start and end apart: 4, of which 2 were waited for; matrix products, arithmetic and copies ran while one was open for 0% of the time, Pallas kernels for 22%

commit v1 on v0

v1 whole, which is shorter than its diff:
```python
import functools

import jax
import jax.numpy as jnp
from jax import lax
from jax.experimental import pallas as pl
from jax.experimental.pallas import tpu as pltpu
from jax.sharding import PartitionSpec as P

NH = 128
P_SIZE = 64
N = 128
NG = 8
PER = NH // NG
W = PER * P_SIZE
T = 128
HALF = NG // 2
LANES = 128
WIDE = 2 * W + LANES
F32 = jnp.float32
BF16 = jnp.bfloat16


MIB = 1024 * 1024
NT = (((1,), (1,)), ((), ()))
CHUNK = 256
HBM_SPEC = pl.BlockSpec(memory_space=pl.ANY)
VMEM_SPEC = pl.BlockSpec(memory_space=pltpu.VMEM)
SMEM_SPEC = pl.BlockSpec(memory_space=pltpu.SMEM)
SPREAD = pltpu.VMEM((LANES, W), BF16)


def in_hbm(values):
    return pltpu.with_memory_space_constraint(values, pltpu.HBM)


def params(mib):
    return pltpu.CompilerParams(vmem_limit_bytes=mib * MIB)


def lane(shape):
    return lax.broadcasted_iota(jnp.int32, shape, len(shape) - 1)


def fill_spread(e_ref):
    row = lax.broadcasted_iota(jnp.int32, (LANES, W), 0)
    col = lax.broadcasted_iota(jnp.int32, (LANES, W), 1)
    e_ref[...] = jnp.where((row & 63) == (col >> 6), 1.0, 0.0).astype(BF16)


def to_half(values, base):
    return pltpu.roll(values, lax.rem(LANES - PER * base, LANES), 1)


def pair_up(values):
    high = values.astype(BF16).astype(F32)
    low = values - high
    return jnp.where(lane(values.shape) < 64, high, pltpu.roll(low, 64, 1))


def of_group(pairs, i):
    if i:
        pairs = pltpu.roll(pairs, LANES - PER * i, 1)
    return pairs.astype(BF16)


def silu(v):
    return v * (0.5 * jnp.tanh(0.5 * v) + 0.5)


def steps_of(dt_ref, bias_ref, alog_ref):
    u = jnp.exp(dt_ref[...].astype(F32) + bias_ref[...])
    one = 1.0 + u
    step = jnp.where(one == 1.0, u, jnp.log(one) * (u / jnp.where(one == 1.0, 1.0, one - 1.0)))
    rate = -step * jnp.exp(alog_ref[...])
    row = lax.broadcasted_iota(jnp.int32, (T, T), 0)
    col = lax.broadcasted_iota(jnp.int32, (T, T), 1)
    tri = jnp.where(row >= col, 1.0, 0.0).astype(BF16)
    running = jnp.zeros((T, NH), F32)
    for _ in range(3):
        piece = rate.astype(BF16)
        running = running + jnp.dot(tri, piece, preferred_element_type=F32)
        rate = rate - piece.astype(F32)
    from_start = jnp.exp(running)
    to_end = jnp.exp(running[T - 1 : T] - running) * step
    return step, running, from_start, to_end


def columns(base, i, width):
    return pl.ds(pl.multiple_of((base + i) * width, width), width)


def states_kernel(first, sc_ref, *refs):
    if first:
        dt_hbm, bias_hbm, alog_hbm, x_hbm, z_hbm, og_hbm, b_hbm, c_hbm, st_hbm, aux_hbm = refs[:10]
        small = ((dt_hbm, refs[-3]), (bias_hbm, refs[-2]), (alog_hbm, refs[-1]))
    else:
        aux_hbm, x_hbm, z_hbm, og_hbm, b_hbm, c_hbm, st_hbm = refs[:7]
    e_ref, x_ref, z_ref, og_ref, b_ref, c_ref, st_ref, aux_ref, sem, sem_out, sem_small = refs[
        (10 if first else 7) : (21 if first else 18)
    ]
    base = sc_ref[0]
    if not first:
        small = ((aux_hbm, aux_ref),)
    smalls = [pltpu.make_async_copy(s, d, sem_small.at[k]) for k, (s, d) in enumerate(small)]
    for copy in smalls:
        copy.start()
    copies = []
    for i in range(HALF):
        row = []
        for k, (src, dst, width) in enumerate(
            (
                (b_hbm, b_ref, N),
                (x_hbm, x_ref, W),
                (c_hbm, c_ref, N),
                (z_hbm, z_ref, W),
                (og_hbm, og_ref, W),
            )
        ):
            row.append(
                pltpu.make_async_copy(src.at[:, columns(base, i, width)], dst.at[i], sem.at[i, k])
            )
            row[-1].start()
        copies.append(row)
    fill_spread(e_ref)
    for copy in smalls:
        copy.wait()
    stores = []
    if first:
        for k, v in enumerate(steps_of(refs[-3], refs[-2], refs[-1])):
            aux_ref[k] = v
        stores.append(pltpu.make_async_copy(aux_ref, aux_hbm, sem_small.at[3]))
        stores[0].start()
    from_start = pair_up(to_half(aux_ref[2], base))
    to_end = pair_up(to_half(aux_ref[3], base))
    for i in range(HALF):
        for copy in copies[i]:
            copy.wait()
        here = slice(i * N, (i + 1) * N)
        te = of_group(to_end, i)
        fs = of_group(from_start, i)
        bt = b_ref[i].T
        ct = c_ref[i].T
        for k in range(W // CHUNK):
            cut = slice(k * CHUNK, (k + 1) * CHUNK)
            e = e_ref[:, cut]
            xs = x_ref[i, :, cut].astype(F32) * jnp.dot(te, e, preferred_element_type=F32)
            st_ref[here, cut] = jnp.dot(
                bt, xs.astype(BF16), preferred_element_type=F32
            ).astype(BF16)
            gate = silu(z_ref[i, :, cut].astype(F32))
            hg = (og_ref[i, :, cut].astype(F32) * gate).astype(BF16)
            gs = hg.astype(F32) * jnp.dot(fs, e, preferred_element_type=F32)
            st_ref[here, slice(W + k * CHUNK, W + (k + 1) * CHUNK)] = jnp.dot(
                ct, gs.astype(BF16), preferred_element_type=F32
            ).astype(BF16)
        decay = jnp.broadcast_to(fs[T - 16 : T].astype(F32)[15:16], (N, LANES))
        st_ref[here, 2 * W :] = decay.astype(BF16)
        stores.append(pltpu.make_async_copy(st_ref.at[here], st_hbm.at[here], sem_out.at[i]))
        stores[-1].start()
    for store in stores:
        store.wait()


def states(first, sc, *args):
    out_shape = [pltpu.HBM((HALF * N, WIDE), BF16)]
    scratch = (
        [SPREAD]
        + [pltpu.VMEM((HALF, T, W), BF16)] * 3
        + [pltpu.VMEM((HALF, T, N), BF16)] * 2
        + [pltpu.VMEM((HALF * N, WIDE), BF16), pltpu.VMEM((4, T, NH), F32)]
        + [pltpu.SemaphoreType.DMA((HALF, 5)), pltpu.SemaphoreType.DMA((HALF,))]
        + [pltpu.SemaphoreType.DMA((4,))]
    )
    if first:
        out_shape.append(pltpu.HBM((4, T, NH), F32))
        scratch += [pltpu.VMEM((T, NH), BF16), pltpu.VMEM((1, NH), F32), pltpu.VMEM((1, NH), F32)]
    return pl.pallas_call(
        functools.partial(states_kernel, first),
        in_specs=[SMEM_SPEC] + [HBM_SPEC] * len(args),
        out_specs=[HBM_SPEC] * len(out_shape),
        out_shape=out_shape,
        scratch_shapes=scratch,
        compiler_params=params(24),
        name="states_send" if first else "states_keep",
    )(sc, *[in_hbm(a) for a in args])


def decay_row(state_ref, at, e_ref):
    pairs = state_ref[at : at + 16, 2 * W :]
    return jnp.dot(pairs, e_ref[...], preferred_element_type=F32)[0:1]


def merge_kernel(sc_ref, own_hbm, got_hbm, out_hbm, e_ref, own_ref, got_ref, out_ref, sem, sem_out):
    loads = []
    for i in range(HALF):
        here = slice(i * N, (i + 1) * N)
        pair = (
            pltpu.make_async_copy(own_hbm.at[here], own_ref.at[here], sem.at[i, 0]),
            pltpu.make_async_copy(got_hbm.at[here], got_ref.at[here], sem.at[i, 1]),
        )
        for copy in pair:
            copy.start()
        loads.append(pair)
    fill_spread(e_ref)

    def merge(r0, r1):
        stores = []
        for i in range(HALF):
            for copy in loads[i]:
                copy.wait()
            here = slice(i * N, (i + 1) * N)
            there = slice(i * N // 8, (i + 1) * N // 8)
            d0 = decay_row(r0, i * N, e_ref)
            d1 = decay_row(r1, i * N, e_ref)
            for k in range(W // CHUNK):
                cut = slice(k * CHUNK, (k + 1) * CHUNK)
                forward = d1[:, cut] * r0[here, cut].astype(F32) + r1[here, cut].astype(F32)
                out_ref[there, :, cut] = forward.reshape(N // 8, 8, CHUNK).astype(BF16)
                back = slice(W + k * CHUNK, W + (k + 1) * CHUNK)
                backward = r0[here, back].astype(F32) + d0[:, cut] * r1[here, back].astype(F32)
                out_ref[there, :, back] = backward.reshape(N // 8, 8, CHUNK).astype(BF16)
            p0 = r0[i * N : i * N + 16, 2 * W :].astype(F32)
            p1 = r1[i * N : i * N + 16, 2 * W :].astype(F32)
            p0 = p0 + pltpu.roll(p0, 64, 1)
            p1 = p1 + pltpu.roll(p1, 64, 1)
            both = pair_up(p0 * p1)[0:8]
            both = jnp.broadcast_to(both[None], (N // 8, 8, LANES))
            out_ref[there, :, 2 * W :] = both.astype(BF16)
            stores.append(pltpu.make_async_copy(out_ref.at[there], out_hbm.at[there], sem_out.at[i]))
            stores[-1].start()
        for store in stores:
            store.wait()

    @pl.when(sc_ref[1] == 0)
    def _():
        merge(own_ref, got_ref)

    @pl.when(sc_ref[1] != 0)
    def _():
        merge(got_ref, own_ref)


def merge(sc, own, got):
    return pl.pallas_call(
        merge_kernel,
        in_specs=[SMEM_SPEC, HBM_SPEC, HBM_SPEC],
        out_specs=HBM_SPEC,
        out_shape=pltpu.HBM((HALF * N // 8, 8, WIDE), BF16),
        scratch_shapes=[
            SPREAD,
            pltpu.VMEM((HALF * N, WIDE), BF16),
            pltpu.VMEM((HALF * N, WIDE), BF16),
            pltpu.VMEM((HALF * N // 8, 8, WIDE), BF16),
            pltpu.SemaphoreType.DMA((HALF, 2)),
            pltpu.SemaphoreType.DMA((HALF,)),
        ],
        compiler_params=params(16),
        name="merge_cores",
    )(sc, in_hbm(own), in_hbm(got))


def scan_kernel(chips, in_ref, after_ref, out_hbm, e_ref, d_ref, out_ref, sem):
    fill_spread(e_ref)
    pairs = in_ref[:, :, 2 * W :].astype(F32).reshape(chips * 8, LANES).astype(BF16)
    d_ref[...] = jnp.dot(pairs, e_ref[...], preferred_element_type=F32).reshape(chips, 8, W)
    zero = jnp.zeros((8, W), F32)

    def forward(k, e):
        out_ref[k, :, :W] = e.astype(BF16)
        return d_ref[k] * e + in_ref[k, :, :W].astype(F32)

    def backward(k, l):
        j = chips - 1 - k
        out_ref[j, :, W:] = l.astype(BF16)
        return d_ref[j] * l + in_ref[j, :, W : 2 * W].astype(F32)

    parts = ((0, chips, slice(0, W)), (chips // 2, chips, slice(W, 2 * W)), (0, chips // 2, slice(W, 2 * W)))
    stores = [
        pltpu.make_async_copy(out_ref.at[a:b, :, cut], out_hbm.at[a:b, :, cut], sem.at[k])
        for k, (a, b, cut) in enumerate(parts)
    ]
    lax.fori_loop(0, chips, forward, zero, unroll=8)
    stores[0].start()
    l = lax.fori_loop(0, chips // 2, backward, zero, unroll=8)
    stores[1].start()
    lax.fori_loop(chips // 2, chips, backward, l, unroll=8)
    stores[2].start()
    for store in stores:
        store.wait()


def scan(parts, after):
    chips = parts.shape[0]
    return pl.pallas_call(
        functools.partial(scan_kernel, chips),
        in_specs=[VMEM_SPEC, HBM_SPEC],
        out_specs=HBM_SPEC,
        out_shape=pltpu.HBM((chips, 8, 2 * W), BF16),
        scratch_shapes=[
            SPREAD,
            pltpu.VMEM((chips, 8, W), F32),
            pltpu.VMEM((chips, 8, 2 * W), BF16),
            pltpu.SemaphoreType.DMA((3,)),
        ],
        compiler_params=params(16),
        name="scan_chips",
    )(parts, in_hbm(after))


def local_kernel(
    sc_ref, aux_ref, skip_ref, got_ref, x_hbm, z_hbm, og_hbm, b_hbm, c_hbm,
    y_ref, dx_ref, xs_ref, gs_ref, pair_ref, db_ref, dc_ref,
    e_ref, x_ref, z_ref, og_ref, b_ref, c_ref, ysum_ref, dxsum_ref, hg_ref,
    runc_ref, run_ref, step_ref, plain_ref, sem,
):
    base = sc_ref[0]
    core = sc_ref[1]
    copies = []
    for i in range(HALF):
        for k, (src, dst, width) in enumerate(
            (
                (x_hbm, x_ref, W),
                (z_hbm, z_ref, W),
                (og_hbm, og_ref, W),
                (b_hbm, b_ref, N),
                (c_hbm, c_ref, N),
            )
        ):
            copies.append(
                pltpu.make_async_copy(src.at[:, columns(base, i, width)], dst.at[i], sem.at[i, k])
            )
            copies[-1].start()
    fill_spread(e_ref)
    start = to_half(aux_ref[2], base)
    end = to_half(aux_ref[3], base)
    gain = to_half(jnp.broadcast_to(skip_ref[...], (16, NH)), base)
    run = to_half(aux_ref[1], base)
    run_t = run.T
    step_t = to_half(aux_ref[0], base).T
    for i in range(HALF):
        decay = got_ref[i * N : i * N + 16, 2 * W :].astype(F32)
        decay = (decay + pltpu.roll(decay, 64, 1))[0:1]
        fs, te, skip, run_c = [pltpu.roll(v, LANES - PER * i, 1) if i else v for v in (start, end, gain, run)]
        plain_ref[i, 0:T] = pair_up(fs).astype(BF16)
        plain_ref[i, T : 2 * T] = pair_up(te).astype(BF16)
        plain_ref[i, 2 * T : 2 * T + 16] = pair_up(skip).astype(BF16)
        pair_ref[i, 0:T] = pair_up(jnp.where(core == 0, fs, fs * decay)).astype(BF16)
        pair_ref[i, T : 2 * T] = pair_up(jnp.where(core == 0, te * decay, te)).astype(BF16)
        runc_ref[i] = run_c
        run_ref[i] = run_t[i * PER : (i + 1) * PER]
        step_ref[i] = step_t[i * PER : (i + 1) * PER]
    for copy in copies:
        copy.wait()
    row = lax.broadcasted_iota(jnp.int32, (T, T), 0)
    col = lax.broadcasted_iota(jnp.int32, (T, T), 1)
    below = row >= col
    left = col < P_SIZE

    def one_group(i, unused):
        b, c = b_ref[i], c_ref[i]
        cb = lax.dot_general(c, b, NT, preferred_element_type=F32)
        run_cols, run_rows, step_rows = runc_ref[i], run_ref[i], step_ref[i]
        mass = jnp.zeros((T, T), F32)
        for pair in range(PER // 2):
            here = slice(pair * LANES, (pair + 1) * LANES)
            e = e_ref[:, here]
            both = jnp.dot(pair_ref[i], e, preferred_element_type=F32)
            skip = jnp.dot(plain_ref[i, 2 * T : 2 * T + 16], e, preferred_element_type=F32)[0:1]
            x = x_ref[i, :, here]
            g = (og_ref[i, :, here].astype(F32) * silu(z_ref[i, :, here].astype(F32))).astype(BF16)
            hg_ref[:, here] = g
            gs_ref[i, :, here] = (g.astype(F32) * both[0:T]).astype(BF16)
            xs_ref[i, :, here] = (x.astype(F32) * both[T : 2 * T]).astype(BF16)
            ys, dxs = [], []
            for k in range(2):
                j = 2 * pair + k
                gap = run_cols[:, j : j + 1] - run_rows[j : j + 1, :]
                weight = jnp.exp(jnp.where(below, gap, -1e30)) * step_rows[j : j + 1, :]
                mine = left if k == 0 else ~left
                inner = lax.dot_general(
                    jnp.where(mine, g, jnp.zeros_like(g)), x, NT, preferred_element_type=F32
                )
                mass = mass + weight * inner
                joint = (weight * cb).astype(BF16)
                ys.append(jnp.dot(joint, x, preferred_element_type=F32))
                dxs.append(jnp.dot(joint.T, g, preferred_element_type=F32))
            ysum_ref[:, here] = jnp.where(left, ys[0], ys[1]) + skip * x.astype(F32)
            dxsum_ref[:, here] = jnp.where(left, dxs[0], dxs[1]) + skip * g.astype(F32)
        high = mass.astype(BF16)
        low = (mass - high.astype(F32)).astype(BF16)
        dc_ref[i] = jnp.dot(high, b, preferred_element_type=F32) + jnp.dot(
            low, b, preferred_element_type=F32
        )
        db_ref[i] = jnp.dot(high.T, c, preferred_element_type=F32) + jnp.dot(
            low.T, c, preferred_element_type=F32
        )
        rows = pl.ds(pl.multiple_of(i * N, N), N)

        @pl.when(core != 0)
        def _():
            partner = got_ref[rows, :W]
            fs = jnp.dot(plain_ref[i, 0:T], e_ref[...], preferred_element_type=F32)
            ysum_ref[...] += fs * jnp.dot(c, partner, preferred_element_type=F32)
            gs = (hg_ref[...].astype(F32) * fs).astype(BF16)
            dc_ref[i] += lax.dot_general(gs, partner, NT, preferred_element_type=F32)

        @pl.when(core == 0)
        def _():
            partner = got_ref[rows, W : 2 * W]
            te = jnp.dot(plain_ref[i, T : 2 * T], e_ref[...], preferred_element_type=F32)
            dxsum_ref[...] += te * jnp.dot(b, partner, preferred_element_type=F32)
            xs = (x_ref[i].astype(F32) * te).astype(BF16)
            db_ref[i] += lax.dot_general(xs, partner, NT, preferred_element_type=F32)

        y_ref[i] = ysum_ref[...].astype(BF16)
        dx_ref[i] = dxsum_ref[...].astype(BF16)
        return unused

    lax.fori_loop(0, HALF, one_group, 0)


def local(name, sc, aux, skip, got, *tokens):
    wide = pltpu.HBM((HALF, T, W), BF16)
    thin = pltpu.HBM((HALF, T, N), F32)
    args = [in_hbm(a) for a in (aux, skip, got, *tokens)]
    return pl.pallas_call(
        local_kernel,
        in_specs=[SMEM_SPEC, VMEM_SPEC, VMEM_SPEC, VMEM_SPEC] + [HBM_SPEC] * 5,
        out_specs=[VMEM_SPEC] * 7,
        out_shape=[wide] * 4 + [pltpu.HBM((HALF, 2 * T, LANES), BF16)] + [thin] * 2,
        scratch_shapes=[SPREAD]
        + [pltpu.VMEM((HALF, T, W), BF16)] * 3
        + [pltpu.VMEM((HALF, T, N), BF16)] * 2
        + [pltpu.VMEM((T, W), F32)] * 2
        + [pltpu.VMEM((T, W), BF16)]
        + [pltpu.VMEM((HALF, T, LANES), F32)]
        + [pltpu.VMEM((HALF, PER, T), F32)] * 2
        + [pltpu.VMEM((HALF, 2 * T + 16, LANES), BF16)]
        + [pltpu.SemaphoreType.DMA((HALF, 5))],
        compiler_params=params(24),
        name=name,
    )(sc, *args)


def final_kernel(aliased, sc_ref, el_ref, *refs):
    sources = refs[:10]
    refs = refs[10 + (4 if aliased else 0) :]
    out_hbm, dx_hbm, db_hbm, dc_hbm = refs[:4]
    e_ref, *targets = refs[4:15]
    out_ref, dx_ref, db_ref, dc_ref, sem_in, sem_out = refs[15:]
    b_ref, c_ref, pair_ref, y_ref, z_ref, dxl_ref, xs_ref, gs_ref, dbl_ref, dcl_ref = targets
    base = sc_ref[0]
    loads = []
    for i in range(HALF):
        row = []
        for k, (src, dst) in enumerate(zip(sources, targets)):
            if k in (0, 1, 4):
                src = src.at[:, columns(base, i, W if k == 4 else N)]
            else:
                src = src.at[i]
            row.append(pltpu.make_async_copy(src, dst.at[i], sem_in.at[i, k]))
            row[-1].start()
        loads.append(row)
    fill_spread(e_ref)
    stores = []
    for i in range(HALF):
        for load in loads[i]:
            load.wait()
        b, c = b_ref[i], c_ref[i]
        rows = slice(i * N, (i + 1) * N)
        for k in range(W // CHUNK):
            cut = slice(k * CHUNK, (k + 1) * CHUNK)
            far = slice(W + k * CHUNK, W + (k + 1) * CHUNK)
            scale = jnp.dot(pair_ref[i], e_ref[:, cut], preferred_element_type=F32)
            mixed = y_ref[i, :, cut].astype(F32) + scale[0:T] * jnp.dot(
                c, el_ref[rows, cut], preferred_element_type=F32
            )
            mixed = mixed.astype(BF16).astype(F32)
            out_ref[i, :, cut] = (mixed * silu(z_ref[i, :, cut].astype(F32))).astype(BF16)
            dx_ref[i, :, cut] = dxl_ref[i, :, cut].astype(F32) + scale[T : 2 * T] * jnp.dot(
                b, el_ref[rows, far], preferred_element_type=F32
            )
        db_ref[i] = dbl_ref[i] + lax.dot_general(
            xs_ref[i], el_ref[rows, W:], NT, preferred_element_type=F32
        )
        dc_ref[i] = dcl_ref[i] + lax.dot_general(
            gs_ref[i], el_ref[rows, :W], NT, preferred_element_type=F32
        )
        for k, (src, dst, width) in enumerate(
            ((out_ref, out_hbm, W), (dx_ref, dx_hbm, W), (db_ref, db_hbm, N), (dc_ref, dc_hbm, N))
        ):
            stores.append(
                pltpu.make_async_copy(src.at[i], dst.at[:, columns(base, i, width)], sem_out.at[i, k])
            )
            stores[-1].start()
    for store in stores:
        store.wait()


def final(name, sc, el, local_parts, z, b, c, earlier):
    y, dx, xs, gs, pairs, db, dc = local_parts
    operands = [in_hbm(a) for a in (b, c, pairs, y, z, dx, xs, gs, db, dc)]
    wide = pltpu.VMEM((HALF, T, W), BF16)
    thin = pltpu.VMEM((HALF, T, N), F32)
    short = pltpu.VMEM((HALF, T, N), BF16)
    return pl.pallas_call(
        functools.partial(final_kernel, bool(earlier)),
        in_specs=[SMEM_SPEC, VMEM_SPEC] + [HBM_SPEC] * (10 + len(earlier)),
        out_specs=[HBM_SPEC] * 4,
        out_shape=[
            pltpu.HBM((T, NH * P_SIZE), BF16),
            pltpu.HBM((T, NH * P_SIZE), F32),
            pltpu.HBM((T, NG * N), F32),
            pltpu.HBM((T, NG * N), F32),
        ],
        input_output_aliases={12 + k: k for k in range(len(earlier))},
        scratch_shapes=[
            SPREAD, short, short, pltpu.VMEM((HALF, 2 * T, LANES), BF16),
            wide, wide, wide, wide, wide, thin, thin,
            wide, pltpu.VMEM((HALF, T, W), F32), thin, thin,
            pltpu.SemaphoreType.DMA((HALF, 10)),
            pltpu.SemaphoreType.DMA((HALF, 4)),
        ],
        compiler_params=params(24),
        name=name,
    )(sc, el, *operands, *earlier)


def body(ssm_input, gate_input, b_input, c_input, dt_raw, dt_bias, a_log, skip_gain, out_grad):
    ctx_count = lax.axis_size("ctx")
    head_count = lax.axis_size("head")
    core = (lax.axis_index("head") % 2).astype(jnp.int32)
    sc_other = jnp.stack([HALF * (1 - core), core])
    sc_own = jnp.stack([HALF * core, core])
    bias, alog, skip = dt_bias[None, :], a_log[None, :], skip_gain[None, :]
    swap = [(k, k ^ 1) for k in range(head_count)]
    chips = [[2 * k + c for k in range(ctx_count * head_count // 2)] for c in range(2)]

    def exchange(parts):
        return lax.all_to_all(
            parts, ("ctx", "head"), split_axis=0, concat_axis=0, tiled=True, axis_index_groups=chips
        )

    tokens = (ssm_input, gate_input, out_grad, b_input, c_input)
    send, aux = states(True, sc_other, dt_raw, bias, alog, *tokens)
    got = lax.ppermute(send, "head", swap)
    keep = states(False, sc_own, aux, *tokens)[0]
    gathered = exchange(merge(sc_own, keep, got))
    got_other = lax.ppermute(keep, "head", swap)
    loc_own = local("local_own", sc_own, aux, skip, got, *tokens)
    back = exchange(scan(gathered, loc_own[6]))
    loc_other = local("local_other", sc_other, aux, skip, got_other, *tokens)
    back, loc_other = lax.optimization_barrier((back, loc_other))
    el = back.reshape(HALF * N, 2 * W)
    el_other = lax.ppermute(el, "head", swap)
    shared = (gate_input, b_input, c_input)
    outs = final("final_own", sc_own, el, loc_own, *shared, ())
    return tuple(final("final_other", sc_other, el_other, loc_other, *shared, tuple(outs)))


def solution(mesh):
    row_spec = P(("ctx", "head"), None)
    in_specs = (row_spec,) * 5 + (P(), P(), P(), row_spec)
    return jax.shard_map(
        body, mesh=mesh, in_specs=in_specs, out_specs=(row_spec,) * 4, check_vma=False
    )
```

time: 138 us -> 112 us (0.81)
  local copies, waits for them, and re-layouts: 19.8 us -> 1.36 us
  waiting for transfers between devices: 37.1 us -> 30 us
    unnamed x58 -> x2, local copies, waits for them, and re-layouts: 19.8 us -> 1.36 us
    all_to_all x2, waiting for transfers between devices: 37.1 us -> 30 us  [exchange(): lax.all_to_all(parts, ('ctx', 'head'), split_axis=0, concat_axis=0, tiled...]
    ppermute x1 -> x2, starting transfers between devices: 3.18 us -> 3.52 us  [the longest x1 3.13 us: body(): el_other = lax.ppermute(el, 'head', swap)]
    pallas_call x9 -> x8, Pallas kernels: 56.4 us -> 56.7 us  [the longest x2 27.2 us: local(): pl.pallas_call(local_kernel, in_specs=[SMEM_SPEC, VMEM_SPEC, VMEM_SPEC, V...]
  transfers between devices with their start and end apart: 4 -> 5, of which waited for: 2 -> 2; matrix products, arithmetic and copies ran while one was open for 0% -> 0% of each run, Pallas kernels for 22% -> 37%
where the time goes in v1:
time: 112 us
  Pallas kernels  56.7 us (51%)
  waiting for transfers between devices  30 us (27%)
  starting transfers between devices  22.8 us (20%)
  local copies, waits for them, and re-layouts  1.36 us (1%)
    all_to_all x2, waiting for transfers between devices, exchange(): lax.all_to_all(parts, ('ctx', 'head'), split_axis=0, concat_axis=0, tiled...  30 us
    pallas_call x2, Pallas kernels, local(): pl.pallas_call(local_kernel, in_specs=[SMEM_SPEC, VMEM_SPEC, VMEM_SPEC, V...  27.2 us
    all_to_all x2, starting transfers between devices, exchange(): lax.all_to_all(parts, ('ctx', 'head'), split_axis=0, concat_axis=0, tiled...  17.8 us
    pallas_call x2, Pallas kernels, states(): pl.pallas_call(functools.partial(states_kernel, first), in_specs=[SMEM_SP...  12.2 us
    pallas_call x2, Pallas kernels, final(): pl.pallas_call(functools.partial(final_kernel, bool(earlier)), in_specs=[...  11.3 us
    pallas_call x1, Pallas kernels, merge(): pl.pallas_call(merge_kernel, in_specs=[SMEM_SPEC, HBM_SPEC, HBM_SPEC], ou...  3.97 us
    ppermute x1, starting transfers between devices, body(): el_other = lax.ppermute(el, 'head', swap)  3.13 us
  transfers between devices with their start and end apart: 5, of which 2 were waited for; matrix products, arithmetic and copies ran while one was open for 0% of the time, Pallas kernels for 37%

profile of v1, /device:TPU:1, one launch (start us, length us, event | category | flops | bytes accessed | tf_op | source)
XLA Modules:
  0.0 111.9 jit_solution(963288695326322207)
XLA Ops:
  0.6 0.1 pad_add_fusion.sc_ref
  0.7 6.1 %states_send.1 = (bf16[512,2176]{1,0:T(8,128)(2,1)}, f32[4,128,128]{2,1,0:T(8,128)}) custom-call(s32[2]{0:T(128)S(1)} %pad_add_fusion.sc_ref, bf16[128,128]{1,0:T(8,128)(2,1)} %refs_0_.3, f32[1,128]{1,0:T(1,128)} %bitcast.11, f32[1,128]{1,0:T(1,128)} %bitcast.12, bf16[128,8192]{1,0:T(8,128)(2,1)} %x_hbm.3, bf16[128,8192]{1,0:T(8,128)(2,1)} %refs_4_.7, ...), custom_call_target="tpu_custom_call" | custom-call | tf_op jit(solution)/shard_map/states_send/pallas_call | solution.py:178
  6.8 1.5 %collective-permute-start = (bf16[512,2176]{1,0:T(8,128)(2,1)}, bf16[512,2176]{1,0:T(8,128)(2,1)S(1)}, u32[]{:S(2)}, u32[]{:S(2)}) collective-permute-start(bf16[512,2176]{1,0:T(8,128)(2,1)} %get-tuple-element.33), channel_id=1, source_target_pairs={{0,1},{1,0},{2,3},{3,2},{4,5},{5,4},{6,7},{7,6},{8,9},{9,8},{10,11... | collective-permute-start | bytes 6684680 | tf_op jit(solution)/shard_map/ppermute | solution.py:547
  8.3 0.1 pad_add_fusion.1.sc_ref
  8.4 6.1 %states_keep.1.own_hbm = bf16[512,2176]{1,0:T(8,128)(2,1)} custom-call(s32[2]{0:T(128)S(1)} %pad_add_fusion.1.sc_ref, f32[4,128,128]{2,1,0:T(8,128)} %get-tuple-element.32.refs_0_.aux_ref, bf16[128,8192]{1,0:T(8,128)(2,1)} %x_hbm.3, bf16[128,8192]{1,0:T(8,128)(2,1)} %refs_4_.7, bf16[128,8192]{1,0:T(8,128)(2,1)} %og_hbm.3, bf16[128,1024]{1,0:T(8,128)(2,1)} %refs_0_.5, ...), custom_call_target="tpu_custom_call" | custom-call | tf_op jit(solution)/shard_map/states_keep/pallas_call | solution.py:178
  14.5 0.0 collective-permute-done.got_hbm.got_ref
  14.5 0.0 copy-start
  14.6 1.4 %copy-done = bf16[512,2176]{1,0:T(8,128)(2,1)} copy-done((bf16[512,2176]{1,0:T(8,128)(2,1)}, bf16[512,2176]{1,0:T(8,128)(2,1)S(1)}, u32[]{:S(2)}) %copy-start) | copy-done | bytes 2228248
  15.9 4.0 %merge_cores.1 = bf16[64,8,2176]{2,1,0:T(8,128)(2,1)} custom-call(s32[2]{0:T(128)S(1)} %pad_add_fusion.1.sc_ref, bf16[512,2176]{1,0:T(8,128)(2,1)} %states_keep.1.own_hbm, bf16[512,2176]{1,0:T(8,128)(2,1)} %copy-done), custom_call_target="tpu_custom_call" | custom-call | tf_op jit(solution)/shard_map/merge_cores/pallas_call | solution.py:245
  19.9 11.2 %all-to-all-start = ((bf16[64,8,2176]{2,1,0:T(8,128)(2,1)}), bf16[64,8,2176]{2,1,0:T(8,128)(2,1)S(1)}, u32[]{:S(2)}, u32[]{:S(2)}) async-start(bf16[64,8,2176]{2,1,0:T(8,128)(2,1)} %merge_cores.1), calls=%async_computation | async-start | bytes 4456448 | tf_op jit(solution)/shard_map/all_to_all | solution.py:541
  31.1 0.4 collective-permute-start.1
  31.5 13.6 %local_own.1 = (bf16[4,128,1024]{2,1,0:T(8,128)(2,1)}, bf16[4,128,1024]{2,1,0:T(8,128)(2,1)}, bf16[4,128,1024]{2,1,0:T(8,128)(2,1)}, bf16[4,128,1024]{2,1,0:T(8,...) custom-call(s32[2]{0:T(128)S(1)} %pad_add_fusion.1.sc_ref, ...), custom_call_target="tpu_custom_call" | custom-call | tf_op jit(solution)/shard_map/local_own/pallas_call | solution.py:427
  45.1 16.1 %all-to-all-done.in_ref = bf16[64,8,2176]{2,1,0:T(8,128)(2,1)S(1)} async-done(((bf16[64,8,2176]{2,1,0:T(8,128)(2,1)}), bf16[64,8,2176]{2,1,0:T(8,128)(2,1)S(1)}, u32[]{:S(2)}, u32[]{:S(2)}) %all-to-all-start) | async-done | bytes 2228256 | tf_op jit(solution)/shard_map/all_to_all | solution.py:541
  61.2 2.1 %scan_chips.1 = bf16[64,8,2048]{2,1,0:T(8,128)(2,1)} custom-call(bf16[64,8,2176]{2,1,0:T(8,128)(2,1)S(1)} %all-to-all-done.in_ref, f32[4,128,128]{2,1,0:T(8,128)} %get-tuple-element.34.after_ref.refs_9_), custom_call_target="tpu_custom_call" | custom-call | tf_op jit(solution)/shard_map/scan_chips/pallas_call | solution.py:295
  63.3 6.5 %all-to-all-start.1 = ((bf16[64,8,2048]{2,1,0:T(8,128)(2,1)}), bf16[64,8,2048]{2,1,0:T(8,128)(2,1)S(1)}, u32[]{:S(2)}, u32[]{:S(2)}) async-start(bf16[64,8,2048]{2,1,0:T(8,128)(2,1)} %scan_chips.1), calls=%async_computation.1 | async-start | bytes 4194304 | tf_op jit(solution)/shard_map/all_to_all | solution.py:541
  69.8 0.0 collective-permute-done.1.got_ref
  69.9 13.6 %local_other.1 = (bf16[4,128,1024]{2,1,0:T(8,128)(2,1)}, bf16[4,128,1024]{2,1,0:T(8,128)(2,1)}, bf16[4,128,1024]{2,1,0:T(8,128)(2,1)}, bf16[4,128,1024]{2,1,0:T(...) custom-call(s32[2]{0:T(128)S(1)} %pad_add_fusion.sc_ref, ...), custom_call_target="tpu_custom_call" | custom-call | tf_op jit(solution)/shard_map/local_other/pallas_call | solution.py:427
  83.4 13.9 %all-to-all-done.1 = bf16[64,8,2048]{2,1,0:T(8,128)(2,1)S(1)} async-done(((bf16[64,8,2048]{2,1,0:T(8,128)(2,1)}), bf16[64,8,2048]{2,1,0:T(8,128)(2,1)S(1)}, u32[]{:S(2)}, u32[]{:S(2)}) %all-to-all-start.1) | async-done | bytes 2097184 | tf_op jit(solution)/shard_map/all_to_all | solution.py:541
  97.3 3.1 %collective-permute-start.2 = (bf16[512,2048]{1,0:T(8,128)(2,1)S(1)}, bf16[512,2048]{1,0:T(8,128)(2,1)S(1)}, u32[]{:S(2)}, u32[]{:S(2)}) collective-permute-start(bf16[512,2048]{1,0:T(8,128)(2,1)S(1)} %bitcast.7), channel_id=1, source_target_pairs={{0,1},{1,0},{2,3},{3,2},{4,5},{5,4},{6,7},{7,6},{8,9},{9,8},{10,11... | collective-permute-start | bytes 6291464 | tf_op jit(solution)/shard_map/ppermute | solution.py:556
  100.5 5.7 %final_own.1 = (bf16[128,8192]{1,0:T(8,128)(2,1)}, f32[128,8192]{1,0:T(8,128)}, f32[128,1024]{1,0:T(8,128)}, f32[128,1024]{1,0:T(8,128)}) custom-call(s32[2]{0:T(128)S(1)} %pad_add_fusion.1.sc_ref, bf16[512,2048]{1,0:T(8,128)(2,1)S(1)} %bitcast.8, bf16[128,1024]{1,0:T(8,128)(2,1)} %refs_0_.5, bf16[128,1024]{1,0:T(8,128)(2,1)} %refs_1_.5, ...), custom_call_target="tpu_custom_call" | custom-call | tf_op jit(solution)/shard_map/final_own/pallas_call | solution.py:507
  106.2 0.0 collective-permute-done.2.el_ref
  106.2 5.6 %final_other.1 = (bf16[128,8192]{1,0:T(8,128)(2,1)}, f32[128,8192]{1,0:T(8,128)}, f32[128,1024]{1,0:T(8,128)}, f32[128,1024]{1,0:T(8,128)}) custom-call(s32[2]{0:T(128)S(1)} %pad_add_fusion.sc_ref, bf16[512,2048]{1,0:T(8,128)(2,1)S(1)} %collective-permute-done.2.el_ref, ...), custom_call_target="tpu_custom_call", output_to_operand_aliasing={{0}: (12, {}), {1}: (13, {}), {2}: (14, {}), {3}: (15, {})} | custom-call | tf_op jit(solution)/shard_map/final_other/pallas_call | solution.py:507
Async XLA Ops:
  6.8 7.7 %collective-permute-start = (bf16[512,2176]{1,0:T(8,128)(2,1)}, bf16[512,2176]{1,0:T(8,128)(2,1)S(1)}, u32[]{:S(2)}, u32[]{:S(2)}) collective-permute-start(bf16[512,2176]{1,0:T(8,128)(2,1)} %get-tuple-element.33), channel_id=1, source_target_pairs={{0,1},{1,0},{2,3},{3,2},{4,5},{5,4},{6,7},{7,6},{8,9},{9,8},{10,11... | collective-permute-start | bytes 6684680 | tf_op jit(solution)/shard_map/ppermute | solution.py:547
  14.5 1.4 %copy-start = (bf16[512,2176]{1,0:T(8,128)(2,1)}, bf16[512,2176]{1,0:T(8,128)(2,1)S(1)}, u32[]{:S(2)}) copy-start(bf16[512,2176]{1,0:T(8,128)(2,1)S(1)} %collective-permute-done.got_hbm.got_ref) | copy-start | bytes 6684676
  19.9 41.3 %all-to-all-start = ((bf16[64,8,2176]{2,1,0:T(8,128)(2,1)}), bf16[64,8,2176]{2,1,0:T(8,128)(2,1)S(1)}, u32[]{:S(2)}, u32[]{:S(2)}) async-start(bf16[64,8,2176]{2,1,0:T(8,128)(2,1)} %merge_cores.1), calls=%async_computation | async-start | bytes 4456448 | tf_op jit(solution)/shard_map/all_to_all | solution.py:541
  31.1 38.7 %collective-permute-start.1 = (bf16[512,2176]{1,0:T(8,128)(2,1)}, bf16[512,2176]{1,0:T(8,128)(2,1)}, u32[]{:S(2)}, u32[]{:S(2)}) collective-permute-start(bf16[512,2176]{1,0:T(8,128)(2,1)} %states_keep.1.own_hbm), channel_id=1, source_target_pairs={{0,1},{1,0},{2,3},{3,2},{4,5},{5,4},{6,7},{7,6},{8,9},{9,8},{10,11... | collective-permute-start | bytes 6684680 | tf_op jit(solution)/shard_map/ppermute | solution.py:550
  63.3 34.0 %all-to-all-start.1 = ((bf16[64,8,2048]{2,1,0:T(8,128)(2,1)}), bf16[64,8,2048]{2,1,0:T(8,128)(2,1)S(1)}, u32[]{:S(2)}, u32[]{:S(2)}) async-start(bf16[64,8,2048]{2,1,0:T(8,128)(2,1)} %scan_chips.1), calls=%async_computation.1 | async-start | bytes 4194304 | tf_op jit(solution)/shard_map/all_to_all | solution.py:541
  97.3 8.9 %collective-permute-start.2 = (bf16[512,2048]{1,0:T(8,128)(2,1)S(1)}, bf16[512,2048]{1,0:T(8,128)(2,1)S(1)}, u32[]{:S(2)}, u32[]{:S(2)}) collective-permute-start(bf16[512,2048]{1,0:T(8,128)(2,1)S(1)} %bitcast.7), channel_id=1, source_target_pairs={{0,1},{1,0},{2,3},{3,2},{4,5},{5,4},{6,7},{7,6},{8,9},{9,8},{10,11... | collective-permute-start | bytes 6291464 | tf_op jit(solution)/shard_map/ppermute | solution.py:556

commit v2 on v1

--- a/solution.py
+++ b/solution.py
@@ -86,56 +86,58 @@
     return step, running, from_start, to_end
 
 
+def base_of(own, sc_ref):
+    return HALF * sc_ref[0] if own else HALF * (1 - sc_ref[0])
+
+
 def columns(base, i, width):
     return pl.ds(pl.multiple_of((base + i) * width, width), width)
 
 
-def states_kernel(first, sc_ref, *refs):
-    if first:
-        dt_hbm, bias_hbm, alog_hbm, x_hbm, z_hbm, og_hbm, b_hbm, c_hbm, st_hbm, aux_hbm = refs[:10]
-        small = ((dt_hbm, refs[-3]), (bias_hbm, refs[-2]), (alog_hbm, refs[-1]))
+def states_kernel(own, sc_ref, *refs):
+    if own:
+        aux_ref, b_ref, x_ref, c_ref, z_ref, og_ref, st_ref, part_hbm, e_ref, sem_out = refs
     else:
-        aux_hbm, x_hbm, z_hbm, og_hbm, b_hbm, c_hbm, st_hbm = refs[:7]
-    e_ref, x_ref, z_ref, og_ref, b_ref, c_ref, st_ref, aux_ref, sem, sem_out, sem_small = refs[
-        (10 if first else 7) : (21 if first else 18)
-    ]
-    base = sc_ref[0]
-    if not first:
-        small = ((aux_hbm, aux_ref),)
-    smalls = [pltpu.make_async_copy(s, d, sem_small.at[k]) for k, (s, d) in enumerate(small)]
-    for copy in smalls:
-        copy.start()
+        dt_hbm, bias_hbm, alog_hbm = refs[:3]
+        tokens = refs[3:8]
+        st_ref, aux_ref, aux_hbm = refs[8:11]
+        kept = refs[11:16]
+        e_ref = refs[16]
+        b_ref, x_ref, c_ref, z_ref, og_ref = used = refs[17:22]
+        small = refs[22:25]
+        sem, sem_small = refs[25:]
+    base = base_of(own, sc_ref)
     copies = []
-    for i in range(HALF):
-        row = []
-        for k, (src, dst, width) in enumerate(
-            (
-                (b_hbm, b_ref, N),
-                (x_hbm, x_ref, W),
-                (c_hbm, c_ref, N),
-                (z_hbm, z_ref, W),
-                (og_hbm, og_ref, W),
-            )
-        ):
-            row.append(
-                pltpu.make_async_copy(src.at[:, columns(base, i, width)], dst.at[i], sem.at[i, k])
-            )
-            row[-1].start()
-        copies.append(row)
+    stores = []
+    if not own:
+        smalls = [
+            pltpu.make_async_copy(s, d, sem_small.at[k])
+            for k, (s, d) in enumerate(zip((dt_hbm, bias_hbm, alog_hbm), small))
+        ]
+        for copy in smalls:
+            copy.start()
+        for half, (first, targets) in enumerate(((base, used), (base_of(True, sc_ref), kept))):
+            for i in range(HALF):
+                row = []
+                for k, (src, dst) in enumerate(zip(tokens, targets)):
+                    cut = columns(first, i, dst.shape[-1])
+                    row.append(pltpu.make_async_copy(src.at[:, cut], dst.at[i], sem.at[half, i, k]))
+                    row[-1].start()
+                copies.append(row)
     fill_spread(e_ref)
-    for copy in smalls:
-        copy.wait()
-    stores = []
-    if first:
-        for k, v in enumerate(steps_of(refs[-3], refs[-2], refs[-1])):
+    if not own:
+        for copy in smalls:
+            copy.wait()
+        for k, v in enumerate(steps_of(*small)):
             aux_ref[k] = v
         stores.append(pltpu.make_async_copy(aux_ref, aux_hbm, sem_small.at[3]))
         stores[0].start()
     from_start = pair_up(to_half(aux_ref[2], base))
     to_end = pair_up(to_half(aux_ref[3], base))
     for i in range(HALF):
-        for copy in copies[i]:
-            copy.wait()
+        if not own:
+            for copy in copies[i]:
+                copy.wait()
         here = slice(i * N, (i + 1) * N)
         te = of_group(to_end, i)
         fs = of_group(from_start, i)
@@ -156,34 +158,58 @@
             ).astype(BF16)
         decay = jnp.broadcast_to(fs[T - 16 : T].astype(F32)[15:16], (N, LANES))
         st_ref[here, 2 * W :] = decay.astype(BF16)
-        stores.append(pltpu.make_async_copy(st_ref.at[here], st_hbm.at[here], sem_out.at[i]))
-        stores[-1].start()
+        if own:
+            stores += part_copies(st_ref, part_hbm, here, sc_ref[0], sem_out.at[i])
+            for store in stores[-2:]:
+                store.start()
+    if not own:
+        for row in copies[HALF:]:
+            for copy in row:
+                copy.wait()
     for store in stores:
         store.wait()
 
 
-def states(first, sc, *args):
-    out_shape = [pltpu.HBM((HALF * N, WIDE), BF16)]
-    scratch = (
-        [SPREAD]
-        + [pltpu.VMEM((HALF, T, W), BF16)] * 3
-        + [pltpu.VMEM((HALF, T, N), BF16)] * 2
-        + [pltpu.VMEM((HALF * N, WIDE), BF16), pltpu.VMEM((4, T, NH), F32)]
-        + [pltpu.SemaphoreType.DMA((HALF, 5)), pltpu.SemaphoreType.DMA((HALF,))]
-        + [pltpu.SemaphoreType.DMA((4,))]
-    )
-    if first:
-        out_shape.append(pltpu.HBM((4, T, NH), F32))
-        scratch += [pltpu.VMEM((T, NH), BF16), pltpu.VMEM((1, NH), F32), pltpu.VMEM((1, NH), F32)]
+def part_copies(st_ref, part_hbm, here, which, sem):
+    cut = pl.ds(pl.multiple_of(which * W, W), W)
+    return [
+        pltpu.make_async_copy(st_ref.at[here, cut], part_hbm.at[here, :W], sem.at[0]),
+        pltpu.make_async_copy(st_ref.at[here, 2 * W :], part_hbm.at[here, W:], sem.at[1]),
+    ]
+
+
+STATE = jax.ShapeDtypeStruct((HALF * N, WIDE), BF16)
+PART = pltpu.HBM((HALF * N, W + LANES), BF16)
+
+
+def states_send(sc, dt, bias, alog, *tokens):
+    shapes = [(HALF, T, N), (HALF, T, W), (HALF, T, N), (HALF, T, W), (HALF, T, W)]
+    aux = jax.ShapeDtypeStruct((4, T, NH), F32)
     return pl.pallas_call(
-        functools.partial(states_kernel, first),
-        in_specs=[SMEM_SPEC] + [HBM_SPEC] * len(args),
-        out_specs=[HBM_SPEC] * len(out_shape),
-        out_shape=out_shape,
-        scratch_shapes=scratch,
+        functools.partial(states_kernel, False),
+        in_specs=[SMEM_SPEC] + [HBM_SPEC] * 8,
+        out_specs=[VMEM_SPEC, VMEM_SPEC, HBM_SPEC] + [VMEM_SPEC] * 5,
+        out_shape=[STATE, aux, pltpu.HBM((4, T, NH), F32)]
+        + [jax.ShapeDtypeStruct(s, BF16) for s in shapes],
+        scratch_shapes=[SPREAD]
+        + [pltpu.VMEM(s, BF16) for s in shapes]
+        + [pltpu.VMEM((T, NH), BF16), pltpu.VMEM((1, NH), F32), pltpu.VMEM((1, NH), F32)]
+        + [pltpu.SemaphoreType.DMA((2, HALF, 5)), pltpu.SemaphoreType.DMA((4,))],
         compiler_params=params(24),
-        name="states_send" if first else "states_keep",
-    )(sc, *[in_hbm(a) for a in args])
+        name="states_send",
+    )(sc, *[in_hbm(a) for a in (dt, bias, alog, *tokens)])
+
+
+def states_keep(sc, aux, *tokens):
+    return pl.pallas_call(
+        functools.partial(states_kernel, True),
+        in_specs=[SMEM_SPEC] + [VMEM_SPEC] * 6,
+        out_specs=[VMEM_SPEC, HBM_SPEC],
+        out_shape=[STATE, PART],
+        scratch_shapes=[SPREAD, pltpu.SemaphoreType.DMA((HALF, 2))],
+        compiler_params=params(12),
+        name="states_keep",
+    )(sc, aux, *tokens)
 
 
 def decay_row(state_ref, at, e_ref):
@@ -191,24 +217,13 @@
     return jnp.dot(pairs, e_ref[...], preferred_element_type=F32)[0:1]
 
 
-def merge_kernel(sc_ref, own_hbm, got_hbm, out_hbm, e_ref, own_ref, got_ref, out_ref, sem, sem_out):
-    loads = []
-    for i in range(HALF):
-        here = slice(i * N, (i + 1) * N)
-        pair = (
-            pltpu.make_async_copy(own_hbm.at[here], own_ref.at[here], sem.at[i, 0]),
-            pltpu.make_async_copy(got_hbm.at[here], got_ref.at[here], sem.at[i, 1]),
-        )
-        for copy in pair:
-            copy.start()
-        loads.append(pair)
+def merge_kernel(sc_ref, own_ref, got_ref, out_hbm, part_hbm, e_ref, out_ref, sem, sem_out):
     fill_spread(e_ref)
+    core = sc_ref[0]
 
     def merge(r0, r1):
         stores = []
         for i in range(HALF):
-            for copy in loads[i]:
-                copy.wait()
             here = slice(i * N, (i + 1) * N)
             there = slice(i * N // 8, (i + 1) * N // 8)
             d0 = decay_row(r0, i * N, e_ref)
@@ -229,14 +244,17 @@
             out_ref[there, :, 2 * W :] = both.astype(BF16)
             stores.append(pltpu.make_async_copy(out_ref.at[there], out_hbm.at[there], sem_out.at[i]))
             stores[-1].start()
+        stores += part_copies(got_ref, part_hbm, slice(0, HALF * N), 1 - core, sem)
+        for store in stores[-2:]:
+            store.start()
         for store in stores:
             store.wait()
 
-    @pl.when(sc_ref[1] == 0)
+    @pl.when(core == 0)
     def _():
         merge(own_ref, got_ref)
 
-    @pl.when(sc_ref[1] != 0)
+    @pl.when(core != 0)
     def _():
         merge(got_ref, own_ref)
 
@@ -244,20 +262,18 @@
 def merge(sc, own, got):
     return pl.pallas_call(
         merge_kernel,
-        in_specs=[SMEM_SPEC, HBM_SPEC, HBM_SPEC],
-        out_specs=HBM_SPEC,
-        out_shape=pltpu.HBM((HALF * N // 8, 8, WIDE), BF16),
+        in_specs=[SMEM_SPEC, VMEM_SPEC, VMEM_SPEC],
+        out_specs=[HBM_SPEC, HBM_SPEC],
+        out_shape=[pltpu.HBM((HALF * N // 8, 8, WIDE), BF16), PART],
         scratch_shapes=[
             SPREAD,
-            pltpu.VMEM((HALF * N, WIDE), BF16),
-            pltpu.VMEM((HALF * N, WIDE), BF16),
             pltpu.VMEM((HALF * N // 8, 8, WIDE), BF16),
-            pltpu.SemaphoreType.DMA((HALF, 2)),
+            pltpu.SemaphoreType.DMA((2,)),
             pltpu.SemaphoreType.DMA((HALF,)),
         ],
         compiler_params=params(16),
         name="merge_cores",
-    )(sc, in_hbm(own), in_hbm(got))
+    )(sc, own, got)
 
 
 def scan_kernel(chips, in_ref, after_ref, out_hbm, e_ref, d_ref, out_ref, sem):
@@ -309,22 +325,22 @@
 
 
 def local_kernel(
-    sc_ref, aux_ref, skip_ref, got_ref, x_hbm, z_hbm, og_hbm, b_hbm, c_hbm,
+    own, sc_ref, aux_ref, skip_ref, got_ref, b_hbm, x_hbm, c_hbm, z_hbm, og_hbm,
     y_ref, dx_ref, xs_ref, gs_ref, pair_ref, db_ref, dc_ref,
     e_ref, x_ref, z_ref, og_ref, b_ref, c_ref, ysum_ref, dxsum_ref, hg_ref,
     runc_ref, run_ref, step_ref, plain_ref, sem,
 ):
-    base = sc_ref[0]
-    core = sc_ref[1]
+    base = base_of(own, sc_ref)
+    core = sc_ref[0]
     copies = []
     for i in range(HALF):
         for k, (src, dst, width) in enumerate(
             (
+                (b_hbm, b_ref, N),
                 (x_hbm, x_ref, W),
+                (c_hbm, c_ref, N),
                 (z_hbm, z_ref, W),
                 (og_hbm, og_ref, W),
-                (b_hbm, b_ref, N),
-                (c_hbm, c_ref, N),
             )
         ):
             copies.append(
@@ -339,7 +355,7 @@
     run_t = run.T
     step_t = to_half(aux_ref[0], base).T
     for i in range(HALF):
-        decay = got_ref[i * N : i * N + 16, 2 * W :].astype(F32)
+        decay = got_ref[i * N : i * N + 16, W:].astype(F32)
         decay = (decay + pltpu.roll(decay, 64, 1))[0:1]
         fs, te, skip, run_c = [pltpu.roll(v, LANES - PER * i, 1) if i else v for v in (start, end, gain, run)]
         plain_ref[i, 0:T] = pair_up(fs).astype(BF16)
@@ -407,7 +423,7 @@
 
         @pl.when(core == 0)
         def _():
-            partner = got_ref[rows, W : 2 * W]
+            partner = got_ref[rows, :W]
             te = jnp.dot(plain_ref[i, T : 2 * T], e_ref[...], preferred_element_type=F32)
             dxsum_ref[...] += te * jnp.dot(b, partner, preferred_element_type=F32)
             xs = (x_ref[i].astype(F32) * te).astype(BF16)
@@ -420,12 +436,12 @@
     lax.fori_loop(0, HALF, one_group, 0)
 
 
-def local(name, sc, aux, skip, got, *tokens):
+def local(own, sc, aux, skip, got, *tokens):
     wide = pltpu.HBM((HALF, T, W), BF16)
     thin = pltpu.HBM((HALF, T, N), F32)
     args = [in_hbm(a) for a in (aux, skip, got, *tokens)]
     return pl.pallas_call(
-        local_kernel,
+        functools.partial(local_kernel, own),
         in_specs=[SMEM_SPEC, VMEM_SPEC, VMEM_SPEC, VMEM_SPEC] + [HBM_SPEC] * 5,
         out_specs=[VMEM_SPEC] * 7,
         out_shape=[wide] * 4 + [pltpu.HBM((HALF, 2 * T, LANES), BF16)] + [thin] * 2,
@@ -439,34 +455,44 @@
         + [pltpu.VMEM((HALF, 2 * T + 16, LANES), BF16)]
         + [pltpu.SemaphoreType.DMA((HALF, 5))],
         compiler_params=params(24),
-        name=name,
+        name="local_own" if own else "local_other",
     )(sc, *args)
 
 
-def final_kernel(aliased, sc_ref, el_ref, *refs):
-    sources = refs[:10]
-    refs = refs[10 + (4 if aliased else 0) :]
-    out_hbm, dx_hbm, db_hbm, dc_hbm = refs[:4]
-    e_ref, *targets = refs[4:15]
-    out_ref, dx_ref, db_ref, dc_ref, sem_in, sem_out = refs[15:]
+def final_kernel(own, sc_ref, el_ref, *refs):
+    if own:
+        sources, others, refs = refs[:10], refs[10:20], refs[20:]
+        out_hbm, dx_hbm, db_hbm, dc_hbm = refs[:4]
+        kept, refs = refs[4:14], refs[14:]
+        e_ref, targets, refs = refs[0], refs[1:11], refs[11:]
+        out_ref, dx_ref, db_ref, dc_ref, sem_out, sem_in = refs
+    else:
+        targets, refs = refs[:10], refs[14:]
+        out_hbm, dx_hbm, db_hbm, dc_hbm = refs[:4]
+        e_ref, out_ref, dx_ref, db_ref, dc_ref, sem_out = refs[4:]
     b_ref, c_ref, pair_ref, y_ref, z_ref, dxl_ref, xs_ref, gs_ref, dbl_ref, dcl_ref = targets
-    base = sc_ref[0]
+    base = base_of(own, sc_ref)
     loads = []
-    for i in range(HALF):
-        row = []
-        for k, (src, dst) in enumerate(zip(sources, targets)):
-            if k in (0, 1, 4):
-                src = src.at[:, columns(base, i, W if k == 4 else N)]
-            else:
-                src = src.at[i]
-            row.append(pltpu.make_async_copy(src, dst.at[i], sem_in.at[i, k]))
-            row[-1].start()
-        loads.append(row)
+    if own:
+        for half, (first, srcs, dsts) in enumerate(
+            ((base, sources, targets), (base_of(False, sc_ref), others, kept))
+        ):
+            for i in range(HALF):
+                row = []
+                for k, (src, dst) in enumerate(zip(srcs, dsts)):
+                    if k in (0, 1, 4):
+                        src = src.at[:, columns(first, i, W if k == 4 else N)]
+                    else:
+                        src = src.at[i]
+                    row.append(pltpu.make_async_copy(src, dst.at[i], sem_in.at[half, i, k]))
+                    row[-1].start()
+                loads.append(row)
     fill_spread(e_ref)
     stores = []
     for i in range(HALF):
-        for load in loads[i]:
-            load.wait()
+        if own:
+            for load in loads[i]:
+                load.wait()
         b, c = b_ref[i], c_ref[i]
         rows = slice(i * N, (i + 1) * N)
         for k in range(W // CHUNK):
@@ -494,45 +520,77 @@
                 pltpu.make_async_copy(src.at[i], dst.at[:, columns(base, i, width)], sem_out.at[i, k])
             )
             stores[-1].start()
+    for row in loads[HALF:]:
+        for load in row:
+            load.wait()
     for store in stores:
         store.wait()
 
 
-def final(name, sc, el, local_parts, z, b, c, earlier):
+LOADED = [
+    ((HALF, T, N), BF16),
+    ((HALF, T, N), BF16),
+    ((HALF, 2 * T, LANES), BF16),
+    ((HALF, T, W), BF16),
+    ((HALF, T, W), BF16),
+    ((HALF, T, W), BF16),
+    ((HALF, T, W), BF16),
+    ((HALF, T, W), BF16),
+    ((HALF, T, N), F32),
+    ((HALF, T, N), F32),
+]
+RESULTS = [
+    ((T, NH * P_SIZE), BF16),
+    ((T, NH * P_SIZE), F32),
+    ((T, NG * N), F32),
+    ((T, NG * N), F32),
+]
+STAGED = [
+    pltpu.VMEM((HALF, T, W), BF16),
+    pltpu.VMEM((HALF, T, W), F32),
+    pltpu.VMEM((HALF, T, N), F32),
+    pltpu.VMEM((HALF, T, N), F32),
+    pltpu.SemaphoreType.DMA((HALF, 4)),
+]
+
+
+def in_order(local_parts, z, b, c):
     y, dx, xs, gs, pairs, db, dc = local_parts
-    operands = [in_hbm(a) for a in (b, c, pairs, y, z, dx, xs, gs, db, dc)]
-    wide = pltpu.VMEM((HALF, T, W), BF16)
-    thin = pltpu.VMEM((HALF, T, N), F32)
-    short = pltpu.VMEM((HALF, T, N), BF16)
+    return [in_hbm(a) for a in (b, c, pairs, y, z, dx, xs, gs, db, dc)]
+
+
+def final_own(sc, el, own_parts, other_parts):
     return pl.pallas_call(
-        functools.partial(final_kernel, bool(earlier)),
-        in_specs=[SMEM_SPEC, VMEM_SPEC] + [HBM_SPEC] * (10 + len(earlier)),
+        functools.partial(final_kernel, True),
+        in_specs=[SMEM_SPEC, VMEM_SPEC] + [HBM_SPEC] * 20,
+        out_specs=[HBM_SPEC] * 4 + [VMEM_SPEC] * 10,
+        out_shape=[pltpu.HBM(*r) for r in RESULTS] + [jax.ShapeDtypeStruct(*r) for r in LOADED],
+        scratch_shapes=[SPREAD]
+        + [pltpu.VMEM(*r) for r in LOADED]
+        + STAGED
+        + [pltpu.SemaphoreType.DMA((2, HALF, 10))],
+        compiler_params=params(24),
+        name="final_own",
+    )(sc, el, *own_parts, *other_parts)
+
+
+def final_other(sc, el, loaded, earlier):
+    return pl.pallas_call(
+        functools.partial(final_kernel, False),
+        in_specs=[SMEM_SPEC, VMEM_SPEC] + [VMEM_SPEC] * 10 + [HBM_SPEC] * 4,
         out_specs=[HBM_SPEC] * 4,
-        out_shape=[
-            pltpu.HBM((T, NH * P_SIZE), BF16),
-            pltpu.HBM((T, NH * P_SIZE), F32),
-            pltpu.HBM((T, NG * N), F32),
-            pltpu.HBM((T, NG * N), F32),
-        ],
-        input_output_aliases={12 + k: k for k in range(len(earlier))},
-        scratch_shapes=[
-            SPREAD, short, short, pltpu.VMEM((HALF, 2 * T, LANES), BF16),
-            wide, wide, wide, wide, wide, thin, thin,
-            wide, pltpu.VMEM((HALF, T, W), F32), thin, thin,
-            pltpu.SemaphoreType.DMA((HALF, 10)),
-            pltpu.SemaphoreType.DMA((HALF, 4)),
-        ],
-        compiler_params=params(24),
-        name=name,
-    )(sc, el, *operands, *earlier)
+        out_shape=[pltpu.HBM(*r) for r in RESULTS],
+        input_output_aliases={12 + k: k for k in range(4)},
+        scratch_shapes=[SPREAD] + STAGED,
+        compiler_params=params(16),
+        name="final_other",
+    )(sc, el, *loaded, *earlier)
 
 
 def body(ssm_input, gate_input, b_input, c_input, dt_raw, dt_bias, a_log, skip_gain, out_grad):
     ctx_count = lax.axis_size("ctx")
     head_count = lax.axis_size("head")
-    core = (lax.axis_index("head") % 2).astype(jnp.int32)
-    sc_other = jnp.stack([HALF * (1 - core), core])
-    sc_own = jnp.stack([HALF * core, core])
+    sc = (lax.axis_index("head") % 2).astype(jnp.int32)[None]
     bias, alog, skip = dt_bias[None, :], a_log[None, :], skip_gain[None, :]
     swap = [(k, k ^ 1) for k in range(head_count)]
     chips = [[2 * k + c for k in range(ctx_count * head_count // 2)] for c in range(2)]
@@ -542,21 +600,22 @@
             parts, ("ctx", "head"), split_axis=0, concat_axis=0, tiled=True, axis_index_groups=chips
         )
 
-    tokens = (ssm_input, gate_input, out_grad, b_input, c_input)
-    send, aux = states(True, sc_other, dt_raw, bias, alog, *tokens)
+    tokens = (b_input, ssm_input, c_input, gate_input, out_grad)
+    send, aux, aux_hbm, *kept = states_send(sc, dt_raw, bias, alog, *tokens)
     got = lax.ppermute(send, "head", swap)
-    keep = states(False, sc_own, aux, *tokens)[0]
-    gathered = exchange(merge(sc_own, keep, got))
-    got_other = lax.ppermute(keep, "head", swap)
-    loc_own = local("local_own", sc_own, aux, skip, got, *tokens)
+    keep, keep_part = states_keep(sc, aux, *kept)
+    payload, got_part = merge(sc, keep, got)
+    gathered = exchange(payload)
+    got_other = lax.ppermute(keep_part, "head", swap)
+    loc_own = local(True, sc, aux_hbm, skip, got_part, *tokens)
     back = exchange(scan(gathered, loc_own[6]))
-    loc_other = local("local_other", sc_other, aux, skip, got_other, *tokens)
+    loc_other = local(False, sc, aux_hbm, skip, got_other, *tokens)
     back, loc_other = lax.optimization_barrier((back, loc_other))
     el = back.reshape(HALF * N, 2 * W)
     el_other = lax.ppermute(el, "head", swap)
     shared = (gate_input, b_input, c_input)
-    outs = final("final_own", sc_own, el, loc_own, *shared, ())
-    return tuple(final("final_other", sc_other, el_other, loc_other, *shared, tuple(outs)))
+    outs = final_own(sc, el, in_order(loc_own, *shared), in_order(loc_other, *shared))
+    return tuple(final_other(sc, el_other, outs[4:], outs[:4]))
 
 
 def solution(mesh):

time: 112 us -> 105 us (0.938)
  Pallas kernels: 56.7 us -> 48.8 us
  starting transfers between devices: 22.8 us -> 26.1 us
  waiting for transfers between devices: 30 us -> 27.6 us
    pallas_call x7, Pallas kernels: 54.6 us -> 46.8 us  [the longest x2 26.5 us: local(): pl.pallas_call(functools.partial(local_kernel, own), in_specs=[SMEM_SPEC,...]
    all_to_all x2, waiting for transfers between devices: 30 us -> 23.5 us  [exchange(): lax.all_to_all(parts, ('ctx', 'head'), split_axis=0, concat_axis=0, tiled...]
    ppermute x1, waiting for transfers between devices: 0.01 us -> 2.47 us  [body(): got_other = lax.ppermute(keep_part, 'head', swap)]
    ppermute x1, starting transfers between devices: 0.38 us -> 2.45 us  [body(): got_other = lax.ppermute(keep_part, 'head', swap)]
    ppermute x1, waiting for transfers between devices: 0.01 us -> 1.62 us  [body(): got = lax.ppermute(send, 'head', swap)]
  transfers between devices with their start and end apart: 5 -> 5, of which waited for: 2 -> 4; matrix products, arithmetic and copies ran while one was open for 0% -> 0% of each run, Pallas kernels for 37% -> 34%
where the time goes in v2:
time: 105 us; the launch traced here: 104 us
  Pallas kernels  48.8 us (46%)
  waiting for transfers between devices  27.6 us (26%)
  starting transfers between devices  26.1 us (25%)
    pallas_call x2, Pallas kernels, local(): pl.pallas_call(functools.partial(local_kernel, own), in_specs=[SMEM_SPEC,...  26.5 us
    all_to_all x2, waiting for transfers between devices, exchange(): lax.all_to_all(parts, ('ctx', 'head'), split_axis=0, concat_axis=0, tiled...  23.5 us
    all_to_all x2, starting transfers between devices, exchange(): lax.all_to_all(parts, ('ctx', 'head'), split_axis=0, concat_axis=0, tiled...  18.2 us
    pallas_call x1, Pallas kernels, final_own(): pl.pallas_call(functools.partial(final_kernel, True), in_specs=[SMEM_SPEC...  6.78 us
    pallas_call x1, Pallas kernels, states_send(): pl.pallas_call(functools.partial(states_kernel, False), in_specs=[SMEM_SP...  5.96 us
    ppermute x1, starting transfers between devices, body(): el_other = lax.ppermute(el, 'head', swap)  4 us
    pallas_call x1, Pallas kernels, final_other(): pl.pallas_call(functools.partial(final_kernel, False), in_specs=[SMEM_SPE...  2.92 us
    ppermute x1, waiting for transfers between devices, body(): got_other = lax.ppermute(keep_part, 'head', swap)  2.47 us
  transfers between devices with their start and end apart: 5, of which 4 were waited for; matrix products, arithmetic and copies ran while one was open for 0% of the time, Pallas kernels for 34%

profile of v2, /device:TPU:1, one launch (start us, length us, event | category | flops | bytes accessed | tf_op | source)
XLA Modules:
  0.0 104.5 jit_solution(17909409398116307020)
XLA Ops:
  0.6 6.0 %states_send.1 = (bf16[512,2176]{1,0:T(8,128)(2,1)S(1)}, f32[4,128,128]{2,1,0:T(8,128)S(1)}, f32[4,128,128]{2,1,0:T(8,128)}, bf16[4,128,128]{2,1,0:T(8,128)(2,1)...) custom-call(s32[1]{0:T(128)} %bitcast.sc_ref, ...), custom_call_target="tpu_custom_call" | custom-call | tf_op jit(solution)/shard_map/states_send/pallas_call | solution.py:188
  6.6 1.5 %collective-permute-start = (bf16[512,2176]{1,0:T(8,128)(2,1)S(1)}, bf16[512,2176]{1,0:T(8,128)(2,1)S(1)}, u32[]{:S(2)}, u32[]{:S(2)}) collective-permute-start(bf16[512,2176]{1,0:T(8,128)(2,1)S(1)} %get-tuple-element.59), channel_id=1, source_target_pairs={{0,1},{1,0},{2,3},{3,2},{4,5},{5,4},{6,7},{7,6},{8,9},{9,8},{10,11... | collective-permute-start | bytes 6684680 | tf_op jit(solution)/shard_map/ppermute | solution.py:605
  8.1 2.3 %states_keep.1 = (bf16[512,2176]{1,0:T(8,128)(2,1)S(1)}, bf16[512,1152]{1,0:T(8,128)(2,1)}) custom-call(s32[1]{0:T(128)} %bitcast.sc_ref, f32[4,128,128]{2,1,0:T(8,128)S(1)} %get-tuple-element.52.refs_0_, bf16[4,128,128]{2,1,0:T(8,128)(2,1)S(1)} %get-tuple-element.53.refs_1_, bf16[4,128,1024]{2,1,0:T(8,128)(2,1)S(1)} %get-tuple-element.54.refs_2_, ...), custom_call_target="tpu_custom_call" | custom-call | tf_op jit(solution)/shard_map/states_keep/pallas_call | solution.py:204
  10.5 1.6 %collective-permute-done.got_ref = bf16[512,2176]{1,0:T(8,128)(2,1)S(1)} collective-permute-done((bf16[512,2176]{1,0:T(8,128)(2,1)S(1)}, bf16[512,2176]{1,0:T(8,128)(2,1)S(1)}, u32[]{:S(2)}, u32[]{:S(2)}) %collective-permute-start) | collective-permute-done | bytes 2228256 | tf_op jit(solution)/shard_map/ppermute | solution.py:605
  12.1 2.2 %merge_cores.1 = (bf16[64,8,2176]{2,1,0:T(8,128)(2,1)}, bf16[512,1152]{1,0:T(8,128)(2,1)}) custom-call(s32[1]{0:T(128)} %bitcast.sc_ref, bf16[512,2176]{1,0:T(8,128)(2,1)S(1)} %get-tuple-element.58.own_ref, bf16[512,2176]{1,0:T(8,128)(2,1)S(1)} %collective-permute-done.got_ref), custom_call_target="tpu_custom_call" | custom-call | tf_op jit(solution)/shard_map/merge_cores/pallas_call | solution.py:263
  14.3 11.2 %all-to-all-start = ((bf16[64,8,2176]{2,1,0:T(8,128)(2,1)}), bf16[64,8,2176]{2,1,0:T(8,128)(2,1)S(1)}, u32[]{:S(2)}, u32[]{:S(2)}) async-start(bf16[64,8,2176]{2,1,0:T(8,128)(2,1)} %get-tuple-element.60), calls=%async_computation | async-start | bytes 4456448 | tf_op jit(solution)/shard_map/all_to_all | solution.py:599
  25.6 13.3 %local_own.1 = (bf16[4,128,1024]{2,1,0:T(8,128)(2,1)}, bf16[4,128,1024]{2,1,0:T(8,128)(2,1)}, bf16[4,128,1024]{2,1,0:T(8,128)(2,1)}, bf16[4,128,1024]{2,1,0:T(8,...) custom-call(s32[1]{0:T(128)} %bitcast.sc_ref, ...), custom_call_target="tpu_custom_call" | custom-call | tf_op jit(solution)/shard_map/local_own/pallas_call | solution.py:443
  38.9 16.1 %all-to-all-done.in_ref = bf16[64,8,2176]{2,1,0:T(8,128)(2,1)S(1)} async-done(((bf16[64,8,2176]{2,1,0:T(8,128)(2,1)}), bf16[64,8,2176]{2,1,0:T(8,128)(2,1)S(1)}, u32[]{:S(2)}, u32[]{:S(2)}) %all-to-all-start) | async-done | bytes 2228256 | tf_op jit(solution)/shard_map/all_to_all | solution.py:599
  54.9 2.0 %scan_chips.1 = bf16[64,8,2048]{2,1,0:T(8,128)(2,1)} custom-call(bf16[64,8,2176]{2,1,0:T(8,128)(2,1)S(1)} %all-to-all-done.in_ref, f32[4,128,128]{2,1,0:T(8,128)} %get-tuple-element.63.after_ref.refs_9_), custom_call_target="tpu_custom_call" | custom-call | tf_op jit(solution)/shard_map/scan_chips/pallas_call | solution.py:311
  57.0 0.0 copy-start.1
  57.0 6.9 %all-to-all-start.1 = ((bf16[64,8,2048]{2,1,0:T(8,128)(2,1)}), bf16[64,8,2048]{2,1,0:T(8,128)(2,1)S(1)}, u32[]{:S(2)}, u32[]{:S(2)}) async-start(bf16[64,8,2048]{2,1,0:T(8,128)(2,1)} %scan_chips.1), calls=%async_computation.1 | async-start | bytes 4194304 | tf_op jit(solution)/shard_map/all_to_all | solution.py:599
  63.9 0.0 copy-done.1
  63.9 2.4 %collective-permute-start.1 = (bf16[512,1152]{1,0:T(8,128)(2,1)S(1)}, bf16[512,1152]{1,0:T(8,128)(2,1)S(1)}, u32[]{:S(2)}, u32[]{:S(2)}) collective-permute-start(bf16[512,1152]{1,0:T(8,128)(2,1)S(1)} %copy-done.1), channel_id=1, source_target_pairs={{0,1},{1,0},{2,3},{3,2},{4,5},{5,4},{6,7},{7,6},{8,9},{9,8},{10,11... | collective-permute-start | bytes 3538952 | tf_op jit(solution)/shard_map/ppermute | solution.py:609
  66.4 2.5 %collective-permute-done.1.got_ref = bf16[512,1152]{1,0:T(8,128)(2,1)S(1)} collective-permute-done((bf16[512,1152]{1,0:T(8,128)(2,1)S(1)}, bf16[512,1152]{1,0:T(8,128)(2,1)S(1)}, u32[]{:S(2)}, u32[]{:S(2)}) %collective-permute-start.1) | collective-permute-done | bytes 1179680 | tf_op jit(solution)/shard_map/ppermute | solution.py:609
  68.9 0.0 copy-start
  68.9 1.0 copy-done
  69.9 13.3 %local_other.1 = (bf16[4,128,1024]{2,1,0:T(8,128)(2,1)}, bf16[4,128,1024]{2,1,0:T(8,128)(2,1)}, bf16[4,128,1024]{2,1,0:T(8,128)(2,1)}, bf16[4,128,1024]{2,1,0:T(...) custom-call(s32[1]{0:T(128)} %bitcast.sc_ref, ...), custom_call_target="tpu_custom_call" | custom-call | tf_op jit(solution)/shard_map/local_other/pallas_call | solution.py:443
  83.1 7.4 %all-to-all-done.1 = bf16[64,8,2048]{2,1,0:T(8,128)(2,1)S(1)} async-done(((bf16[64,8,2048]{2,1,0:T(8,128)(2,1)}), bf16[64,8,2048]{2,1,0:T(8,128)(2,1)S(1)}, u32[]{:S(2)}, u32[]{:S(2)}) %all-to-all-start.1) | async-done | bytes 2097184 | tf_op jit(solution)/shard_map/all_to_all | solution.py:599
  90.6 4.0 %collective-permute-start.2 = (bf16[512,2048]{1,0:T(8,128)(2,1)S(1)}, bf16[512,2048]{1,0:T(8,128)(2,1)S(1)}, u32[]{:S(2)}, u32[]{:S(2)}) collective-permute-start(bf16[512,2048]{1,0:T(8,128)(2,1)S(1)} %bitcast.5), channel_id=1, source_target_pairs={{0,1},{1,0},{2,3},{3,2},{4,5},{5,4},{6,7},{7,6},{8,9},{9,8},{10,11... | collective-permute-start | bytes 6291464 | tf_op jit(solution)/shard_map/ppermute | solution.py:615
  94.6 6.8 %final_own.1 = (bf16[128,8192]{1,0:T(8,128)(2,1)}, f32[128,8192]{1,0:T(8,128)}, f32[128,1024]{1,0:T(8,128)}, f32[128,1024]{1,0:T(8,128)}, bf16[4,128,128]{2,1,0:...) custom-call(s32[1]{0:T(128)} %bitcast.sc_ref, ...), custom_call_target="tpu_custom_call" | custom-call | tf_op jit(solution)/shard_map/final_own/pallas_call | solution.py:563
  101.4 0.0 collective-permute-done.2.el_ref
  101.4 2.9 %final_other.1 = (bf16[128,8192]{1,0:T(8,128)(2,1)}, f32[128,8192]{1,0:T(8,128)}, f32[128,1024]{1,0:T(8,128)}, f32[128,1024]{1,0:T(8,128)}) custom-call(s32[1]{0:T(128)} %bitcast.sc_ref, bf16[512,2048]{1,0:T(8,128)(2,1)S(1)} %collective-permute-done.2.el_ref, ...), custom_call_target="tpu_custom_call", output_to_operand_aliasing={{0}: (12, {}), {1}: (13, {}), {2}: (14, {}), {3}: (15, {})} | custom-call | tf_op jit(solution)/shard_map/final_other/pallas_call | solution.py:578
Async XLA Ops:
  6.6 5.5 %collective-permute-start = (bf16[512,2176]{1,0:T(8,128)(2,1)S(1)}, bf16[512,2176]{1,0:T(8,128)(2,1)S(1)}, u32[]{:S(2)}, u32[]{:S(2)}) collective-permute-start(bf16[512,2176]{1,0:T(8,128)(2,1)S(1)} %get-tuple-element.59), channel_id=1, source_target_pairs={{0,1},{1,0},{2,3},{3,2},{4,5},{5,4},{6,7},{7,6},{8,9},{9,8},{10,11... | collective-permute-start | bytes 6684680 | tf_op jit(solution)/shard_map/ppermute | solution.py:605
  14.3 40.6 %all-to-all-start = ((bf16[64,8,2176]{2,1,0:T(8,128)(2,1)}), bf16[64,8,2176]{2,1,0:T(8,128)(2,1)S(1)}, u32[]{:S(2)}, u32[]{:S(2)}) async-start(bf16[64,8,2176]{2,1,0:T(8,128)(2,1)} %get-tuple-element.60), calls=%async_computation | async-start | bytes 4456448 | tf_op jit(solution)/shard_map/all_to_all | solution.py:599
  57.0 7.0 %copy-start.1 = (bf16[512,1152]{1,0:T(8,128)(2,1)S(1)}, bf16[512,1152]{1,0:T(8,128)(2,1)}, u32[]{:S(2)}) copy-start(bf16[512,1152]{1,0:T(8,128)(2,1)} %get-tuple-element.64) | copy-start | bytes 3538948
  57.0 33.6 %all-to-all-start.1 = ((bf16[64,8,2048]{2,1,0:T(8,128)(2,1)}), bf16[64,8,2048]{2,1,0:T(8,128)(2,1)S(1)}, u32[]{:S(2)}, u32[]{:S(2)}) async-start(bf16[64,8,2048]{2,1,0:T(8,128)(2,1)} %scan_chips.1), calls=%async_computation.1 | async-start | bytes 4194304 | tf_op jit(solution)/shard_map/all_to_all | solution.py:599
  63.9 4.9 %collective-permute-start.1 = (bf16[512,1152]{1,0:T(8,128)(2,1)S(1)}, bf16[512,1152]{1,0:T(8,128)(2,1)S(1)}, u32[]{:S(2)}, u32[]{:S(2)}) collective-permute-start(bf16[512,1152]{1,0:T(8,128)(2,1)S(1)} %copy-done.1), channel_id=1, source_target_pairs={{0,1},{1,0},{2,3},{3,2},{4,5},{5,4},{6,7},{7,6},{8,9},{9,8},{10,11... | collective-permute-start | bytes 3538952 | tf_op jit(solution)/shard_map/ppermute | solution.py:609
  68.9 1.0 copy-start
  90.6 10.8 %collective-permute-start.2 = (bf16[512,2048]{1,0:T(8,128)(2,1)S(1)}, bf16[512,2048]{1,0:T(8,128)(2,1)S(1)}, u32[]{:S(2)}, u32[]{:S(2)}) collective-permute-start(bf16[512,2048]{1,0:T(8,128)(2,1)S(1)} %bitcast.5), channel_id=1, source_target_pairs={{0,1},{1,0},{2,3},{3,2},{4,5},{5,4},{6,7},{7,6},{8,9},{9,8},{10,11... | collective-permute-start | bytes 6291464 | tf_op jit(solution)/shard_map/ppermute | solution.py:615

commit v3 on v2

--- a/solution.py
+++ b/solution.py
@@ -27,6 +27,7 @@
 HBM_SPEC = pl.BlockSpec(memory_space=pl.ANY)
 VMEM_SPEC = pl.BlockSpec(memory_space=pltpu.VMEM)
 SMEM_SPEC = pl.BlockSpec(memory_space=pltpu.SMEM)
+KEPT = 2
 SPREAD = pltpu.VMEM((LANES, W), BF16)
 
 
@@ -96,19 +97,33 @@
 
 def states_kernel(own, sc_ref, *refs):
     if own:
-        aux_ref, b_ref, x_ref, c_ref, z_ref, og_ref, st_ref, part_hbm, e_ref, sem_out = refs
+        aux_ref, kept, tokens, refs = refs[0], refs[1:6], refs[6:11], refs[11:]
+        st_ref, part_hbm, e_ref, used, (sem, sem_out) = refs[0], refs[1], refs[2], refs[3:8], refs[8:]
+        early = KEPT
     else:
         dt_hbm, bias_hbm, alog_hbm = refs[:3]
         tokens = refs[3:8]
         st_ref, aux_ref, aux_hbm = refs[8:11]
         kept = refs[11:16]
         e_ref = refs[16]
-        b_ref, x_ref, c_ref, z_ref, og_ref = used = refs[17:22]
+        used = refs[17:22]
         small = refs[22:25]
-        sem, sem_small = refs[25:]
+        sem, sem_small, sem_kept = refs[25:]
+        early = 0
     base = base_of(own, sc_ref)
-    copies = []
     stores = []
+
+    def loads(first, groups, targets, sems):
+        rows = []
+        for k, i in enumerate(groups):
+            row = []
+            for j, (src, dst) in enumerate(zip(tokens, targets)):
+                cut = columns(first, i, dst.shape[-1])
+                row.append(pltpu.make_async_copy(src.at[:, cut], dst.at[k], sems.at[k, j]))
+                row[-1].start()
+            rows.append(row)
+        return rows
+
     if not own:
         smalls = [
             pltpu.make_async_copy(s, d, sem_small.at[k])
@@ -116,14 +131,7 @@
         ]
         for copy in smalls:
             copy.start()
-        for half, (first, targets) in enumerate(((base, used), (base_of(True, sc_ref), kept))):
-            for i in range(HALF):
-                row = []
-                for k, (src, dst) in enumerate(zip(tokens, targets)):
-                    cut = columns(first, i, dst.shape[-1])
-                    row.append(pltpu.make_async_copy(src.at[:, cut], dst.at[i], sem.at[half, i, k]))
-                    row[-1].start()
-                copies.append(row)
+    copies = loads(base, range(early, HALF), used, sem)
     fill_spread(e_ref)
     if not own:
         for copy in smalls:
@@ -135,23 +143,29 @@
     from_start = pair_up(to_half(aux_ref[2], base))
     to_end = pair_up(to_half(aux_ref[3], base))
     for i in range(HALF):
-        if not own:
-            for copy in copies[i]:
+        if i >= early:
+            for copy in copies[i - early]:
                 copy.wait()
+        if not own and i == 0:
+            ahead = loads(base_of(True, sc_ref), range(KEPT), kept, sem_kept)
+        at = i if i < early else i - early
+        b_ref, x_ref, c_ref, z_ref, og_ref = [
+            r.at[at] for r in (kept if i < early else used)
+        ]
         here = slice(i * N, (i + 1) * N)
         te = of_group(to_end, i)
         fs = of_group(from_start, i)
-        bt = b_ref[i].T
-        ct = c_ref[i].T
+        bt = b_ref[...].T
+        ct = c_ref[...].T
         for k in range(W // CHUNK):
             cut = slice(k * CHUNK, (k + 1) * CHUNK)
             e = e_ref[:, cut]
-            xs = x_ref[i, :, cut].astype(F32) * jnp.dot(te, e, preferred_element_type=F32)
+            xs = x_ref[:, cut].astype(F32) * jnp.dot(te, e, preferred_element_type=F32)
             st_ref[here, cut] = jnp.dot(
                 bt, xs.astype(BF16), preferred_element_type=F32
             ).astype(BF16)
-            gate = silu(z_ref[i, :, cut].astype(F32))
-            hg = (og_ref[i, :, cut].astype(F32) * gate).astype(BF16)
+            gate = silu(z_ref[:, cut].astype(F32))
+            hg = (og_ref[:, cut].astype(F32) * gate).astype(BF16)
             gs = hg.astype(F32) * jnp.dot(fs, e, preferred_element_type=F32)
             st_ref[here, slice(W + k * CHUNK, W + (k + 1) * CHUNK)] = jnp.dot(
                 ct, gs.astype(BF16), preferred_element_type=F32
@@ -163,7 +177,7 @@
             for store in stores[-2:]:
                 store.start()
     if not own:
-        for row in copies[HALF:]:
+        for row in ahead:
             for copy in row:
                 copy.wait()
     for store in stores:
@@ -182,34 +196,40 @@
 PART = pltpu.HBM((HALF * N, W + LANES), BF16)
 
 
+def token_shapes(groups):
+    return [(groups, T, width) for width in (N, W, N, W, W)]
+
+
 def states_send(sc, dt, bias, alog, *tokens):
-    shapes = [(HALF, T, N), (HALF, T, W), (HALF, T, N), (HALF, T, W), (HALF, T, W)]
     aux = jax.ShapeDtypeStruct((4, T, NH), F32)
     return pl.pallas_call(
         functools.partial(states_kernel, False),
         in_specs=[SMEM_SPEC] + [HBM_SPEC] * 8,
         out_specs=[VMEM_SPEC, VMEM_SPEC, HBM_SPEC] + [VMEM_SPEC] * 5,
         out_shape=[STATE, aux, pltpu.HBM((4, T, NH), F32)]
-        + [jax.ShapeDtypeStruct(s, BF16) for s in shapes],
+        + [jax.ShapeDtypeStruct(s, BF16) for s in token_shapes(KEPT)],
         scratch_shapes=[SPREAD]
-        + [pltpu.VMEM(s, BF16) for s in shapes]
+        + [pltpu.VMEM(s, BF16) for s in token_shapes(HALF)]
         + [pltpu.VMEM((T, NH), BF16), pltpu.VMEM((1, NH), F32), pltpu.VMEM((1, NH), F32)]
-        + [pltpu.SemaphoreType.DMA((2, HALF, 5)), pltpu.SemaphoreType.DMA((4,))],
+        + [pltpu.SemaphoreType.DMA((HALF, 5)), pltpu.SemaphoreType.DMA((4,))]
+        + [pltpu.SemaphoreType.DMA((KEPT, 5))],
         compiler_params=params(24),
         name="states_send",
     )(sc, *[in_hbm(a) for a in (dt, bias, alog, *tokens)])
 
 
-def states_keep(sc, aux, *tokens):
+def states_keep(sc, aux, kept, tokens):
     return pl.pallas_call(
         functools.partial(states_kernel, True),
-        in_specs=[SMEM_SPEC] + [VMEM_SPEC] * 6,
+        in_specs=[SMEM_SPEC] + [VMEM_SPEC] * 6 + [HBM_SPEC] * 5,
         out_specs=[VMEM_SPEC, HBM_SPEC],
         out_shape=[STATE, PART],
-        scratch_shapes=[SPREAD, pltpu.SemaphoreType.DMA((HALF, 2))],
+        scratch_shapes=[SPREAD]
+        + [pltpu.VMEM(s, BF16) for s in token_shapes(HALF - KEPT)]
+        + [pltpu.SemaphoreType.DMA((HALF - KEPT, 5)), pltpu.SemaphoreType.DMA((HALF, 2))],
         compiler_params=params(12),
         name="states_keep",
-    )(sc, aux, *tokens)
+    )(sc, aux, *kept, *[in_hbm(a) for a in tokens])
 
 
 def decay_row(state_ref, at, e_ref):
@@ -325,14 +345,28 @@
 
 
 def local_kernel(
-    own, sc_ref, aux_ref, skip_ref, got_ref, b_hbm, x_hbm, c_hbm, z_hbm, og_hbm,
-    y_ref, dx_ref, xs_ref, gs_ref, pair_ref, db_ref, dc_ref,
+    own, sc_ref, aux_ref, skip_ref, got_ref, b_hbm, x_hbm, c_hbm, z_hbm, og_hbm, *refs
+):
+    if own:
+        results, refs = refs[:7], refs[7:]
+        fetched = ()
+    else:
+        ready, results, fetched, refs = refs[:5], refs[5:12], refs[12:20], refs[20:]
+    y_ref, dx_ref, xs_ref, gs_ref, pair_ref, db_ref, dc_ref = results
+    (
     e_ref, x_ref, z_ref, og_ref, b_ref, c_ref, ysum_ref, dxsum_ref, hg_ref,
-    runc_ref, run_ref, step_ref, plain_ref, sem,
-):
+    runc_ref, run_ref, step_ref, plain_ref, sem, *more,
+    ) = refs
     base = base_of(own, sc_ref)
     core = sc_ref[0]
     copies = []
+    if not own:
+        first = base_of(True, sc_ref)
+        sources = [r.at[:, columns(first, 0, w)] for r, w in ((b_hbm, N), (c_hbm, N), (z_hbm, W))]
+        sources += [r.at[0] for r in ready]
+        for k, (src, dst) in enumerate(zip(sources, fetched)):
+            copies.append(pltpu.make_async_copy(src, dst, more[0].at[k]))
+            copies[-1].start()
     for i in range(HALF):
         for k, (src, dst, width) in enumerate(
             (
@@ -436,15 +470,21 @@
     lax.fori_loop(0, HALF, one_group, 0)
 
 
-def local(own, sc, aux, skip, got, *tokens):
+FETCHED = (
+    [((T, N), BF16)] * 2 + [((T, W), BF16)] * 5 + [((2 * T, LANES), BF16)]
+)
+
+
+def local(own, sc, aux, skip, got, tokens, ready=()):
     wide = pltpu.HBM((HALF, T, W), BF16)
     thin = pltpu.HBM((HALF, T, N), F32)
-    args = [in_hbm(a) for a in (aux, skip, got, *tokens)]
+    args = [in_hbm(a) for a in (aux, skip, got, *tokens, *ready)]
+    fetched = [] if own else [jax.ShapeDtypeStruct(*f) for f in FETCHED]
     return pl.pallas_call(
         functools.partial(local_kernel, own),
-        in_specs=[SMEM_SPEC, VMEM_SPEC, VMEM_SPEC, VMEM_SPEC] + [HBM_SPEC] * 5,
-        out_specs=[VMEM_SPEC] * 7,
-        out_shape=[wide] * 4 + [pltpu.HBM((HALF, 2 * T, LANES), BF16)] + [thin] * 2,
+        in_specs=[SMEM_SPEC, VMEM_SPEC, VMEM_SPEC, VMEM_SPEC] + [HBM_SPEC] * (5 + len(ready)),
+        out_specs=[VMEM_SPEC] * (7 + len(fetched)),
+        out_shape=[wide] * 4 + [pltpu.HBM((HALF, 2 * T, LANES), BF16)] + [thin] * 2 + fetched,
         scratch_shapes=[SPREAD]
         + [pltpu.VMEM((HALF, T, W), BF16)] * 3
         + [pltpu.VMEM((HALF, T, N), BF16)] * 2
@@ -453,7 +493,8 @@
         + [pltpu.VMEM((HALF, T, LANES), F32)]
         + [pltpu.VMEM((HALF, PER, T), F32)] * 2
         + [pltpu.VMEM((HALF, 2 * T + 16, LANES), BF16)]
-        + [pltpu.SemaphoreType.DMA((HALF, 5))],
+        + [pltpu.SemaphoreType.DMA((HALF, 5))]
+        + ([] if own else [pltpu.SemaphoreType.DMA((len(FETCHED),))]),
         compiler_params=params(24),
         name="local_own" if own else "local_other",
     )(sc, *args)
@@ -461,6 +502,9 @@
 
 def final_kernel(own, sc_ref, el_ref, *refs):
     if own:
+        b0, c0, z0, y0, dx0, xs0, gs0, pair0 = refs[:8]
+        fetched = (b0, c0, pair0, y0, z0, dx0, xs0, gs0)
+        refs = refs[8:]
         sources, others, refs = refs[:10], refs[10:20], refs[20:]
         out_hbm, dx_hbm, db_hbm, dc_hbm = refs[:4]
         kept, refs = refs[4:14], refs[14:]
@@ -470,48 +514,59 @@
         targets, refs = refs[:10], refs[14:]
         out_hbm, dx_hbm, db_hbm, dc_hbm = refs[:4]
         e_ref, out_ref, dx_ref, db_ref, dc_ref, sem_out = refs[4:]
-    b_ref, c_ref, pair_ref, y_ref, z_ref, dxl_ref, xs_ref, gs_ref, dbl_ref, dcl_ref = targets
     base = base_of(own, sc_ref)
-    loads = []
-    if own:
-        for half, (first, srcs, dsts) in enumerate(
-            ((base, sources, targets), (base_of(False, sc_ref), others, kept))
-        ):
-            for i in range(HALF):
-                row = []
-                for k, (src, dst) in enumerate(zip(srcs, dsts)):
-                    if k in (0, 1, 4):
-                        src = src.at[:, columns(first, i, W if k == 4 else N)]
-                    else:
-                        src = src.at[i]
-                    row.append(pltpu.make_async_copy(src, dst.at[i], sem_in.at[half, i, k]))
-                    row[-1].start()
-                loads.append(row)
+
+    def loads(first, srcs, dsts, sems, skip=()):
+        rows = []
+        for i in range(HALF):
+            row = []
+            for k, (src, dst) in enumerate(zip(srcs, dsts)):
+                if i == 0 and k in skip:
+                    continue
+                if k in (0, 1, 4):
+                    src = src.at[:, columns(first, i, W if k == 4 else N)]
+                else:
+                    src = src.at[i]
+                row.append(pltpu.make_async_copy(src, dst.at[i], sems.at[i, k]))
+                row[-1].start()
+            rows.append(row)
+        return rows
+
+    copies = loads(base, sources, targets, sem_in.at[0], range(8)) if own else []
+    ahead = []
     fill_spread(e_ref)
     stores = []
     for i in range(HALF):
         if own:
-            for load in loads[i]:
+            for load in copies[i] if i else ():
                 load.wait()
-        b, c = b_ref[i], c_ref[i]
+            if i == 1:
+                ahead = loads(base_of(False, sc_ref), others, kept, sem_in.at[1])
+        group = [r.at[i] for r in targets]
+        if own and i == 0:
+            group[:8] = fetched
+        b_ref, c_ref, pair_ref, y_ref, z_ref, dxl_ref, xs_ref, gs_ref, dbl_ref, dcl_ref = group
+        b, c = b_ref[...], c_ref[...]
         rows = slice(i * N, (i + 1) * N)
         for k in range(W // CHUNK):
             cut = slice(k * CHUNK, (k + 1) * CHUNK)
             far = slice(W + k * CHUNK, W + (k + 1) * CHUNK)
-            scale = jnp.dot(pair_ref[i], e_ref[:, cut], preferred_element_type=F32)
-            mixed = y_ref[i, :, cut].astype(F32) + scale[0:T] * jnp.dot(
+            scale = jnp.dot(pair_ref[...], e_ref[:, cut], preferred_element_type=F32)
+            mixed = y_ref[:, cut].astype(F32) + scale[0:T] * jnp.dot(
                 c, el_ref[rows, cut], preferred_element_type=F32
             )
             mixed = mixed.astype(BF16).astype(F32)
-            out_ref[i, :, cut] = (mixed * silu(z_ref[i, :, cut].astype(F32))).astype(BF16)
-            dx_ref[i, :, cut] = dxl_ref[i, :, cut].astype(F32) + scale[T : 2 * T] * jnp.dot(
+            out_ref[i, :, cut] = (mixed * silu(z_ref[:, cut].astype(F32))).astype(BF16)
+            dx_ref[i, :, cut] = dxl_ref[:, cut].astype(F32) + scale[T : 2 * T] * jnp.dot(
                 b, el_ref[rows, far], preferred_element_type=F32
             )
-        db_ref[i] = dbl_ref[i] + lax.dot_general(
-            xs_ref[i], el_ref[rows, W:], NT, preferred_element_type=F32
+        for load in copies[0] if own and i == 0 else ():
+            load.wait()
+        db_ref[i] = dbl_ref[...] + lax.dot_general(
+            xs_ref[...], el_ref[rows, W:], NT, preferred_element_type=F32
         )
-        dc_ref[i] = dcl_ref[i] + lax.dot_general(
-            gs_ref[i], el_ref[rows, :W], NT, preferred_element_type=F32
+        dc_ref[i] = dcl_ref[...] + lax.dot_general(
+            gs_ref[...], el_ref[rows, :W], NT, preferred_element_type=F32
         )
         for k, (src, dst, width) in enumerate(
             ((out_ref, out_hbm, W), (dx_ref, dx_hbm, W), (db_ref, db_hbm, N), (dc_ref, dc_hbm, N))
@@ -520,7 +575,7 @@
                 pltpu.make_async_copy(src.at[i], dst.at[:, columns(base, i, width)], sem_out.at[i, k])
             )
             stores[-1].start()
-    for row in loads[HALF:]:
+    for row in ahead:
         for load in row:
             load.wait()
     for store in stores:
@@ -559,10 +614,10 @@
     return [in_hbm(a) for a in (b, c, pairs, y, z, dx, xs, gs, db, dc)]
 
 
-def final_own(sc, el, own_parts, other_parts):
+def final_own(sc, el, fetched, own_parts, other_parts):
     return pl.pallas_call(
         functools.partial(final_kernel, True),
-        in_specs=[SMEM_SPEC, VMEM_SPEC] + [HBM_SPEC] * 20,
+        in_specs=[SMEM_SPEC, VMEM_SPEC] + [VMEM_SPEC] * 8 + [HBM_SPEC] * 20,
         out_specs=[HBM_SPEC] * 4 + [VMEM_SPEC] * 10,
         out_shape=[pltpu.HBM(*r) for r in RESULTS] + [jax.ShapeDtypeStruct(*r) for r in LOADED],
         scratch_shapes=[SPREAD]
@@ -571,7 +626,7 @@
         + [pltpu.SemaphoreType.DMA((2, HALF, 10))],
         compiler_params=params(24),
         name="final_own",
-    )(sc, el, *own_parts, *other_parts)
+    )(sc, el, *fetched, *own_parts, *other_parts)
 
 
 def final_other(sc, el, loaded, earlier):
@@ -603,18 +658,19 @@
     tokens = (b_input, ssm_input, c_input, gate_input, out_grad)
     send, aux, aux_hbm, *kept = states_send(sc, dt_raw, bias, alog, *tokens)
     got = lax.ppermute(send, "head", swap)
-    keep, keep_part = states_keep(sc, aux, *kept)
+    keep, keep_part = states_keep(sc, aux, kept, tokens)
     payload, got_part = merge(sc, keep, got)
     gathered = exchange(payload)
     got_other = lax.ppermute(keep_part, "head", swap)
-    loc_own = local(True, sc, aux_hbm, skip, got_part, *tokens)
+    loc_own = local(True, sc, aux_hbm, skip, got_part, tokens)
     back = exchange(scan(gathered, loc_own[6]))
-    loc_other = local(False, sc, aux_hbm, skip, got_other, *tokens)
+    loc_other = local(False, sc, aux_hbm, skip, got_other, tokens, loc_own[:5])
     back, loc_other = lax.optimization_barrier((back, loc_other))
     el = back.reshape(HALF * N, 2 * W)
     el_other = lax.ppermute(el, "head", swap)
     shared = (gate_input, b_input, c_input)
-    outs = final_own(sc, el, in_order(loc_own, *shared), in_order(loc_other, *shared))
+    own_parts, other_parts = in_order(loc_own, *shared), in_order(loc_other[:7], *shared)
+    outs = final_own(sc, el, loc_other[7:], own_parts, other_parts)
     return tuple(final_other(sc, el_other, outs[4:], outs[:4]))
 
 

time: 105 us -> 104 us (level)
  starting transfers between devices: 26.1 us -> 24.7 us
  Pallas kernels: 48.8 us -> 50.1 us
    pallas_call x1, Pallas kernels: 2.35 us -> 4.21 us  [states_keep(): pl.pallas_call(functools.partial(states_kernel, True), in_specs=[SMEM_SPE...]
    ppermute x1, waiting for transfers between devices: 1.62 us -> 0.01 us  [body(): got = lax.ppermute(send, 'head', swap)]
    pallas_call x1, Pallas kernels: 5.96 us -> 4.82 us  [states_send(): pl.pallas_call(functools.partial(states_kernel, False), in_specs=[SMEM_SP...]
  transfers between devices with their start and end apart: 5 -> 5, of which waited for: 4 -> 3; matrix products, arithmetic and copies ran while one was open for 0% -> 0% of each run, Pallas kernels for 34% -> 37%
where the time goes in v3:
time: 104 us
  Pallas kernels  50.1 us (48%)
  waiting for transfers between devices  27 us (26%)
  starting transfers between devices  24.7 us (24%)
    pallas_call x2, Pallas kernels, local(): pl.pallas_call(functools.partial(local_kernel, own), in_specs=[SMEM_SPEC,...  27.1 us
    all_to_all x2, waiting for transfers between devices, exchange(): lax.all_to_all(parts, ('ctx', 'head'), split_axis=0, concat_axis=0, tiled...  24.5 us
    all_to_all x2, starting transfers between devices, exchange(): lax.all_to_all(parts, ('ctx', 'head'), split_axis=0, concat_axis=0, tiled...  17.6 us
    pallas_call x1, Pallas kernels, final_own(): pl.pallas_call(functools.partial(final_kernel, True), in_specs=[SMEM_SPEC...  6.84 us
    pallas_call x1, Pallas kernels, states_send(): pl.pallas_call(functools.partial(states_kernel, False), in_specs=[SMEM_SP...  4.82 us
    pallas_call x1, Pallas kernels, states_keep(): pl.pallas_call(functools.partial(states_kernel, True), in_specs=[SMEM_SPE...  4.21 us
    ppermute x1, starting transfers between devices, body(): el_other = lax.ppermute(el, 'head', swap)  3.43 us
    pallas_call x1, Pallas kernels, final_other(): pl.pallas_call(functools.partial(final_kernel, False), in_specs=[SMEM_SPE...  2.92 us
  transfers between devices with their start and end apart: 5, of which 3 were waited for; matrix products, arithmetic and copies ran while one was open for 0% of the time, Pallas kernels for 37%

profile of v3, /device:TPU:1, one launch (start us, length us, event | category | flops | bytes accessed | tf_op | source)
XLA Modules:
  0.0 103.7 jit_solution(17237692715396937130)
XLA Ops:
  0.6 4.8 %states_send.1 = (bf16[512,2176]{1,0:T(8,128)(2,1)S(1)}, f32[4,128,128]{2,1,0:T(8,128)S(1)}, f32[4,128,128]{2,1,0:T(8,128)}, bf16[2,128,128]{2,1,0:T(8,128)(2,1)...) custom-call(s32[1]{0:T(128)} %bitcast.sc_ref, ...), custom_call_target="tpu_custom_call" | custom-call | tf_op jit(solution)/shard_map/states_send/pallas_call | solution.py:205
  5.5 1.5 %collective-permute-start = (bf16[512,2176]{1,0:T(8,128)(2,1)S(1)}, bf16[512,2176]{1,0:T(8,128)(2,1)S(1)}, u32[]{:S(2)}, u32[]{:S(2)}) collective-permute-start(bf16[512,2176]{1,0:T(8,128)(2,1)S(1)} %get-tuple-element.75), channel_id=1, source_target_pairs={{0,1},{1,0},{2,3},{3,2},{4,5},{5,4},{6,7},{7,6},{8,9},{9,8},{10,11... | collective-permute-start | bytes 6684680 | tf_op jit(solution)/shard_map/ppermute | solution.py:660
  7.0 4.2 %states_keep.1 = (bf16[512,2176]{1,0:T(8,128)(2,1)S(1)}, bf16[512,1152]{1,0:T(8,128)(2,1)}) custom-call(s32[1]{0:T(128)} %bitcast.sc_ref, f32[4,128,128]{2,1,0:T(8,128)S(1)} %get-tuple-element.68.refs_0_, bf16[2,128,128]{2,1,0:T(8,128)(2,1)S(1)} %get-tuple-element.69.refs_1_, bf16[2,128,1024]{2,1,0:T(8,128)(2,1)S(1)} %get-tuple-element.70.refs_2_, ...), custom_call_target="tpu_custom_call" | custom-call | tf_op jit(solution)/shard_map/states_keep/pallas_call | solution.py:222
  11.2 0.0 collective-permute-done.got_ref
  11.2 2.2 %merge_cores.1 = (bf16[64,8,2176]{2,1,0:T(8,128)(2,1)}, bf16[512,1152]{1,0:T(8,128)(2,1)}) custom-call(s32[1]{0:T(128)} %bitcast.sc_ref, bf16[512,2176]{1,0:T(8,128)(2,1)S(1)} %get-tuple-element.74.own_ref, bf16[512,2176]{1,0:T(8,128)(2,1)S(1)} %collective-permute-done.got_ref), custom_call_target="tpu_custom_call" | custom-call | tf_op jit(solution)/shard_map/merge_cores/pallas_call | solution.py:283
  13.5 11.2 %all-to-all-start = ((bf16[64,8,2176]{2,1,0:T(8,128)(2,1)}), bf16[64,8,2176]{2,1,0:T(8,128)(2,1)S(1)}, u32[]{:S(2)}, u32[]{:S(2)}) async-start(bf16[64,8,2176]{2,1,0:T(8,128)(2,1)} %get-tuple-element.76), calls=%async_computation | async-start | bytes 4456448 | tf_op jit(solution)/shard_map/all_to_all | solution.py:654
  24.7 13.3 %local_own.1 = (bf16[4,128,1024]{2,1,0:T(8,128)(2,1)}, bf16[4,128,1024]{2,1,0:T(8,128)(2,1)}, bf16[4,128,1024]{2,1,0:T(8,128)(2,1)}, bf16[4,128,1024]{2,1,0:T(8,...) custom-call(s32[1]{0:T(128)} %bitcast.sc_ref, ...), custom_call_target="tpu_custom_call" | custom-call | tf_op jit(solution)/shard_map/local_own/pallas_call | solution.py:483
  38.0 16.7 %all-to-all-done.in_ref = bf16[64,8,2176]{2,1,0:T(8,128)(2,1)S(1)} async-done(((bf16[64,8,2176]{2,1,0:T(8,128)(2,1)}), bf16[64,8,2176]{2,1,0:T(8,128)(2,1)S(1)}, u32[]{:S(2)}, u32[]{:S(2)}) %all-to-all-start) | async-done | bytes 2228256 | tf_op jit(solution)/shard_map/all_to_all | solution.py:654
  54.7 2.0 %scan_chips.1 = bf16[64,8,2048]{2,1,0:T(8,128)(2,1)} custom-call(bf16[64,8,2176]{2,1,0:T(8,128)(2,1)S(1)} %all-to-all-done.in_ref, f32[4,128,128]{2,1,0:T(8,128)} %get-tuple-element.79.after_ref.refs_17_), custom_call_target="tpu_custom_call" | custom-call | tf_op jit(solution)/shard_map/scan_chips/pallas_call | solution.py:331
  56.8 0.0 copy-start.1
  56.8 6.4 %all-to-all-start.1 = ((bf16[64,8,2048]{2,1,0:T(8,128)(2,1)}), bf16[64,8,2048]{2,1,0:T(8,128)(2,1)S(1)}, u32[]{:S(2)}, u32[]{:S(2)}) async-start(bf16[64,8,2048]{2,1,0:T(8,128)(2,1)} %scan_chips.1), calls=%async_computation.1 | async-start | bytes 4194304 | tf_op jit(solution)/shard_map/all_to_all | solution.py:654
  63.2 0.0 copy-done.1
  63.2 2.1 %collective-permute-start.1 = (bf16[512,1152]{1,0:T(8,128)(2,1)S(1)}, bf16[512,1152]{1,0:T(8,128)(2,1)S(1)}, u32[]{:S(2)}, u32[]{:S(2)}) collective-permute-start(bf16[512,1152]{1,0:T(8,128)(2,1)S(1)} %copy-done.1), channel_id=1, source_target_pairs={{0,1},{1,0},{2,3},{3,2},{4,5},{5,4},{6,7},{7,6},{8,9},{9,8},{10,11... | collective-permute-start | bytes 3538952 | tf_op jit(solution)/shard_map/ppermute | solution.py:664
  65.3 2.5 %collective-permute-done.1.got_ref = bf16[512,1152]{1,0:T(8,128)(2,1)S(1)} collective-permute-done((bf16[512,1152]{1,0:T(8,128)(2,1)S(1)}, bf16[512,1152]{1,0:T(8,128)(2,1)S(1)}, u32[]{:S(2)}, u32[]{:S(2)}) %collective-permute-start.1) | collective-permute-done | bytes 1179680 | tf_op jit(solution)/shard_map/ppermute | solution.py:664
  67.8 0.0 copy-start
  67.8 1.0 copy-done
  68.8 13.8 %local_other.1 = (bf16[4,128,1024]{2,1,0:T(8,128)(2,1)}, bf16[4,128,1024]{2,1,0:T(8,128)(2,1)}, bf16[4,128,1024]{2,1,0:T(8,128)(2,1)}, bf16[4,128,1024]{2,1,0:T(...) custom-call(s32[1]{0:T(128)} %bitcast.sc_ref, ...), custom_call_target="tpu_custom_call" | custom-call | tf_op jit(solution)/shard_map/local_other/pallas_call | solution.py:483
  82.6 7.8 %all-to-all-done.1 = bf16[64,8,2048]{2,1,0:T(8,128)(2,1)S(1)} async-done(((bf16[64,8,2048]{2,1,0:T(8,128)(2,1)}), bf16[64,8,2048]{2,1,0:T(8,128)(2,1)S(1)}, u32[]{:S(2)}, u32[]{:S(2)}) %all-to-all-start.1) | async-done | bytes 2097184 | tf_op jit(solution)/shard_map/all_to_all | solution.py:654
  90.4 3.4 %collective-permute-start.2 = (bf16[512,2048]{1,0:T(8,128)(2,1)S(1)}, bf16[512,2048]{1,0:T(8,128)(2,1)S(1)}, u32[]{:S(2)}, u32[]{:S(2)}) collective-permute-start(bf16[512,2048]{1,0:T(8,128)(2,1)S(1)} %bitcast.5), channel_id=1, source_target_pairs={{0,1},{1,0},{2,3},{3,2},{4,5},{5,4},{6,7},{7,6},{8,9},{9,8},{10,11... | collective-permute-start | bytes 6291464 | tf_op jit(solution)/shard_map/ppermute | solution.py:670
  93.8 6.8 %final_own.1 = (bf16[128,8192]{1,0:T(8,128)(2,1)}, f32[128,8192]{1,0:T(8,128)}, f32[128,1024]{1,0:T(8,128)}, f32[128,1024]{1,0:T(8,128)}, bf16[4,128,128]{2,1,0:...) custom-call(s32[1]{0:T(128)} %bitcast.sc_ref, ...), custom_call_target="tpu_custom_call" | custom-call | tf_op jit(solution)/shard_map/final_own/pallas_call | solution.py:618
  100.6 0.0 collective-permute-done.2.el_ref
  100.7 2.9 %final_other.1 = (bf16[128,8192]{1,0:T(8,128)(2,1)}, f32[128,8192]{1,0:T(8,128)}, f32[128,1024]{1,0:T(8,128)}, f32[128,1024]{1,0:T(8,128)}) custom-call(s32[1]{0:T(128)} %bitcast.sc_ref, bf16[512,2048]{1,0:T(8,128)(2,1)S(1)} %collective-permute-done.2.el_ref, ...), custom_call_target="tpu_custom_call", output_to_operand_aliasing={{0}: (12, {}), {1}: (13, {}), {2}: (14, {}), {3}: (15, {})} | custom-call | tf_op jit(solution)/shard_map/final_other/pallas_call | solution.py:633
Async XLA Ops:
  5.5 5.7 %collective-permute-start = (bf16[512,2176]{1,0:T(8,128)(2,1)S(1)}, bf16[512,2176]{1,0:T(8,128)(2,1)S(1)}, u32[]{:S(2)}, u32[]{:S(2)}) collective-permute-start(bf16[512,2176]{1,0:T(8,128)(2,1)S(1)} %get-tuple-element.75), channel_id=1, source_target_pairs={{0,1},{1,0},{2,3},{3,2},{4,5},{5,4},{6,7},{7,6},{8,9},{9,8},{10,11... | collective-permute-start | bytes 6684680 | tf_op jit(solution)/shard_map/ppermute | solution.py:660
  13.5 41.3 %all-to-all-start = ((bf16[64,8,2176]{2,1,0:T(8,128)(2,1)}), bf16[64,8,2176]{2,1,0:T(8,128)(2,1)S(1)}, u32[]{:S(2)}, u32[]{:S(2)}) async-start(bf16[64,8,2176]{2,1,0:T(8,128)(2,1)} %get-tuple-element.76), calls=%async_computation | async-start | bytes 4456448 | tf_op jit(solution)/shard_map/all_to_all | solution.py:654
  56.8 6.4 %copy-start.1 = (bf16[512,1152]{1,0:T(8,128)(2,1)S(1)}, bf16[512,1152]{1,0:T(8,128)(2,1)}, u32[]{:S(2)}) copy-start(bf16[512,1152]{1,0:T(8,128)(2,1)} %get-tuple-element.80) | copy-start | bytes 3538948
  56.8 33.6 %all-to-all-start.1 = ((bf16[64,8,2048]{2,1,0:T(8,128)(2,1)}), bf16[64,8,2048]{2,1,0:T(8,128)(2,1)S(1)}, u32[]{:S(2)}, u32[]{:S(2)}) async-start(bf16[64,8,2048]{2,1,0:T(8,128)(2,1)} %scan_chips.1), calls=%async_computation.1 | async-start | bytes 4194304 | tf_op jit(solution)/shard_map/all_to_all | solution.py:654
  63.2 4.6 %collective-permute-start.1 = (bf16[512,1152]{1,0:T(8,128)(2,1)S(1)}, bf16[512,1152]{1,0:T(8,128)(2,1)S(1)}, u32[]{:S(2)}, u32[]{:S(2)}) collective-permute-start(bf16[512,1152]{1,0:T(8,128)(2,1)S(1)} %copy-done.1), channel_id=1, source_target_pairs={{0,1},{1,0},{2,3},{3,2},{4,5},{5,4},{6,7},{7,6},{8,9},{9,8},{10,11... | collective-permute-start | bytes 3538952 | tf_op jit(solution)/shard_map/ppermute | solution.py:664
  67.8 1.0 copy-start
  90.4 10.3 %collective-permute-start.2 = (bf16[512,2048]{1,0:T(8,128)(2,1)S(1)}, bf16[512,2048]{1,0:T(8,128)(2,1)S(1)}, u32[]{:S(2)}, u32[]{:S(2)}) collective-permute-start(bf16[512,2048]{1,0:T(8,128)(2,1)S(1)} %bitcast.5), channel_id=1, source_target_pairs={{0,1},{1,0},{2,3},{3,2},{4,5},{5,4},{6,7},{7,6},{8,9},{9,8},{10,11... | collective-permute-start | bytes 6291464 | tf_op jit(solution)/shard_map/ppermute | solution.py:670

commit v4 on v3

--- a/solution.py
+++ b/solution.py
@@ -27,7 +27,7 @@
 HBM_SPEC = pl.BlockSpec(memory_space=pl.ANY)
 VMEM_SPEC = pl.BlockSpec(memory_space=pltpu.VMEM)
 SMEM_SPEC = pl.BlockSpec(memory_space=pltpu.SMEM)
-KEPT = 2
+KEPT = 3
 SPREAD = pltpu.VMEM((LANES, W), BF16)
 
 
@@ -533,15 +533,13 @@
         return rows
 
     copies = loads(base, sources, targets, sem_in.at[0], range(8)) if own else []
-    ahead = []
+    ahead = loads(base_of(False, sc_ref), others, kept, sem_in.at[1]) if own else []
     fill_spread(e_ref)
     stores = []
     for i in range(HALF):
         if own:
             for load in copies[i] if i else ():
                 load.wait()
-            if i == 1:
-                ahead = loads(base_of(False, sc_ref), others, kept, sem_in.at[1])
         group = [r.at[i] for r in targets]
         if own and i == 0:
             group[:8] = fetched

time: 104 us -> 104 us (level)
  waiting for transfers between devices: 27 us -> 25.6 us
  starting transfers between devices: 24.7 us -> 26 us
    all_to_all x2, waiting for transfers between devices: 24.5 us -> 23 us  [exchange(): lax.all_to_all(parts, ('ctx', 'head'), split_axis=0, concat_axis=0, tiled...]
  transfers between devices with their start and end apart: 5 -> 5, of which waited for: 3 -> 4; matrix products, arithmetic and copies ran while one was open for 0% -> 0% of each run, Pallas kernels for 37% -> 36%
where the time goes in v4:
time: 104 us; the launch traced here: 103 us
  Pallas kernels  49.8 us (48%)
  starting transfers between devices  26 us (25%)
  waiting for transfers between devices  25.6 us (25%)
    pallas_call x2, Pallas kernels, local(): pl.pallas_call(functools.partial(local_kernel, own), in_specs=[SMEM_SPEC,...  27.1 us
    all_to_all x2, waiting for transfers between devices, exchange(): lax.all_to_all(parts, ('ctx', 'head'), split_axis=0, concat_axis=0, tiled...  23 us
    all_to_all x2, starting transfers between devices, exchange(): lax.all_to_all(parts, ('ctx', 'head'), split_axis=0, concat_axis=0, tiled...  18.2 us
    pallas_call x1, Pallas kernels, final_own(): pl.pallas_call(functools.partial(final_kernel, True), in_specs=[SMEM_SPEC...  6.7 us
    pallas_call x1, Pallas kernels, states_send(): pl.pallas_call(functools.partial(states_kernel, False), in_specs=[SMEM_SP...  5 us
    ppermute x1, starting transfers between devices, body(): el_other = lax.ppermute(el, 'head', swap)  4 us
    pallas_call x1, Pallas kernels, states_keep(): pl.pallas_call(functools.partial(states_kernel, True), in_specs=[SMEM_SPE...  3.82 us
    pallas_call x1, Pallas kernels, final_other(): pl.pallas_call(functools.partial(final_kernel, False), in_specs=[SMEM_SPE...  2.92 us
  transfers between devices with their start and end apart: 5, of which 4 were waited for; matrix products, arithmetic and copies ran while one was open for 0% of the time, Pallas kernels for 36%

profile of v4, /device:TPU:1, one launch (start us, length us, event | category | flops | bytes accessed | tf_op | source)
XLA Modules:
  0.0 103.3 jit_solution(7238136087380153910)
XLA Ops:
  0.6 5.0 %states_send.1 = (bf16[512,2176]{1,0:T(8,128)(2,1)S(1)}, f32[4,128,128]{2,1,0:T(8,128)S(1)}, f32[4,128,128]{2,1,0:T(8,128)}, bf16[3,128,128]{2,1,0:T(8,128)(2,1)...) custom-call(s32[1]{0:T(128)} %bitcast.sc_ref, ...), custom_call_target="tpu_custom_call" | custom-call | tf_op jit(solution)/shard_map/states_send/pallas_call | solution.py:205
  5.7 1.4 %collective-permute-start = (bf16[512,2176]{1,0:T(8,128)(2,1)S(1)}, bf16[512,2176]{1,0:T(8,128)(2,1)S(1)}, u32[]{:S(2)}, u32[]{:S(2)}) collective-permute-start(bf16[512,2176]{1,0:T(8,128)(2,1)S(1)} %get-tuple-element.75), channel_id=1, source_target_pairs={{0,1},{1,0},{2,3},{3,2},{4,5},{5,4},{6,7},{7,6},{8,9},{9,8},{10,11... | collective-permute-start | bytes 6684680 | tf_op jit(solution)/shard_map/ppermute | solution.py:658
  7.0 3.8 %states_keep.1 = (bf16[512,2176]{1,0:T(8,128)(2,1)S(1)}, bf16[512,1152]{1,0:T(8,128)(2,1)}) custom-call(s32[1]{0:T(128)} %bitcast.sc_ref, f32[4,128,128]{2,1,0:T(8,128)S(1)} %get-tuple-element.68.refs_0_, bf16[3,128,128]{2,1,0:T(8,128)(2,1)S(1)} %get-tuple-element.69.refs_1_, bf16[3,128,1024]{2,1,0:T(8,128)(2,1)S(1)} %get-tuple-element.70.refs_2_, ...), custom_call_target="tpu_custom_call" | custom-call | tf_op jit(solution)/shard_map/states_keep/pallas_call | solution.py:222
  10.9 0.1 collective-permute-done.got_ref
  11.0 2.2 %merge_cores.1 = (bf16[64,8,2176]{2,1,0:T(8,128)(2,1)}, bf16[512,1152]{1,0:T(8,128)(2,1)}) custom-call(s32[1]{0:T(128)} %bitcast.sc_ref, bf16[512,2176]{1,0:T(8,128)(2,1)S(1)} %get-tuple-element.74.own_ref, bf16[512,2176]{1,0:T(8,128)(2,1)S(1)} %collective-permute-done.got_ref), custom_call_target="tpu_custom_call" | custom-call | tf_op jit(solution)/shard_map/merge_cores/pallas_call | solution.py:283
  13.3 11.2 %all-to-all-start = ((bf16[64,8,2176]{2,1,0:T(8,128)(2,1)}), bf16[64,8,2176]{2,1,0:T(8,128)(2,1)S(1)}, u32[]{:S(2)}, u32[]{:S(2)}) async-start(bf16[64,8,2176]{2,1,0:T(8,128)(2,1)} %get-tuple-element.76), calls=%async_computation | async-start | bytes 4456448 | tf_op jit(solution)/shard_map/all_to_all | solution.py:652
  24.5 13.3 %local_own.1 = (bf16[4,128,1024]{2,1,0:T(8,128)(2,1)}, bf16[4,128,1024]{2,1,0:T(8,128)(2,1)}, bf16[4,128,1024]{2,1,0:T(8,128)(2,1)}, bf16[4,128,1024]{2,1,0:T(8,...) custom-call(s32[1]{0:T(128)} %bitcast.sc_ref, ...), custom_call_target="tpu_custom_call" | custom-call | tf_op jit(solution)/shard_map/local_own/pallas_call | solution.py:483
  37.8 16.1 %all-to-all-done.in_ref = bf16[64,8,2176]{2,1,0:T(8,128)(2,1)S(1)} async-done(((bf16[64,8,2176]{2,1,0:T(8,128)(2,1)}), bf16[64,8,2176]{2,1,0:T(8,128)(2,1)S(1)}, u32[]{:S(2)}, u32[]{:S(2)}) %all-to-all-start) | async-done | bytes 2228256 | tf_op jit(solution)/shard_map/all_to_all | solution.py:652
  53.8 2.0 %scan_chips.1 = bf16[64,8,2048]{2,1,0:T(8,128)(2,1)} custom-call(bf16[64,8,2176]{2,1,0:T(8,128)(2,1)S(1)} %all-to-all-done.in_ref, f32[4,128,128]{2,1,0:T(8,128)} %get-tuple-element.79.after_ref.refs_17_), custom_call_target="tpu_custom_call" | custom-call | tf_op jit(solution)/shard_map/scan_chips/pallas_call | solution.py:331
  55.9 0.0 copy-start.1
  55.9 6.9 %all-to-all-start.1 = ((bf16[64,8,2048]{2,1,0:T(8,128)(2,1)}), bf16[64,8,2048]{2,1,0:T(8,128)(2,1)S(1)}, u32[]{:S(2)}, u32[]{:S(2)}) async-start(bf16[64,8,2048]{2,1,0:T(8,128)(2,1)} %scan_chips.1), calls=%async_computation.1 | async-start | bytes 4194304 | tf_op jit(solution)/shard_map/all_to_all | solution.py:652
  62.8 0.0 copy-done.1
  62.8 2.4 %collective-permute-start.1 = (bf16[512,1152]{1,0:T(8,128)(2,1)S(1)}, bf16[512,1152]{1,0:T(8,128)(2,1)S(1)}, u32[]{:S(2)}, u32[]{:S(2)}) collective-permute-start(bf16[512,1152]{1,0:T(8,128)(2,1)S(1)} %copy-done.1), channel_id=1, source_target_pairs={{0,1},{1,0},{2,3},{3,2},{4,5},{5,4},{6,7},{7,6},{8,9},{9,8},{10,11... | collective-permute-start | bytes 3538952 | tf_op jit(solution)/shard_map/ppermute | solution.py:662
  65.3 2.5 %collective-permute-done.1.got_ref = bf16[512,1152]{1,0:T(8,128)(2,1)S(1)} collective-permute-done((bf16[512,1152]{1,0:T(8,128)(2,1)S(1)}, bf16[512,1152]{1,0:T(8,128)(2,1)S(1)}, u32[]{:S(2)}, u32[]{:S(2)}) %collective-permute-start.1) | collective-permute-done | bytes 1179680 | tf_op jit(solution)/shard_map/ppermute | solution.py:662
  67.8 0.0 copy-start
  67.8 1.0 copy-done
  68.8 13.8 %local_other.1 = (bf16[4,128,1024]{2,1,0:T(8,128)(2,1)}, bf16[4,128,1024]{2,1,0:T(8,128)(2,1)}, bf16[4,128,1024]{2,1,0:T(8,128)(2,1)}, bf16[4,128,1024]{2,1,0:T(...) custom-call(s32[1]{0:T(128)} %bitcast.sc_ref, ...), custom_call_target="tpu_custom_call" | custom-call | tf_op jit(solution)/shard_map/local_other/pallas_call | solution.py:483
  82.6 6.9 %all-to-all-done.1 = bf16[64,8,2048]{2,1,0:T(8,128)(2,1)S(1)} async-done(((bf16[64,8,2048]{2,1,0:T(8,128)(2,1)}), bf16[64,8,2048]{2,1,0:T(8,128)(2,1)S(1)}, u32[]{:S(2)}, u32[]{:S(2)}) %all-to-all-start.1) | async-done | bytes 2097184 | tf_op jit(solution)/shard_map/all_to_all | solution.py:652
  89.5 4.0 %collective-permute-start.2 = (bf16[512,2048]{1,0:T(8,128)(2,1)S(1)}, bf16[512,2048]{1,0:T(8,128)(2,1)S(1)}, u32[]{:S(2)}, u32[]{:S(2)}) collective-permute-start(bf16[512,2048]{1,0:T(8,128)(2,1)S(1)} %bitcast.5), channel_id=1, source_target_pairs={{0,1},{1,0},{2,3},{3,2},{4,5},{5,4},{6,7},{7,6},{8,9},{9,8},{10,11... | collective-permute-start | bytes 6291464 | tf_op jit(solution)/shard_map/ppermute | solution.py:668
  93.5 6.7 %final_own.1 = (bf16[128,8192]{1,0:T(8,128)(2,1)}, f32[128,8192]{1,0:T(8,128)}, f32[128,1024]{1,0:T(8,128)}, f32[128,1024]{1,0:T(8,128)}, bf16[4,128,128]{2,1,0:...) custom-call(s32[1]{0:T(128)} %bitcast.sc_ref, ...), custom_call_target="tpu_custom_call" | custom-call | tf_op jit(solution)/shard_map/final_own/pallas_call | solution.py:616
  100.2 0.0 collective-permute-done.2.el_ref
  100.2 2.9 %final_other.1 = (bf16[128,8192]{1,0:T(8,128)(2,1)}, f32[128,8192]{1,0:T(8,128)}, f32[128,1024]{1,0:T(8,128)}, f32[128,1024]{1,0:T(8,128)}) custom-call(s32[1]{0:T(128)} %bitcast.sc_ref, bf16[512,2048]{1,0:T(8,128)(2,1)S(1)} %collective-permute-done.2.el_ref, ...), custom_call_target="tpu_custom_call", output_to_operand_aliasing={{0}: (12, {}), {1}: (13, {}), {2}: (14, {}), {3}: (15, {})} | custom-call | tf_op jit(solution)/shard_map/final_other/pallas_call | solution.py:631
Async XLA Ops:
  5.7 5.4 %collective-permute-start = (bf16[512,2176]{1,0:T(8,128)(2,1)S(1)}, bf16[512,2176]{1,0:T(8,128)(2,1)S(1)}, u32[]{:S(2)}, u32[]{:S(2)}) collective-permute-start(bf16[512,2176]{1,0:T(8,128)(2,1)S(1)} %get-tuple-element.75), channel_id=1, source_target_pairs={{0,1},{1,0},{2,3},{3,2},{4,5},{5,4},{6,7},{7,6},{8,9},{9,8},{10,11... | collective-permute-start | bytes 6684680 | tf_op jit(solution)/shard_map/ppermute | solution.py:658
  13.3 40.6 %all-to-all-start = ((bf16[64,8,2176]{2,1,0:T(8,128)(2,1)}), bf16[64,8,2176]{2,1,0:T(8,128)(2,1)S(1)}, u32[]{:S(2)}, u32[]{:S(2)}) async-start(bf16[64,8,2176]{2,1,0:T(8,128)(2,1)} %get-tuple-element.76), calls=%async_computation | async-start | bytes 4456448 | tf_op jit(solution)/shard_map/all_to_all | solution.py:652
  55.9 7.0 %copy-start.1 = (bf16[512,1152]{1,0:T(8,128)(2,1)S(1)}, bf16[512,1152]{1,0:T(8,128)(2,1)}, u32[]{:S(2)}) copy-start(bf16[512,1152]{1,0:T(8,128)(2,1)} %get-tuple-element.80) | copy-start | bytes 3538948
  55.9 33.6 %all-to-all-start.1 = ((bf16[64,8,2048]{2,1,0:T(8,128)(2,1)}), bf16[64,8,2048]{2,1,0:T(8,128)(2,1)S(1)}, u32[]{:S(2)}, u32[]{:S(2)}) async-start(bf16[64,8,2048]{2,1,0:T(8,128)(2,1)} %scan_chips.1), calls=%async_computation.1 | async-start | bytes 4194304 | tf_op jit(solution)/shard_map/all_to_all | solution.py:652
  62.8 4.9 %collective-permute-start.1 = (bf16[512,1152]{1,0:T(8,128)(2,1)S(1)}, bf16[512,1152]{1,0:T(8,128)(2,1)S(1)}, u32[]{:S(2)}, u32[]{:S(2)}) collective-permute-start(bf16[512,1152]{1,0:T(8,128)(2,1)S(1)} %copy-done.1), channel_id=1, source_target_pairs={{0,1},{1,0},{2,3},{3,2},{4,5},{5,4},{6,7},{7,6},{8,9},{9,8},{10,11... | collective-permute-start | bytes 3538952 | tf_op jit(solution)/shard_map/ppermute | solution.py:662
  67.8 1.0 copy-start
  89.5 10.7 %collective-permute-start.2 = (bf16[512,2048]{1,0:T(8,128)(2,1)S(1)}, bf16[512,2048]{1,0:T(8,128)(2,1)S(1)}, u32[]{:S(2)}, u32[]{:S(2)}) collective-permute-start(bf16[512,2048]{1,0:T(8,128)(2,1)S(1)} %bitcast.5), channel_id=1, source_target_pairs={{0,1},{1,0},{2,3},{3,2},{4,5},{5,4},{6,7},{7,6},{8,9},{9,8},{10,11... | collective-permute-start | bytes 6291464 | tf_op jit(solution)/shard_map/ppermute | solution.py:668

commit v5 on v4

--- a/solution.py
+++ b/solution.py
@@ -238,8 +238,11 @@
 
 
 def merge_kernel(sc_ref, own_ref, got_ref, out_hbm, part_hbm, e_ref, out_ref, sem, sem_out):
+    core = sc_ref[0]
+    parts = part_copies(got_ref, part_hbm, slice(0, HALF * N), 1 - core, sem)
+    for part in parts:
+        part.start()
     fill_spread(e_ref)
-    core = sc_ref[0]
 
     def merge(r0, r1):
         stores = []
@@ -264,9 +267,6 @@
             out_ref[there, :, 2 * W :] = both.astype(BF16)
             stores.append(pltpu.make_async_copy(out_ref.at[there], out_hbm.at[there], sem_out.at[i]))
             stores[-1].start()
-        stores += part_copies(got_ref, part_hbm, slice(0, HALF * N), 1 - core, sem)
-        for store in stores[-2:]:
-            store.start()
         for store in stores:
             store.wait()
 
@@ -277,6 +277,9 @@
     @pl.when(core != 0)
     def _():
         merge(got_ref, own_ref)
+
+    for part in parts:
+        part.wait()
 
 
 def merge(sc, own, got):
@@ -354,7 +357,7 @@
         ready, results, fetched, refs = refs[:5], refs[5:12], refs[12:20], refs[20:]
     y_ref, dx_ref, xs_ref, gs_ref, pair_ref, db_ref, dc_ref = results
     (
-    e_ref, x_ref, z_ref, og_ref, b_ref, c_ref, ysum_ref, dxsum_ref, hg_ref,
+    e_ref, x_ref, z_ref, og_ref, b_ref, c_ref, ysum_ref, dxsum_ref, dbsum_ref, dcsum_ref, hg_ref,
     runc_ref, run_ref, step_ref, plain_ref, sem, *more,
     ) = refs
     base = base_of(own, sc_ref)
@@ -439,10 +442,10 @@
             dxsum_ref[:, here] = jnp.where(left, dxs[0], dxs[1]) + skip * g.astype(F32)
         high = mass.astype(BF16)
         low = (mass - high.astype(F32)).astype(BF16)
-        dc_ref[i] = jnp.dot(high, b, preferred_element_type=F32) + jnp.dot(
+        dcsum_ref[...] = jnp.dot(high, b, preferred_element_type=F32) + jnp.dot(
             low, b, preferred_element_type=F32
         )
-        db_ref[i] = jnp.dot(high.T, c, preferred_element_type=F32) + jnp.dot(
+        dbsum_ref[...] = jnp.dot(high.T, c, preferred_element_type=F32) + jnp.dot(
             low.T, c, preferred_element_type=F32
         )
         rows = pl.ds(pl.multiple_of(i * N, N), N)
@@ -453,7 +456,7 @@
             fs = jnp.dot(plain_ref[i, 0:T], e_ref[...], preferred_element_type=F32)
             ysum_ref[...] += fs * jnp.dot(c, partner, preferred_element_type=F32)
             gs = (hg_ref[...].astype(F32) * fs).astype(BF16)
-            dc_ref[i] += lax.dot_general(gs, partner, NT, preferred_element_type=F32)
+            dcsum_ref[...] += lax.dot_general(gs, partner, NT, preferred_element_type=F32)
 
         @pl.when(core == 0)
         def _():
@@ -461,10 +464,12 @@
             te = jnp.dot(plain_ref[i, T : 2 * T], e_ref[...], preferred_element_type=F32)
             dxsum_ref[...] += te * jnp.dot(b, partner, preferred_element_type=F32)
             xs = (x_ref[i].astype(F32) * te).astype(BF16)
-            db_ref[i] += lax.dot_general(xs, partner, NT, preferred_element_type=F32)
+            dbsum_ref[...] += lax.dot_general(xs, partner, NT, preferred_element_type=F32)
 
         y_ref[i] = ysum_ref[...].astype(BF16)
         dx_ref[i] = dxsum_ref[...].astype(BF16)
+        db_ref[i] = dbsum_ref[...].astype(BF16)
+        dc_ref[i] = dcsum_ref[...].astype(BF16)
         return unused
 
     lax.fori_loop(0, HALF, one_group, 0)
@@ -477,7 +482,7 @@
 
 def local(own, sc, aux, skip, got, tokens, ready=()):
     wide = pltpu.HBM((HALF, T, W), BF16)
-    thin = pltpu.HBM((HALF, T, N), F32)
+    thin = pltpu.HBM((HALF, T, N), BF16)
     args = [in_hbm(a) for a in (aux, skip, got, *tokens, *ready)]
     fetched = [] if own else [jax.ShapeDtypeStruct(*f) for f in FETCHED]
     return pl.pallas_call(
@@ -489,6 +494,7 @@
         + [pltpu.VMEM((HALF, T, W), BF16)] * 3
         + [pltpu.VMEM((HALF, T, N), BF16)] * 2
         + [pltpu.VMEM((T, W), F32)] * 2
+        + [pltpu.VMEM((T, N), F32)] * 2
         + [pltpu.VMEM((T, W), BF16)]
         + [pltpu.VMEM((HALF, T, LANES), F32)]
         + [pltpu.VMEM((HALF, PER, T), F32)] * 2
@@ -560,10 +566,10 @@
             )
         for load in copies[0] if own and i == 0 else ():
             load.wait()
-        db_ref[i] = dbl_ref[...] + lax.dot_general(
+        db_ref[i] = dbl_ref[...].astype(F32) + lax.dot_general(
             xs_ref[...], el_ref[rows, W:], NT, preferred_element_type=F32
         )
-        dc_ref[i] = dcl_ref[...] + lax.dot_general(
+        dc_ref[i] = dcl_ref[...].astype(F32) + lax.dot_general(
             gs_ref[...], el_ref[rows, :W], NT, preferred_element_type=F32
         )
         for k, (src, dst, width) in enumerate(
@@ -589,8 +595,8 @@
     ((HALF, T, W), BF16),
     ((HALF, T, W), BF16),
     ((HALF, T, W), BF16),
-    ((HALF, T, N), F32),
-    ((HALF, T, N), F32),
+    ((HALF, T, N), BF16),
+    ((HALF, T, N), BF16),
 ]
 RESULTS = [
     ((T, NH * P_SIZE), BF16),

time: 104 us -> 103 us (level)
  no operation moved by 1% of the time
where the time goes in v5:
time: 103 us
  Pallas kernels  49.1 us (48%)
  starting transfers between devices  26 us (25%)
  waiting for transfers between devices  25.7 us (25%)
    pallas_call x2, Pallas kernels, local(): pl.pallas_call(functools.partial(local_kernel, own), in_specs=[SMEM_SPEC,...  26.9 us
    all_to_all x2, waiting for transfers between devices, exchange(): lax.all_to_all(parts, ('ctx', 'head'), split_axis=0, concat_axis=0, tiled...  23.1 us
    all_to_all x2, starting transfers between devices, exchange(): lax.all_to_all(parts, ('ctx', 'head'), split_axis=0, concat_axis=0, tiled...  18.2 us
    pallas_call x1, Pallas kernels, final_own(): pl.pallas_call(functools.partial(final_kernel, True), in_specs=[SMEM_SPEC...  6.56 us
    pallas_call x1, Pallas kernels, states_send(): pl.pallas_call(functools.partial(states_kernel, False), in_specs=[SMEM_SP...  5 us
    ppermute x1, starting transfers between devices, body(): el_other = lax.ppermute(el, 'head', swap)  4 us
    pallas_call x1, Pallas kernels, states_keep(): pl.pallas_call(functools.partial(states_kernel, True), in_specs=[SMEM_SPE...  3.84 us
    pallas_call x1, Pallas kernels, final_other(): pl.pallas_call(functools.partial(final_kernel, False), in_specs=[SMEM_SPE...  2.92 us
  transfers between devices with their start and end apart: 5, of which 4 were waited for; matrix products, arithmetic and copies ran while one was open for 0% of the time, Pallas kernels for 36%

profile of v5, /device:TPU:1, one launch (start us, length us, event | category | flops | bytes accessed | tf_op | source)
XLA Modules:
  0.0 102.8 jit_solution(9496870517511070381)
XLA Ops:
  0.6 5.0 %states_send.1 = (bf16[512,2176]{1,0:T(8,128)(2,1)S(1)}, f32[4,128,128]{2,1,0:T(8,128)S(1)}, f32[4,128,128]{2,1,0:T(8,128)}, bf16[3,128,128]{2,1,0:T(8,128)(2,1)...) custom-call(s32[1]{0:T(128)} %bitcast.sc_ref, ...), custom_call_target="tpu_custom_call" | custom-call | tf_op jit(solution)/shard_map/states_send/pallas_call | solution.py:205
  5.7 1.4 %collective-permute-start = (bf16[512,2176]{1,0:T(8,128)(2,1)S(1)}, bf16[512,2176]{1,0:T(8,128)(2,1)S(1)}, u32[]{:S(2)}, u32[]{:S(2)}) collective-permute-start(bf16[512,2176]{1,0:T(8,128)(2,1)S(1)} %get-tuple-element.75), channel_id=1, source_target_pairs={{0,1},{1,0},{2,3},{3,2},{4,5},{5,4},{6,7},{7,6},{8,9},{9,8},{10,11... | collective-permute-start | bytes 6684680 | tf_op jit(solution)/shard_map/ppermute | solution.py:664
  7.0 3.8 %states_keep.1 = (bf16[512,2176]{1,0:T(8,128)(2,1)S(1)}, bf16[512,1152]{1,0:T(8,128)(2,1)}) custom-call(s32[1]{0:T(128)} %bitcast.sc_ref, f32[4,128,128]{2,1,0:T(8,128)S(1)} %get-tuple-element.68.refs_0_, bf16[3,128,128]{2,1,0:T(8,128)(2,1)S(1)} %get-tuple-element.69.refs_1_, bf16[3,128,1024]{2,1,0:T(8,128)(2,1)S(1)} %get-tuple-element.70.refs_2_, ...), custom_call_target="tpu_custom_call" | custom-call | tf_op jit(solution)/shard_map/states_keep/pallas_call | solution.py:222
  10.9 0.1 collective-permute-done.got_ref
  11.0 1.9 %merge_cores.1 = (bf16[64,8,2176]{2,1,0:T(8,128)(2,1)}, bf16[512,1152]{1,0:T(8,128)(2,1)}) custom-call(s32[1]{0:T(128)} %bitcast.sc_ref, bf16[512,2176]{1,0:T(8,128)(2,1)S(1)} %get-tuple-element.74.own_ref, bf16[512,2176]{1,0:T(8,128)(2,1)S(1)} %collective-permute-done.got_ref), custom_call_target="tpu_custom_call" | custom-call | tf_op jit(solution)/shard_map/merge_cores/pallas_call | solution.py:286
  12.9 11.2 %all-to-all-start = ((bf16[64,8,2176]{2,1,0:T(8,128)(2,1)}), bf16[64,8,2176]{2,1,0:T(8,128)(2,1)S(1)}, u32[]{:S(2)}, u32[]{:S(2)}) async-start(bf16[64,8,2176]{2,1,0:T(8,128)(2,1)} %get-tuple-element.76), calls=%async_computation | async-start | bytes 4456448 | tf_op jit(solution)/shard_map/all_to_all | solution.py:658
  24.1 13.1 %local_own.1 = (bf16[4,128,1024]{2,1,0:T(8,128)(2,1)}, bf16[4,128,1024]{2,1,0:T(8,128)(2,1)}, bf16[4,128,1024]{2,1,0:T(8,128)(2,1)}, bf16[4,128,1024]{2,1,0:T(8,...) custom-call(s32[1]{0:T(128)} %bitcast.sc_ref, ...), custom_call_target="tpu_custom_call" | custom-call | tf_op jit(solution)/shard_map/local_own/pallas_call | solution.py:488
  37.3 16.2 %all-to-all-done.in_ref = bf16[64,8,2176]{2,1,0:T(8,128)(2,1)S(1)} async-done(((bf16[64,8,2176]{2,1,0:T(8,128)(2,1)}), bf16[64,8,2176]{2,1,0:T(8,128)(2,1)S(1)}, u32[]{:S(2)}, u32[]{:S(2)}) %all-to-all-start) | async-done | bytes 2228256 | tf_op jit(solution)/shard_map/all_to_all | solution.py:658
  53.5 2.0 %scan_chips.1 = bf16[64,8,2048]{2,1,0:T(8,128)(2,1)} custom-call(bf16[64,8,2176]{2,1,0:T(8,128)(2,1)S(1)} %all-to-all-done.in_ref, bf16[4,128,128]{2,1,0:T(8,128)(2,1)} %get-tuple-element.79.after_ref.refs_17_), custom_call_target="tpu_custom_call" | custom-call | tf_op jit(solution)/shard_map/scan_chips/pallas_call | solution.py:334
  55.5 0.0 copy-start.1
  55.5 6.9 %all-to-all-start.1 = ((bf16[64,8,2048]{2,1,0:T(8,128)(2,1)}), bf16[64,8,2048]{2,1,0:T(8,128)(2,1)S(1)}, u32[]{:S(2)}, u32[]{:S(2)}) async-start(bf16[64,8,2048]{2,1,0:T(8,128)(2,1)} %scan_chips.1), calls=%async_computation.1 | async-start | bytes 4194304 | tf_op jit(solution)/shard_map/all_to_all | solution.py:658
  62.4 0.0 copy-done.1
  62.5 2.4 %collective-permute-start.1 = (bf16[512,1152]{1,0:T(8,128)(2,1)S(1)}, bf16[512,1152]{1,0:T(8,128)(2,1)S(1)}, u32[]{:S(2)}, u32[]{:S(2)}) collective-permute-start(bf16[512,1152]{1,0:T(8,128)(2,1)S(1)} %copy-done.1), channel_id=1, source_target_pairs={{0,1},{1,0},{2,3},{3,2},{4,5},{5,4},{6,7},{7,6},{8,9},{9,8},{10,11... | collective-permute-start | bytes 3538952 | tf_op jit(solution)/shard_map/ppermute | solution.py:668
  64.9 2.5 %collective-permute-done.1.got_ref = bf16[512,1152]{1,0:T(8,128)(2,1)S(1)} collective-permute-done((bf16[512,1152]{1,0:T(8,128)(2,1)S(1)}, bf16[512,1152]{1,0:T(8,128)(2,1)S(1)}, u32[]{:S(2)}, u32[]{:S(2)}) %collective-permute-start.1) | collective-permute-done | bytes 1179680 | tf_op jit(solution)/shard_map/ppermute | solution.py:668
  67.4 0.0 copy-start
  67.4 1.0 copy-done
  68.4 13.8 %local_other.1 = (bf16[4,128,1024]{2,1,0:T(8,128)(2,1)}, bf16[4,128,1024]{2,1,0:T(8,128)(2,1)}, bf16[4,128,1024]{2,1,0:T(8,128)(2,1)}, bf16[4,128,1024]{2,1,0:T(...) custom-call(s32[1]{0:T(128)} %bitcast.sc_ref, ...), custom_call_target="tpu_custom_call" | custom-call | tf_op jit(solution)/shard_map/local_other/pallas_call | solution.py:488
  82.2 6.9 %all-to-all-done.1 = bf16[64,8,2048]{2,1,0:T(8,128)(2,1)S(1)} async-done(((bf16[64,8,2048]{2,1,0:T(8,128)(2,1)}), bf16[64,8,2048]{2,1,0:T(8,128)(2,1)S(1)}, u32[]{:S(2)}, u32[]{:S(2)}) %all-to-all-start.1) | async-done | bytes 2097184 | tf_op jit(solution)/shard_map/all_to_all | solution.py:658
  89.1 4.0 %collective-permute-start.2 = (bf16[512,2048]{1,0:T(8,128)(2,1)S(1)}, bf16[512,2048]{1,0:T(8,128)(2,1)S(1)}, u32[]{:S(2)}, u32[]{:S(2)}) collective-permute-start(bf16[512,2048]{1,0:T(8,128)(2,1)S(1)} %bitcast.5), channel_id=1, source_target_pairs={{0,1},{1,0},{2,3},{3,2},{4,5},{5,4},{6,7},{7,6},{8,9},{9,8},{10,11... | collective-permute-start | bytes 6291464 | tf_op jit(solution)/shard_map/ppermute | solution.py:674
  93.1 6.6 %final_own.1 = (bf16[128,8192]{1,0:T(8,128)(2,1)}, f32[128,8192]{1,0:T(8,128)}, f32[128,1024]{1,0:T(8,128)}, f32[128,1024]{1,0:T(8,128)}, bf16[4,128,128]{2,1,0:...) custom-call(s32[1]{0:T(128)} %bitcast.sc_ref, ...), custom_call_target="tpu_custom_call" | custom-call | tf_op jit(solution)/shard_map/final_own/pallas_call | solution.py:622
  99.7 0.0 collective-permute-done.2.el_ref
  99.7 2.9 %final_other.1 = (bf16[128,8192]{1,0:T(8,128)(2,1)}, f32[128,8192]{1,0:T(8,128)}, f32[128,1024]{1,0:T(8,128)}, f32[128,1024]{1,0:T(8,128)}) custom-call(s32[1]{0:T(128)} %bitcast.sc_ref, bf16[512,2048]{1,0:T(8,128)(2,1)S(1)} %collective-permute-done.2.el_ref, ...), custom_call_target="tpu_custom_call", output_to_operand_aliasing={{0}: (12, {}), {1}: (13, {}), {2}: (14, {}), {3}: (15, {})} | custom-call | tf_op jit(solution)/shard_map/final_other/pallas_call | solution.py:637
Async XLA Ops:
  5.7 5.4 %collective-permute-start = (bf16[512,2176]{1,0:T(8,128)(2,1)S(1)}, bf16[512,2176]{1,0:T(8,128)(2,1)S(1)}, u32[]{:S(2)}, u32[]{:S(2)}) collective-permute-start(bf16[512,2176]{1,0:T(8,128)(2,1)S(1)} %get-tuple-element.75), channel_id=1, source_target_pairs={{0,1},{1,0},{2,3},{3,2},{4,5},{5,4},{6,7},{7,6},{8,9},{9,8},{10,11... | collective-permute-start | bytes 6684680 | tf_op jit(solution)/shard_map/ppermute | solution.py:664
  12.9 40.6 %all-to-all-start = ((bf16[64,8,2176]{2,1,0:T(8,128)(2,1)}), bf16[64,8,2176]{2,1,0:T(8,128)(2,1)S(1)}, u32[]{:S(2)}, u32[]{:S(2)}) async-start(bf16[64,8,2176]{2,1,0:T(8,128)(2,1)} %get-tuple-element.76), calls=%async_computation | async-start | bytes 4456448 | tf_op jit(solution)/shard_map/all_to_all | solution.py:658
  55.5 7.0 %copy-start.1 = (bf16[512,1152]{1,0:T(8,128)(2,1)S(1)}, bf16[512,1152]{1,0:T(8,128)(2,1)}, u32[]{:S(2)}) copy-start(bf16[512,1152]{1,0:T(8,128)(2,1)} %get-tuple-element.80) | copy-start | bytes 3538948
  55.5 33.6 %all-to-all-start.1 = ((bf16[64,8,2048]{2,1,0:T(8,128)(2,1)}), bf16[64,8,2048]{2,1,0:T(8,128)(2,1)S(1)}, u32[]{:S(2)}, u32[]{:S(2)}) async-start(bf16[64,8,2048]{2,1,0:T(8,128)(2,1)} %scan_chips.1), calls=%async_computation.1 | async-start | bytes 4194304 | tf_op jit(solution)/shard_map/all_to_all | solution.py:658
  62.5 4.9 %collective-permute-start.1 = (bf16[512,1152]{1,0:T(8,128)(2,1)S(1)}, bf16[512,1152]{1,0:T(8,128)(2,1)S(1)}, u32[]{:S(2)}, u32[]{:S(2)}) collective-permute-start(bf16[512,1152]{1,0:T(8,128)(2,1)S(1)} %copy-done.1), channel_id=1, source_target_pairs={{0,1},{1,0},{2,3},{3,2},{4,5},{5,4},{6,7},{7,6},{8,9},{9,8},{10,11... | collective-permute-start | bytes 3538952 | tf_op jit(solution)/shard_map/ppermute | solution.py:668
  67.4 1.0 copy-start
  89.1 10.6 %collective-permute-start.2 = (bf16[512,2048]{1,0:T(8,128)(2,1)S(1)}, bf16[512,2048]{1,0:T(8,128)(2,1)S(1)}, u32[]{:S(2)}, u32[]{:S(2)}) collective-permute-start(bf16[512,2048]{1,0:T(8,128)(2,1)S(1)} %bitcast.5), channel_id=1, source_target_pairs={{0,1},{1,0},{2,3},{3,2},{4,5},{5,4},{6,7},{7,6},{8,9},{9,8},{10,11... | collective-permute-start | bytes 6291464 | tf_op jit(solution)/shard_map/ppermute | solution.py:674

commit v6 on v5

--- a/solution.py
+++ b/solution.py
@@ -542,6 +542,13 @@
     ahead = loads(base_of(False, sc_ref), others, kept, sem_in.at[1]) if own else []
     fill_spread(e_ref)
     stores = []
+
+    def put(k, src, dst, width):
+        stores.append(
+            pltpu.make_async_copy(src.at[i], dst.at[:, columns(base, i, width)], sem_out.at[i, k])
+        )
+        stores[-1].start()
+
     for i in range(HALF):
         if own:
             for load in copies[i] if i else ():
@@ -564,6 +571,8 @@
             dx_ref[i, :, cut] = dxl_ref[:, cut].astype(F32) + scale[T : 2 * T] * jnp.dot(
                 b, el_ref[rows, far], preferred_element_type=F32
             )
+        put(0, out_ref, out_hbm, W)
+        put(1, dx_ref, dx_hbm, W)
         for load in copies[0] if own and i == 0 else ():
             load.wait()
         db_ref[i] = dbl_ref[...].astype(F32) + lax.dot_general(
@@ -572,13 +581,8 @@
         dc_ref[i] = dcl_ref[...].astype(F32) + lax.dot_general(
             gs_ref[...], el_ref[rows, :W], NT, preferred_element_type=F32
         )
-        for k, (src, dst, width) in enumerate(
-            ((out_ref, out_hbm, W), (dx_ref, dx_hbm, W), (db_ref, db_hbm, N), (dc_ref, dc_hbm, N))
-        ):
-            stores.append(
-                pltpu.make_async_copy(src.at[i], dst.at[:, columns(base, i, width)], sem_out.at[i, k])
-            )
-            stores[-1].start()
+        put(2, db_ref, db_hbm, N)
+        put(3, dc_ref, dc_hbm, N)
     for row in ahead:
         for load in row:
             load.wait()

time: 103 us -> 103 us (level)
  no operation moved by 1% of the time
where the time goes in v6:
time: 103 us
  Pallas kernels  49.1 us (48%)
  starting transfers between devices  26 us (25%)
  waiting for transfers between devices  25.7 us (25%)
    pallas_call x2, Pallas kernels, local(): pl.pallas_call(functools.partial(local_kernel, own), in_specs=[SMEM_SPEC,...  26.9 us
    all_to_all x2, waiting for transfers between devices, exchange(): lax.all_to_all(parts, ('ctx', 'head'), split_axis=0, concat_axis=0, tiled...  23.1 us
    all_to_all x2, starting transfers between devices, exchange(): lax.all_to_all(parts, ('ctx', 'head'), split_axis=0, concat_axis=0, tiled...  18.2 us
    pallas_call x1, Pallas kernels, final_own(): pl.pallas_call(functools.partial(final_kernel, True), in_specs=[SMEM_SPEC...  6.56 us
    pallas_call x1, Pallas kernels, states_send(): pl.pallas_call(functools.partial(states_kernel, False), in_specs=[SMEM_SP...  5 us
    ppermute x1, starting transfers between devices, body(): el_other = lax.ppermute(el, 'head', swap)  4 us
    pallas_call x1, Pallas kernels, states_keep(): pl.pallas_call(functools.partial(states_kernel, True), in_specs=[SMEM_SPE...  3.84 us
    pallas_call x1, Pallas kernels, final_other(): pl.pallas_call(functools.partial(final_kernel, False), in_specs=[SMEM_SPE...  2.92 us
  transfers between devices with their start and end apart: 5, of which 4 were waited for; matrix products, arithmetic and copies ran while one was open for 0% of the time, Pallas kernels for 36%

profile of v6, /device:TPU:1, one launch (start us, length us, event | category | flops | bytes accessed | tf_op | source)
XLA Modules:
  0.0 102.8 jit_solution(12514968242788020922)
XLA Ops:
  0.6 5.0 %states_send.1 = (bf16[512,2176]{1,0:T(8,128)(2,1)S(1)}, f32[4,128,128]{2,1,0:T(8,128)S(1)}, f32[4,128,128]{2,1,0:T(8,128)}, bf16[3,128,128]{2,1,0:T(8,128)(2,1)...) custom-call(s32[1]{0:T(128)} %bitcast.sc_ref, ...), custom_call_target="tpu_custom_call" | custom-call | tf_op jit(solution)/shard_map/states_send/pallas_call | solution.py:205
  5.7 1.4 %collective-permute-start = (bf16[512,2176]{1,0:T(8,128)(2,1)S(1)}, bf16[512,2176]{1,0:T(8,128)(2,1)S(1)}, u32[]{:S(2)}, u32[]{:S(2)}) collective-permute-start(bf16[512,2176]{1,0:T(8,128)(2,1)S(1)} %get-tuple-element.75), channel_id=1, source_target_pairs={{0,1},{1,0},{2,3},{3,2},{4,5},{5,4},{6,7},{7,6},{8,9},{9,8},{10,11... | collective-permute-start | bytes 6684680 | tf_op jit(solution)/shard_map/ppermute | solution.py:668
  7.0 3.8 %states_keep.1 = (bf16[512,2176]{1,0:T(8,128)(2,1)S(1)}, bf16[512,1152]{1,0:T(8,128)(2,1)}) custom-call(s32[1]{0:T(128)} %bitcast.sc_ref, f32[4,128,128]{2,1,0:T(8,128)S(1)} %get-tuple-element.68.refs_0_, bf16[3,128,128]{2,1,0:T(8,128)(2,1)S(1)} %get-tuple-element.69.refs_1_, bf16[3,128,1024]{2,1,0:T(8,128)(2,1)S(1)} %get-tuple-element.70.refs_2_, ...), custom_call_target="tpu_custom_call" | custom-call | tf_op jit(solution)/shard_map/states_keep/pallas_call | solution.py:222
  10.9 0.1 collective-permute-done.got_ref
  11.0 1.9 %merge_cores.1 = (bf16[64,8,2176]{2,1,0:T(8,128)(2,1)}, bf16[512,1152]{1,0:T(8,128)(2,1)}) custom-call(s32[1]{0:T(128)} %bitcast.sc_ref, bf16[512,2176]{1,0:T(8,128)(2,1)S(1)} %get-tuple-element.74.own_ref, bf16[512,2176]{1,0:T(8,128)(2,1)S(1)} %collective-permute-done.got_ref), custom_call_target="tpu_custom_call" | custom-call | tf_op jit(solution)/shard_map/merge_cores/pallas_call | solution.py:286
  12.9 11.2 %all-to-all-start = ((bf16[64,8,2176]{2,1,0:T(8,128)(2,1)}), bf16[64,8,2176]{2,1,0:T(8,128)(2,1)S(1)}, u32[]{:S(2)}, u32[]{:S(2)}) async-start(bf16[64,8,2176]{2,1,0:T(8,128)(2,1)} %get-tuple-element.76), calls=%async_computation | async-start | bytes 4456448 | tf_op jit(solution)/shard_map/all_to_all | solution.py:662
  24.1 13.1 %local_own.1 = (bf16[4,128,1024]{2,1,0:T(8,128)(2,1)}, bf16[4,128,1024]{2,1,0:T(8,128)(2,1)}, bf16[4,128,1024]{2,1,0:T(8,128)(2,1)}, bf16[4,128,1024]{2,1,0:T(8,...) custom-call(s32[1]{0:T(128)} %bitcast.sc_ref, ...), custom_call_target="tpu_custom_call" | custom-call | tf_op jit(solution)/shard_map/local_own/pallas_call | solution.py:488
  37.3 16.2 %all-to-all-done.in_ref = bf16[64,8,2176]{2,1,0:T(8,128)(2,1)S(1)} async-done(((bf16[64,8,2176]{2,1,0:T(8,128)(2,1)}), bf16[64,8,2176]{2,1,0:T(8,128)(2,1)S(1)}, u32[]{:S(2)}, u32[]{:S(2)}) %all-to-all-start) | async-done | bytes 2228256 | tf_op jit(solution)/shard_map/all_to_all | solution.py:662
  53.5 2.0 %scan_chips.1 = bf16[64,8,2048]{2,1,0:T(8,128)(2,1)} custom-call(bf16[64,8,2176]{2,1,0:T(8,128)(2,1)S(1)} %all-to-all-done.in_ref, bf16[4,128,128]{2,1,0:T(8,128)(2,1)} %get-tuple-element.79.after_ref.refs_17_), custom_call_target="tpu_custom_call" | custom-call | tf_op jit(solution)/shard_map/scan_chips/pallas_call | solution.py:334
  55.5 0.0 copy-start.1
  55.5 6.9 %all-to-all-start.1 = ((bf16[64,8,2048]{2,1,0:T(8,128)(2,1)}), bf16[64,8,2048]{2,1,0:T(8,128)(2,1)S(1)}, u32[]{:S(2)}, u32[]{:S(2)}) async-start(bf16[64,8,2048]{2,1,0:T(8,128)(2,1)} %scan_chips.1), calls=%async_computation.1 | async-start | bytes 4194304 | tf_op jit(solution)/shard_map/all_to_all | solution.py:662
  62.4 0.0 copy-done.1
  62.5 2.4 %collective-permute-start.1 = (bf16[512,1152]{1,0:T(8,128)(2,1)S(1)}, bf16[512,1152]{1,0:T(8,128)(2,1)S(1)}, u32[]{:S(2)}, u32[]{:S(2)}) collective-permute-start(bf16[512,1152]{1,0:T(8,128)(2,1)S(1)} %copy-done.1), channel_id=1, source_target_pairs={{0,1},{1,0},{2,3},{3,2},{4,5},{5,4},{6,7},{7,6},{8,9},{9,8},{10,11... | collective-permute-start | bytes 3538952 | tf_op jit(solution)/shard_map/ppermute | solution.py:672
  64.9 2.5 %collective-permute-done.1.got_ref = bf16[512,1152]{1,0:T(8,128)(2,1)S(1)} collective-permute-done((bf16[512,1152]{1,0:T(8,128)(2,1)S(1)}, bf16[512,1152]{1,0:T(8,128)(2,1)S(1)}, u32[]{:S(2)}, u32[]{:S(2)}) %collective-permute-start.1) | collective-permute-done | bytes 1179680 | tf_op jit(solution)/shard_map/ppermute | solution.py:672
  67.4 0.0 copy-start
  67.4 1.0 copy-done
  68.4 13.8 %local_other.1 = (bf16[4,128,1024]{2,1,0:T(8,128)(2,1)}, bf16[4,128,1024]{2,1,0:T(8,128)(2,1)}, bf16[4,128,1024]{2,1,0:T(8,128)(2,1)}, bf16[4,128,1024]{2,1,0:T(...) custom-call(s32[1]{0:T(128)} %bitcast.sc_ref, ...), custom_call_target="tpu_custom_call" | custom-call | tf_op jit(solution)/shard_map/local_other/pallas_call | solution.py:488
  82.2 6.9 %all-to-all-done.1 = bf16[64,8,2048]{2,1,0:T(8,128)(2,1)S(1)} async-done(((bf16[64,8,2048]{2,1,0:T(8,128)(2,1)}), bf16[64,8,2048]{2,1,0:T(8,128)(2,1)S(1)}, u32[]{:S(2)}, u32[]{:S(2)}) %all-to-all-start.1) | async-done | bytes 2097184 | tf_op jit(solution)/shard_map/all_to_all | solution.py:662
  89.1 4.0 %collective-permute-start.2 = (bf16[512,2048]{1,0:T(8,128)(2,1)S(1)}, bf16[512,2048]{1,0:T(8,128)(2,1)S(1)}, u32[]{:S(2)}, u32[]{:S(2)}) collective-permute-start(bf16[512,2048]{1,0:T(8,128)(2,1)S(1)} %bitcast.5), channel_id=1, source_target_pairs={{0,1},{1,0},{2,3},{3,2},{4,5},{5,4},{6,7},{7,6},{8,9},{9,8},{10,11... | collective-permute-start | bytes 6291464 | tf_op jit(solution)/shard_map/ppermute | solution.py:678
  93.1 6.6 %final_own.1 = (bf16[128,8192]{1,0:T(8,128)(2,1)}, f32[128,8192]{1,0:T(8,128)}, f32[128,1024]{1,0:T(8,128)}, f32[128,1024]{1,0:T(8,128)}, bf16[4,128,128]{2,1,0:...) custom-call(s32[1]{0:T(128)} %bitcast.sc_ref, ...), custom_call_target="tpu_custom_call" | custom-call | tf_op jit(solution)/shard_map/final_own/pallas_call | solution.py:626
  99.7 0.0 collective-permute-done.2.el_ref
  99.7 2.9 %final_other.1 = (bf16[128,8192]{1,0:T(8,128)(2,1)}, f32[128,8192]{1,0:T(8,128)}, f32[128,1024]{1,0:T(8,128)}, f32[128,1024]{1,0:T(8,128)}) custom-call(s32[1]{0:T(128)} %bitcast.sc_ref, bf16[512,2048]{1,0:T(8,128)(2,1)S(1)} %collective-permute-done.2.el_ref, ...), custom_call_target="tpu_custom_call", output_to_operand_aliasing={{0}: (12, {}), {1}: (13, {}), {2}: (14, {}), {3}: (15, {})} | custom-call | tf_op jit(solution)/shard_map/final_other/pallas_call | solution.py:641
Async XLA Ops:
  5.7 5.4 %collective-permute-start = (bf16[512,2176]{1,0:T(8,128)(2,1)S(1)}, bf16[512,2176]{1,0:T(8,128)(2,1)S(1)}, u32[]{:S(2)}, u32[]{:S(2)}) collective-permute-start(bf16[512,2176]{1,0:T(8,128)(2,1)S(1)} %get-tuple-element.75), channel_id=1, source_target_pairs={{0,1},{1,0},{2,3},{3,2},{4,5},{5,4},{6,7},{7,6},{8,9},{9,8},{10,11... | collective-permute-start | bytes 6684680 | tf_op jit(solution)/shard_map/ppermute | solution.py:668
  12.9 40.6 %all-to-all-start = ((bf16[64,8,2176]{2,1,0:T(8,128)(2,1)}), bf16[64,8,2176]{2,1,0:T(8,128)(2,1)S(1)}, u32[]{:S(2)}, u32[]{:S(2)}) async-start(bf16[64,8,2176]{2,1,0:T(8,128)(2,1)} %get-tuple-element.76), calls=%async_computation | async-start | bytes 4456448 | tf_op jit(solution)/shard_map/all_to_all | solution.py:662
  55.5 7.0 %copy-start.1 = (bf16[512,1152]{1,0:T(8,128)(2,1)S(1)}, bf16[512,1152]{1,0:T(8,128)(2,1)}, u32[]{:S(2)}) copy-start(bf16[512,1152]{1,0:T(8,128)(2,1)} %get-tuple-element.80) | copy-start | bytes 3538948
  55.5 33.6 %all-to-all-start.1 = ((bf16[64,8,2048]{2,1,0:T(8,128)(2,1)}), bf16[64,8,2048]{2,1,0:T(8,128)(2,1)S(1)}, u32[]{:S(2)}, u32[]{:S(2)}) async-start(bf16[64,8,2048]{2,1,0:T(8,128)(2,1)} %scan_chips.1), calls=%async_computation.1 | async-start | bytes 4194304 | tf_op jit(solution)/shard_map/all_to_all | solution.py:662
  62.5 4.9 %collective-permute-start.1 = (bf16[512,1152]{1,0:T(8,128)(2,1)S(1)}, bf16[512,1152]{1,0:T(8,128)(2,1)S(1)}, u32[]{:S(2)}, u32[]{:S(2)}) collective-permute-start(bf16[512,1152]{1,0:T(8,128)(2,1)S(1)} %copy-done.1), channel_id=1, source_target_pairs={{0,1},{1,0},{2,3},{3,2},{4,5},{5,4},{6,7},{7,6},{8,9},{9,8},{10,11... | collective-permute-start | bytes 3538952 | tf_op jit(solution)/shard_map/ppermute | solution.py:672
  67.4 1.0 copy-start
  89.1 10.6 %collective-permute-start.2 = (bf16[512,2048]{1,0:T(8,128)(2,1)S(1)}, bf16[512,2048]{1,0:T(8,128)(2,1)S(1)}, u32[]{:S(2)}, u32[]{:S(2)}) collective-permute-start(bf16[512,2048]{1,0:T(8,128)(2,1)S(1)} %bitcast.5), channel_id=1, source_target_pairs={{0,1},{1,0},{2,3},{3,2},{4,5},{5,4},{6,7},{7,6},{8,9},{9,8},{10,11... | collective-permute-start | bytes 6291464 | tf_op jit(solution)/shard_map/ppermute | solution.py:678

commit v7 on v6

--- a/solution.py
+++ b/solution.py
@@ -314,16 +314,16 @@
         out_ref[j, :, W:] = l.astype(BF16)
         return d_ref[j] * l + in_ref[j, :, W : 2 * W].astype(F32)
 
-    parts = ((0, chips, slice(0, W)), (chips // 2, chips, slice(W, 2 * W)), (0, chips // 2, slice(W, 2 * W)))
+    parts = ((0, chips, slice(0, W)), (chips // 4, chips, slice(W, 2 * W)), (0, chips // 4, slice(W, 2 * W)))
     stores = [
         pltpu.make_async_copy(out_ref.at[a:b, :, cut], out_hbm.at[a:b, :, cut], sem.at[k])
         for k, (a, b, cut) in enumerate(parts)
     ]
     lax.fori_loop(0, chips, forward, zero, unroll=8)
     stores[0].start()
-    l = lax.fori_loop(0, chips // 2, backward, zero, unroll=8)
+    l = lax.fori_loop(0, chips - chips // 4, backward, zero, unroll=8)
     stores[1].start()
-    lax.fori_loop(chips // 2, chips, backward, l, unroll=8)
+    lax.fori_loop(chips - chips // 4, chips, backward, l, unroll=8)
     stores[2].start()
     for store in stores:
         store.wait()

time: 103 us -> 103 us (level)
  no operation moved by 1% of the time
where the time goes in v7:
time: 103 us
  Pallas kernels  49.1 us (48%)
  starting transfers between devices  26 us (25%)
  waiting for transfers between devices  25.8 us (25%)
    pallas_call x2, Pallas kernels, local(): pl.pallas_call(functools.partial(local_kernel, own), in_specs=[SMEM_SPEC,...  26.9 us
    all_to_all x2, waiting for transfers between devices, exchange(): lax.all_to_all(parts, ('ctx', 'head'), split_axis=0, concat_axis=0, tiled...  23.1 us
    all_to_all x2, starting transfers between devices, exchange(): lax.all_to_all(parts, ('ctx', 'head'), split_axis=0, concat_axis=0, tiled...  18.2 us
    pallas_call x1, Pallas kernels, final_own(): pl.pallas_call(functools.partial(final_kernel, True), in_specs=[SMEM_SPEC...  6.56 us
    pallas_call x1, Pallas kernels, states_send(): pl.pallas_call(functools.partial(states_kernel, False), in_specs=[SMEM_SP...  5 us
    ppermute x1, starting transfers between devices, body(): el_other = lax.ppermute(el, 'head', swap)  4 us
    pallas_call x1, Pallas kernels, states_keep(): pl.pallas_call(functools.partial(states_kernel, True), in_specs=[SMEM_SPE...  3.84 us
    pallas_call x1, Pallas kernels, final_other(): pl.pallas_call(functools.partial(final_kernel, False), in_specs=[SMEM_SPE...  2.92 us
  transfers between devices with their start and end apart: 5, of which 4 were waited for; matrix products, arithmetic and copies ran while one was open for 0% of the time, Pallas kernels for 36%

profile of v7, /device:TPU:1, one launch (start us, length us, event | category | flops | bytes accessed | tf_op | source)
XLA Modules:
  0.0 102.8 jit_solution(13472611908795544215)
XLA Ops:
  0.6 5.0 %states_send.1 = (bf16[512,2176]{1,0:T(8,128)(2,1)S(1)}, f32[4,128,128]{2,1,0:T(8,128)S(1)}, f32[4,128,128]{2,1,0:T(8,128)}, bf16[3,128,128]{2,1,0:T(8,128)(2,1)...) custom-call(s32[1]{0:T(128)} %bitcast.sc_ref, ...), custom_call_target="tpu_custom_call" | custom-call | tf_op jit(solution)/shard_map/states_send/pallas_call | solution.py:205
  5.7 1.4 %collective-permute-start = (bf16[512,2176]{1,0:T(8,128)(2,1)S(1)}, bf16[512,2176]{1,0:T(8,128)(2,1)S(1)}, u32[]{:S(2)}, u32[]{:S(2)}) collective-permute-start(bf16[512,2176]{1,0:T(8,128)(2,1)S(1)} %get-tuple-element.75), channel_id=1, source_target_pairs={{0,1},{1,0},{2,3},{3,2},{4,5},{5,4},{6,7},{7,6},{8,9},{9,8},{10,11... | collective-permute-start | bytes 6684680 | tf_op jit(solution)/shard_map/ppermute | solution.py:668
  7.0 3.8 %states_keep.1 = (bf16[512,2176]{1,0:T(8,128)(2,1)S(1)}, bf16[512,1152]{1,0:T(8,128)(2,1)}) custom-call(s32[1]{0:T(128)} %bitcast.sc_ref, f32[4,128,128]{2,1,0:T(8,128)S(1)} %get-tuple-element.68.refs_0_, bf16[3,128,128]{2,1,0:T(8,128)(2,1)S(1)} %get-tuple-element.69.refs_1_, bf16[3,128,1024]{2,1,0:T(8,128)(2,1)S(1)} %get-tuple-element.70.refs_2_, ...), custom_call_target="tpu_custom_call" | custom-call | tf_op jit(solution)/shard_map/states_keep/pallas_call | solution.py:222
  10.9 0.1 collective-permute-done.got_ref
  11.0 1.9 %merge_cores.1 = (bf16[64,8,2176]{2,1,0:T(8,128)(2,1)}, bf16[512,1152]{1,0:T(8,128)(2,1)}) custom-call(s32[1]{0:T(128)} %bitcast.sc_ref, bf16[512,2176]{1,0:T(8,128)(2,1)S(1)} %get-tuple-element.74.own_ref, bf16[512,2176]{1,0:T(8,128)(2,1)S(1)} %collective-permute-done.got_ref), custom_call_target="tpu_custom_call" | custom-call | tf_op jit(solution)/shard_map/merge_cores/pallas_call | solution.py:286
  12.9 11.2 %all-to-all-start = ((bf16[64,8,2176]{2,1,0:T(8,128)(2,1)}), bf16[64,8,2176]{2,1,0:T(8,128)(2,1)S(1)}, u32[]{:S(2)}, u32[]{:S(2)}) async-start(bf16[64,8,2176]{2,1,0:T(8,128)(2,1)} %get-tuple-element.76), calls=%async_computation | async-start | bytes 4456448 | tf_op jit(solution)/shard_map/all_to_all | solution.py:662
  24.1 13.1 %local_own.1 = (bf16[4,128,1024]{2,1,0:T(8,128)(2,1)}, bf16[4,128,1024]{2,1,0:T(8,128)(2,1)}, bf16[4,128,1024]{2,1,0:T(8,128)(2,1)}, bf16[4,128,1024]{2,1,0:T(8,...) custom-call(s32[1]{0:T(128)} %bitcast.sc_ref, ...), custom_call_target="tpu_custom_call" | custom-call | tf_op jit(solution)/shard_map/local_own/pallas_call | solution.py:488
  37.3 16.2 %all-to-all-done.in_ref = bf16[64,8,2176]{2,1,0:T(8,128)(2,1)S(1)} async-done(((bf16[64,8,2176]{2,1,0:T(8,128)(2,1)}), bf16[64,8,2176]{2,1,0:T(8,128)(2,1)S(1)}, u32[]{:S(2)}, u32[]{:S(2)}) %all-to-all-start) | async-done | bytes 2228256 | tf_op jit(solution)/shard_map/all_to_all | solution.py:662
  53.5 2.0 %scan_chips.1 = bf16[64,8,2048]{2,1,0:T(8,128)(2,1)} custom-call(bf16[64,8,2176]{2,1,0:T(8,128)(2,1)S(1)} %all-to-all-done.in_ref, bf16[4,128,128]{2,1,0:T(8,128)(2,1)} %get-tuple-element.79.after_ref.refs_17_), custom_call_target="tpu_custom_call" | custom-call | tf_op jit(solution)/shard_map/scan_chips/pallas_call | solution.py:334
  55.5 0.0 copy-start.1
  55.5 6.9 %all-to-all-start.1 = ((bf16[64,8,2048]{2,1,0:T(8,128)(2,1)}), bf16[64,8,2048]{2,1,0:T(8,128)(2,1)S(1)}, u32[]{:S(2)}, u32[]{:S(2)}) async-start(bf16[64,8,2048]{2,1,0:T(8,128)(2,1)} %scan_chips.1), calls=%async_computation.1 | async-start | bytes 4194304 | tf_op jit(solution)/shard_map/all_to_all | solution.py:662
  62.4 0.0 copy-done.1
  62.5 2.4 %collective-permute-start.1 = (bf16[512,1152]{1,0:T(8,128)(2,1)S(1)}, bf16[512,1152]{1,0:T(8,128)(2,1)S(1)}, u32[]{:S(2)}, u32[]{:S(2)}) collective-permute-start(bf16[512,1152]{1,0:T(8,128)(2,1)S(1)} %copy-done.1), channel_id=1, source_target_pairs={{0,1},{1,0},{2,3},{3,2},{4,5},{5,4},{6,7},{7,6},{8,9},{9,8},{10,11... | collective-permute-start | bytes 3538952 | tf_op jit(solution)/shard_map/ppermute | solution.py:672
  64.9 2.5 %collective-permute-done.1.got_ref = bf16[512,1152]{1,0:T(8,128)(2,1)S(1)} collective-permute-done((bf16[512,1152]{1,0:T(8,128)(2,1)S(1)}, bf16[512,1152]{1,0:T(8,128)(2,1)S(1)}, u32[]{:S(2)}, u32[]{:S(2)}) %collective-permute-start.1) | collective-permute-done | bytes 1179680 | tf_op jit(solution)/shard_map/ppermute | solution.py:672
  67.4 0.0 copy-start
  67.4 1.0 copy-done
  68.4 13.8 %local_other.1 = (bf16[4,128,1024]{2,1,0:T(8,128)(2,1)}, bf16[4,128,1024]{2,1,0:T(8,128)(2,1)}, bf16[4,128,1024]{2,1,0:T(8,128)(2,1)}, bf16[4,128,1024]{2,1,0:T(...) custom-call(s32[1]{0:T(128)} %bitcast.sc_ref, ...), custom_call_target="tpu_custom_call" | custom-call | tf_op jit(solution)/shard_map/local_other/pallas_call | solution.py:488
  82.2 6.9 %all-to-all-done.1 = bf16[64,8,2048]{2,1,0:T(8,128)(2,1)S(1)} async-done(((bf16[64,8,2048]{2,1,0:T(8,128)(2,1)}), bf16[64,8,2048]{2,1,0:T(8,128)(2,1)S(1)}, u32[]{:S(2)}, u32[]{:S(2)}) %all-to-all-start.1) | async-done | bytes 2097184 | tf_op jit(solution)/shard_map/all_to_all | solution.py:662
  89.1 4.0 %collective-permute-start.2 = (bf16[512,2048]{1,0:T(8,128)(2,1)S(1)}, bf16[512,2048]{1,0:T(8,128)(2,1)S(1)}, u32[]{:S(2)}, u32[]{:S(2)}) collective-permute-start(bf16[512,2048]{1,0:T(8,128)(2,1)S(1)} %bitcast.5), channel_id=1, source_target_pairs={{0,1},{1,0},{2,3},{3,2},{4,5},{5,4},{6,7},{7,6},{8,9},{9,8},{10,11... | collective-permute-start | bytes 6291464 | tf_op jit(solution)/shard_map/ppermute | solution.py:678
  93.1 6.6 %final_own.1 = (bf16[128,8192]{1,0:T(8,128)(2,1)}, f32[128,8192]{1,0:T(8,128)}, f32[128,1024]{1,0:T(8,128)}, f32[128,1024]{1,0:T(8,128)}, bf16[4,128,128]{2,1,0:...) custom-call(s32[1]{0:T(128)} %bitcast.sc_ref, ...), custom_call_target="tpu_custom_call" | custom-call | tf_op jit(solution)/shard_map/final_own/pallas_call | solution.py:626
  99.7 0.0 collective-permute-done.2.el_ref
  99.7 2.9 %final_other.1 = (bf16[128,8192]{1,0:T(8,128)(2,1)}, f32[128,8192]{1,0:T(8,128)}, f32[128,1024]{1,0:T(8,128)}, f32[128,1024]{1,0:T(8,128)}) custom-call(s32[1]{0:T(128)} %bitcast.sc_ref, bf16[512,2048]{1,0:T(8,128)(2,1)S(1)} %collective-permute-done.2.el_ref, ...), custom_call_target="tpu_custom_call", output_to_operand_aliasing={{0}: (12, {}), {1}: (13, {}), {2}: (14, {}), {3}: (15, {})} | custom-call | tf_op jit(solution)/shard_map/final_other/pallas_call | solution.py:641
Async XLA Ops:
  5.7 5.4 %collective-permute-start = (bf16[512,2176]{1,0:T(8,128)(2,1)S(1)}, bf16[512,2176]{1,0:T(8,128)(2,1)S(1)}, u32[]{:S(2)}, u32[]{:S(2)}) collective-permute-start(bf16[512,2176]{1,0:T(8,128)(2,1)S(1)} %get-tuple-element.75), channel_id=1, source_target_pairs={{0,1},{1,0},{2,3},{3,2},{4,5},{5,4},{6,7},{7,6},{8,9},{9,8},{10,11... | collective-permute-start | bytes 6684680 | tf_op jit(solution)/shard_map/ppermute | solution.py:668
  12.9 40.6 %all-to-all-start = ((bf16[64,8,2176]{2,1,0:T(8,128)(2,1)}), bf16[64,8,2176]{2,1,0:T(8,128)(2,1)S(1)}, u32[]{:S(2)}, u32[]{:S(2)}) async-start(bf16[64,8,2176]{2,1,0:T(8,128)(2,1)} %get-tuple-element.76), calls=%async_computation | async-start | bytes 4456448 | tf_op jit(solution)/shard_map/all_to_all | solution.py:662
  55.5 7.0 %copy-start.1 = (bf16[512,1152]{1,0:T(8,128)(2,1)S(1)}, bf16[512,1152]{1,0:T(8,128)(2,1)}, u32[]{:S(2)}) copy-start(bf16[512,1152]{1,0:T(8,128)(2,1)} %get-tuple-element.80) | copy-start | bytes 3538948
  55.5 33.6 %all-to-all-start.1 = ((bf16[64,8,2048]{2,1,0:T(8,128)(2,1)}), bf16[64,8,2048]{2,1,0:T(8,128)(2,1)S(1)}, u32[]{:S(2)}, u32[]{:S(2)}) async-start(bf16[64,8,2048]{2,1,0:T(8,128)(2,1)} %scan_chips.1), calls=%async_computation.1 | async-start | bytes 4194304 | tf_op jit(solution)/shard_map/all_to_all | solution.py:662
  62.5 4.9 %collective-permute-start.1 = (bf16[512,1152]{1,0:T(8,128)(2,1)S(1)}, bf16[512,1152]{1,0:T(8,128)(2,1)S(1)}, u32[]{:S(2)}, u32[]{:S(2)}) collective-permute-start(bf16[512,1152]{1,0:T(8,128)(2,1)S(1)} %copy-done.1), channel_id=1, source_target_pairs={{0,1},{1,0},{2,3},{3,2},{4,5},{5,4},{6,7},{7,6},{8,9},{9,8},{10,11... | collective-permute-start | bytes 3538952 | tf_op jit(solution)/shard_map/ppermute | solution.py:672
  67.4 1.0 copy-start
  89.1 10.6 %collective-permute-start.2 = (bf16[512,2048]{1,0:T(8,128)(2,1)S(1)}, bf16[512,2048]{1,0:T(8,128)(2,1)S(1)}, u32[]{:S(2)}, u32[]{:S(2)}) collective-permute-start(bf16[512,2048]{1,0:T(8,128)(2,1)S(1)} %bitcast.5), channel_id=1, source_target_pairs={{0,1},{1,0},{2,3},{3,2},{4,5},{5,4},{6,7},{7,6},{8,9},{9,8},{10,11... | collective-permute-start | bytes 6291464 | tf_op jit(solution)/shard_map/ppermute | solution.py:678
